TPU v7x, 256 devices: a whole 4x4x8 slice. The times are simulated.
256 devices in a mesh: head: 8 (over x, y_hi), seq: 32 (over y_lo, z, core).
Axes of the slice: x: 4, y: 4 (y_hi: 2, y_lo: 2; y = y_hi * 2 + y_lo), z: 8, core: 2. Of those that a mesh axis runs over, the one named last changes fastest.
Arguments:
- video_q: bfloat16 [8192, 3072], P(('seq', 'head')), may hold values from -160 to 160
- video_k: bfloat16 [8192, 3072], P(('seq', 'head')), may hold values from -6 to 6
- video_v: bfloat16 [8192, 3072], P(('seq', 'head')), may hold values from -6 to 6
- audio_q: bfloat16 [512, 3072], P('seq', 'head'), may hold values from -160 to 160
- audio_k: bfloat16 [512, 3072], P('seq', 'head'), may hold values from -6 to 6
- audio_v: bfloat16 [512, 3072], P('seq', 'head'), may hold values from -6 to 6
- align: int32 [8192], P(('seq', 'head')), may hold values from 0 to 511, as said below
Outputs:
- video_out: bfloat16 [8192, 3072], P(('seq', 'head'))
- audio_out: bfloat16 [512, 3072], P('seq', 'head')
Inputs may be any that keep to these rules, and one draw needn't show every extreme that they name: align is non-decreasing, align[0] = 0, align[8191] = 511, and every align[i] lies within 2 of floor(i * 512 / 8192).
All inputs are finite; a program needn't handle non-finite values.
Results may differ from a plain program's by a relative error of at most 0.025.
Values may be sent and summed in bfloat16 or wider, within the bound.
No kernel may reach another device: no remote copies, remote signals or barrier semaphores. Data moves between devices by JAX's collectives and lax.ppermute only.
A program may use at most 128 MiB of HBM per device.

v0:
```python
import jax
import jax.numpy as jnp
from jax import lax
from jax.sharding import PartitionSpec as P

HD = 128


NEG = -1e30
KEY_BLOCK = 2048


def head_scores(queries, keys):
    return jnp.einsum("hrd,hkd->hrk", queries, keys, preferred_element_type=jnp.float32) * HD ** (
        -0.5
    )


def absorb(state, scores, allowed, values):
    top, total, accum = state
    if allowed is not None:
        scores = jnp.where(allowed[None], scores, NEG)
    fresh = jnp.maximum(top, jnp.max(scores, axis=-1))
    shrink = jnp.exp(top - fresh)
    weights = jnp.exp(scores - fresh[..., None])
    if allowed is not None:
        weights = jnp.where(allowed[None], weights, 0.0)
    total = total * shrink + jnp.sum(weights, axis=-1)
    accum = accum * shrink[..., None] + jnp.einsum(
        "hrk,hkd->hrd", weights.astype(jnp.bfloat16), values, preferred_element_type=jnp.float32
    )
    return (fresh, total, accum)


def sweep_keys(state, queries, keys, values, times, near_fn):
    count = keys.shape[1]
    for begin in range(0, count, KEY_BLOCK):
        finish_at = min(begin + KEY_BLOCK, count)
        allowed = None
        if near_fn is not None:
            allowed = near_fn(times[0, begin:finish_at])
        state = absorb(
            state,
            head_scores(queries, keys[:, begin:finish_at]),
            allowed,
            values[:, begin:finish_at],
        )
    return state


def start_state(heads, count):
    return (
        jnp.full((heads, count), NEG, jnp.float32),
        jnp.zeros((heads, count), jnp.float32),
        jnp.zeros((heads, count, HD), jnp.float32),
    )


def finish(state):
    out = state[2] / state[1][..., None]
    return out.transpose(1, 0, 2).reshape(out.shape[1], out.shape[0] * HD).astype(jnp.bfloat16)


def head_major(x, heads):
    return x.reshape(x.shape[0], heads, HD).transpose(1, 0, 2)


def on_device(video_q, video_k, video_v, audio_q, audio_k, audio_v, align):
    heads = audio_q.shape[1] // HD
    q_local, k_local, v_local = (
        lax.all_to_all(video_q, "head", split_axis=1, concat_axis=0, tiled=True),
        lax.all_to_all(video_k, "head", split_axis=1, concat_axis=0, tiled=True),
        lax.all_to_all(video_v, "head", split_axis=1, concat_axis=0, tiled=True),
    )
    rows = q_local.shape[0]
    stamps = lax.all_gather(align, "head", axis=0, tiled=True)
    audio_keys, audio_values = (
        lax.all_gather(head_major(audio_k, heads), "seq", axis=1, tiled=True),
        lax.all_gather(head_major(audio_v, heads), "seq", axis=1, tiled=True),
    )
    audio_rows = audio_q.shape[0]
    audio_all = audio_keys.shape[1]
    window = audio_all // 8
    video_rows_q = head_major(q_local, heads)
    keys_video = head_major(k_local, heads)
    values_video = head_major(v_local, heads)
    times_video = stamps.reshape(1, rows)
    audio_rows_q = head_major(audio_q, heads)
    audio_index = jnp.arange(audio_all, dtype=jnp.int32)
    near_audio = jnp.abs(audio_index[None, :] - stamps[:, None]) <= window
    video_state = absorb(
        start_state(heads, rows), head_scores(video_rows_q, audio_keys), near_audio, audio_values
    )
    audio_state = absorb(
        start_state(heads, audio_rows), head_scores(audio_rows_q, audio_keys), None, audio_values
    )
    own_audio = lax.axis_index("seq") * audio_rows + jnp.arange(audio_rows, dtype=jnp.int32)

    def near_own(block_times):
        return jnp.abs(own_audio[:, None] - block_times[None, :]) <= window

    keys = lax.all_gather(keys_video, "seq", axis=1, tiled=True)
    values = lax.all_gather(values_video, "seq", axis=1, tiled=True)
    times = lax.all_gather(times_video, "seq", axis=1, tiled=True)
    video_next = sweep_keys(video_state, video_rows_q, keys, values, times, None)
    audio_next = sweep_keys(audio_state, audio_rows_q, keys, values, times, near_own)
    video_out = lax.all_to_all(finish(video_next), "head", split_axis=0, concat_axis=1, tiled=True)
    return (video_out, finish(audio_next))


def solution(mesh):
    placed = (
        P(("seq", "head"), None),
        P(("seq", "head"), None),
        P(("seq", "head"), None),
        P("seq", "head"),
        P("seq", "head"),
        P("seq", "head"),
        P(("seq", "head")),
    )
    return jax.shard_map(
        on_device,
        mesh=mesh,
        in_specs=placed,
        out_specs=(P(("seq", "head"), None), P("seq", "head")),
        check_vma=False,
    )
```

profile of v0, /device:TPU:24, one launch (start us, length us, event | category | flops | bytes accessed | tf_op | source)
XLA Modules:
  0.0 218.9 jit_solution(10189751495136876981)
XLA Ops:
  8.2 12.8 %all_to_all.64 = bf16[32,8,384]{2,0,1:T(8,128)(2,1)S(1)} all-to-all(bf16[32,8,384]{2,0,1:T(8,128)(2,1)S(1)} %bitcast.342), channel_id=1, replica_groups=mesh['head'=8,'seq'=32] {'head'}, dimensions={1} | all-to-all | bytes 393216 | tf_op jit(solution)/shard_map/all_to_all | solution.py:72
  22.8 11.0 %all_to_all.65 = bf16[32,8,384]{2,0,1:T(8,128)(2,1)S(1)} all-to-all(bf16[32,8,384]{2,0,1:T(8,128)(2,1)S(1)} %bitcast.343), channel_id=1, replica_groups=mesh['head'=8,'seq'=32] {'head'}, dimensions={1} | all-to-all | bytes 393216 | tf_op jit(solution)/shard_map/all_to_all | solution.py:73
  34.6 1.6 copy.124
  36.2 5.7 %all-to-all-start = ((bf16[32,8,384]{2,0,1:T(8,128)(2,1)}), bf16[32,8,384]{2,0,1:T(8,128)(2,1)S(1)}, u32[]{:S(2)}, u32[]{:S(2)}) async-start(bf16[32,8,384]{2,0,1:T(8,128)(2,1)} %bitcast.330), calls=%async_computation | async-start | bytes 393216 | tf_op jit(solution)/shard_map/all_to_all | solution.py:71
  42.6 1.3 dynamic-slice
  45.4 13.1 %all-reduce = s32[256]{0:T(256)S(1)} all-reduce(s32[256]{0:T(256)S(1)} %dynamic-update-slice), channel_id=1, replica_groups=mesh['head'=8,'seq'=32] {'head'}, use_global_device_ids=true, to_apply=%add | all-reduce | flops 256 | bytes 2048
  58.5 36.4 %all-gather.1 = s32[32,1,256]{2,1,0:T(1,128)S(1)} all-gather(s32[1,1,256]{2,1,0:T(1,128)S(1)} %bitcast.359), channel_id=2, replica_groups=mesh['head'=8,'seq'=32] {'seq'}, dimensions={0}, use_global_device_ids=true | all-gather | bytes 33792 | tf_op jit(solution)/shard_map/all_gather | solution.py:104
  95.0 32.0 %all_gather.19 = bf16[3,512,128]{2,1,0:T(8,128)(2,1)S(1)} all-gather(bf16[3,16,128]{2,1,0:T(8,128)(2,1)S(1)} %bitcast_bitcast_fusion.1), channel_id=1, replica_groups=mesh['head'=8,'seq'=32] {'seq'}, dimensions={1}, use_global_device_ids=true | all-gather | bytes 405504 | tf_op jit(solution)/shard_map/all_gather | solution.py:78
  128.4 33.8 %all_gather.20 = bf16[3,512,128]{2,1,0:T(8,128)(2,1)S(1)} all-gather(bf16[3,16,128]{2,1,0:T(8,128)(2,1)S(1)} %bitcast_bitcast_fusion), channel_id=1, replica_groups=mesh['head'=8,'seq'=32] {'seq'}, dimensions={1}, use_global_device_ids=true | all-gather | bytes 405504 | tf_op jit(solution)/shard_map/all_gather | solution.py:79
  162.9 2.6 %multiply_reduce_fusion = (f32[3,256]{1,0:T(4,128)S(1)}, f32[3,256,2048]{2,1,0:T(8,128)S(1)}) fusion(bf16[3,8192,128]{2,1,0:T(8,128)(2,1)} %all-gather.5.cloned.1.call-done, bf16[256,3,128]{2,1,0:T(4,128)(2,1)S(1)} %reshape.403), kind=kOutput, calls=%fused_computation.4 | convolution fusion | flops 405798144 | bytes 8064000 | tf_op jit(solution)/shard_map/hrd,hkd->hrk/dot_general | solution.py:14
  169.9 2.5 %fusion = (f32[3,256]{1,0:T(4,128)S(1)}, f32[3,256]{1,0:T(4,128)S(1)}) fusion(f32[3,256,2048]{2,1,0:T(8,128)S(1)} %get-tuple-element.39, f32[3,256]{1,0:T(4,128)S(1)} %get-tuple-element.17, f32[3,256]{1,0:T(4,128)S(1)} %get-tuple-element.16, f32[3,256,2048]{2,1,0:T(8,128)S(1)} %get-tuple-element.37), kind=kLoop, calls=%fused_computation.8 | loop fusion | flops 9435648 | bytes 12595200 | tf_op jit(solution)/shard_map/reduce_sum | solution.py:28
  173.4 1.1 copy-done.3
  174.4 2.3 %fusion.4 = (f32[3,256]{1,0:T(4,128)S(1)}, f32[3,256]{1,0:T(4,128)S(1)}) fusion(f32[3,256,2048]{2,1,0:T(8,128)S(1)} %get-tuple-element.35, f32[3,256]{1,0:T(4,128)S(1)} %get-tuple-element.15, f32[3,256]{1,0:T(4,128)S(1)} %get-tuple-element.14, f32[3,256,2048]{2,1,0:T(8,128)S(1)} %get-tuple-element.33), kind=kLoop, calls=%fused_computation.12 | loop fusion | flops 9435648 | bytes 12595200 | tf_op jit(solution)/shard_map/reduce_sum | solution.py:28
  176.8 4.7 %fusion.54 = f32[256,3,128]{2,0,1:T(8,128)S(1)} fusion(bf16[3,8192,128]{2,1,0:T(8,128)(2,1)} %all-gather.7.cloned.1.call-done, f32[3,256,2048]{2,1,0:T(8,128)} %copy-done.6, f32[3,256]{1,0:T(4,128)S(1)} %get-tuple-element.17), kind=kOutput, calls=%fused_computation.64 | convolution fusion | flops 407371776 | bytes 8260608 | tf_op jit(solution)/shard_map/hrk,hkd->hrd/dot_general | solution.py:29
  181.6 5.4 %fusion.59 = f32[256,3,128]{2,0,1:T(8,128)S(1)} fusion(bf16[3,8192,128]{2,1,0:T(8,128)(2,1)} %all-gather.7.cloned.1.call-done, f32[3,256,2048]{2,1,0:T(8,128)} %copy-done.5, f32[3,256]{1,0:T(4,128)S(1)} %get-tuple-element.16), kind=kOutput, calls=%fused_computation.65 | convolution fusion | flops 407371776 | bytes 8260608 | tf_op jit(solution)/shard_map/hrk,hkd->hrd/dot_general | solution.py:29
  187.0 1.4 fusion.64
  188.7 1.4 fusion.69
  192.1 4.8 %all-to-all-start.3 = ((bf16[8,32,384]{2,1,0:T(8,128)(2,1)}), bf16[8,32,384]{2,1,0:T(8,128)(2,1)S(1)}, u32[]{:S(2)}, u32[]{:S(2)}) async-start(bf16[8,32,384]{2,1,0:T(8,128)(2,1)} %convert_element_type.49), calls=%async_computation.3 | async-start | bytes 393216 | tf_op jit(solution)/shard_map/all_to_all | solution.py:107
  196.9 2.1 fusion.211
  199.1 2.0 fusion.212
  201.1 2.0 fusion.213
  203.1 2.2 fusion.214
  206.4 1.8 fusion.112
  208.2 1.8 fusion.115
  (70 shorter events, 18.1 us)
Async XLA Ops:
  7.2 87.8 %copy-start = (bf16[16,384]{1,0:T(8,128)(2,1)S(1)}, bf16[16,384]{1,0:T(8,128)(2,1)}, u32[]{:S(2)}) copy-start(bf16[16,384]{1,0:T(8,128)(2,1)} %param.11) | copy-start | bytes 36868
  7.2 155.7 %all-gather.5.cloned.1.call-start = ((), (), s32[]{:S(2)}) async-start(), calls=%async_computation.4 | async-start | bytes 6488064 | tf_op jit(solution)/shard_map/all_gather | solution.py:102
  21.8 155.0 %all-gather.7.cloned.1.call-start = ((), (), s32[]{:S(2)}) async-start(), calls=%async_computation.5 | async-start | bytes 6488064 | tf_op jit(solution)/shard_map/all_gather | solution.py:103
  36.2 126.1 %all-to-all-start = ((bf16[32,8,384]{2,0,1:T(8,128)(2,1)}), bf16[32,8,384]{2,0,1:T(8,128)(2,1)S(1)}, u32[]{:S(2)}, u32[]{:S(2)}) async-start(bf16[32,8,384]{2,0,1:T(8,128)(2,1)} %bitcast.330), calls=%async_computation | async-start | bytes 393216 | tf_op jit(solution)/shard_map/all_to_all | solution.py:71
  162.9 3.3 %copy-start.1 = (bf16[3,8192,128]{2,1,0:T(8,128)(2,1)S(1)}, bf16[3,8192,128]{2,1,0:T(8,128)(2,1)}, u32[]{:S(2)}) copy-start(bf16[3,8192,128]{2,1,0:T(8,128)(2,1)} %all-gather.5.cloned.1.call-done) | copy-start | bytes 18874372
  166.2 7.2 %copy-start.2 = (f32[3,256,2048]{2,1,0:T(8,128)}, f32[3,256,2048]{2,1,0:T(8,128)S(1)}, u32[]{:S(2)}) copy-start(f32[3,256,2048]{2,1,0:T(8,128)S(1)} %get-tuple-element.33) | copy-start | bytes 18874372
  167.2 7.2 %copy-start.3 = (f32[3,256,2048]{2,1,0:T(8,128)}, f32[3,256,2048]{2,1,0:T(8,128)S(1)}, u32[]{:S(2)}) copy-start(f32[3,256,2048]{2,1,0:T(8,128)S(1)} %get-tuple-element.35) | copy-start | bytes 18874372
  168.3 4.2 %copy-start.5 = (f32[3,256,2048]{2,1,0:T(8,128)}, f32[3,256,2048]{2,1,0:T(8,128)S(1)}, u32[]{:S(2)}) copy-start(f32[3,256,2048]{2,1,0:T(8,128)S(1)} %get-tuple-element.37) | copy-start | bytes 18874372
  169.4 4.0 %copy-start.6 = (f32[3,256,2048]{2,1,0:T(8,128)}, f32[3,256,2048]{2,1,0:T(8,128)S(1)}, u32[]{:S(2)}) copy-start(f32[3,256,2048]{2,1,0:T(8,128)S(1)} %get-tuple-element.39) | copy-start | bytes 18874372
  176.8 10.1 %copy-start.4 = (f32[3,256,2048]{2,1,0:T(8,128)S(1)}, f32[3,256,2048]{2,1,0:T(8,128)}, u32[]{:S(2)}) copy-start(f32[3,256,2048]{2,1,0:T(8,128)} %copy-done.3) | copy-start | bytes 18874372
  176.8 10.1 %copy-start.7 = (bf16[3,8192,128]{2,1,0:T(8,128)(2,1)S(1)}, bf16[3,8192,128]{2,1,0:T(8,128)(2,1)}, u32[]{:S(2)}) copy-start(bf16[3,8192,128]{2,1,0:T(8,128)(2,1)} %all-gather.7.cloned.1.call-done) | copy-start | bytes 18874372
  181.6 6.8 %slice-start = ((s8[6291456]{0:T(1024)(128)(4,1)}), s8[4194304]{0:T(1024)(128)(4,1)S(1)}, s32[]{:S(2)}) async-start(s8[6291456]{0:T(1024)(128)(4,1)} %bitcast.334), calls=%async_computation.6 | async-start | bytes 8388608
  187.0 1.7 slice-start.1
  192.1 19.3 %all-to-all-start.3 = ((bf16[8,32,384]{2,1,0:T(8,128)(2,1)}), bf16[8,32,384]{2,1,0:T(8,128)(2,1)S(1)}, u32[]{:S(2)}, u32[]{:S(2)}) async-start(bf16[8,32,384]{2,1,0:T(8,128)(2,1)} %convert_element_type.49), calls=%async_computation.3 | async-start | bytes 393216 | tf_op jit(solution)/shard_map/all_to_all | solution.py:107
  196.9 13.0 %slice-start.2 = ((s8[6291456]{0:T(1024)(128)(4,1)}), s8[4194304]{0:T(1024)(128)(4,1)S(1)}, s32[]{:S(2)}) async-start(s8[6291456]{0:T(1024)(128)(4,1)} %bitcast.360), calls=%async_computation.8 | async-start | bytes 8388608
  203.1 6.8 %slice-start.3 = ((s8[6291456]{0:T(1024)(128)(4,1)}), s8[2097152]{0:T(1024)(128)(4,1)S(1)}, s32[]{:S(2)}) async-start(s8[6291456]{0:T(1024)(128)(4,1)} %bitcast.360), calls=%async_computation.9 | async-start | bytes 4194304
Sparse Core Ops, SparseCore 0:
  21.9 70.5 all-gather.4
  94.9 70.1 all-gather.6
where the time goes:
time: 221 us; the launch traced here: 219 us
  blocking collectives  139 us (63%)
  matrix products  33.4 us (15%)
  between operations  15 us (7%)
  local copies, waits for them, and re-layouts  14 us (6%)
  starting transfers between devices  10.6 us (5%)
  other arithmetic  6.67 us (3%)
    all_gather x1, blocking collectives, on_device(): times = lax.all_gather(times_video, 'seq', axis=1, tiled=True)  36.4 us
    all_gather x1, blocking collectives, on_device(): lax.all_gather(head_major(audio_v, heads), 'seq', axis=1, tiled=True)  33.8 us
    all_gather x1, blocking collectives, on_device(): lax.all_gather(head_major(audio_k, heads), 'seq', axis=1, tiled=True)  32 us
    dot_general x10, matrix products, absorb(): jnp.einsum('hrk,hkd->hrd', weights.astype(jnp.bfloat16), values, preferre...  18.4 us
    dot_general x10, matrix products, head_scores(): jnp.einsum('hrd,hkd->hrk', queries, keys, preferred_element_type=jnp.floa...  15 us
    unnamed x1, blocking collectives  13.1 us
    all_to_all x1, blocking collectives, on_device(): lax.all_to_all(video_k, 'head', split_axis=1, concat_axis=0, tiled=True)  12.8 us
    all_to_all x1, blocking collectives, on_device(): lax.all_to_all(video_v, 'head', split_axis=1, concat_axis=0, tiled=True)  11 us
  transfers between devices with their start and end apart: 4, of which 0 were waited for; matrix products, arithmetic and copies ran while one was open for 15% of the time, Pallas kernels for 0%

commit v1 on v0

v1 whole, which is shorter than its diff:
```python
import functools

import jax
import jax.numpy as jnp
import numpy as np
from jax import lax
from jax.experimental import pallas as pl
from jax.experimental.pallas import tpu as pltpu
from jax.sharding import Mesh
from jax.sharding import PartitionSpec as P

HD = 128
HPG = 3
GW = HPG * HD
NZ, NX, NY, NC = 8, 4, 4, 2
TOK = 32
AUD = 16
VID = NZ * TOK
AUX = 16
QROWS = VID + AUD + AUX
KROWS = 2 * VID + 2 * AUD + AUX
NKB = NY * NC
WIN = 64.0
NEG = -1e30
C2 = HD**-0.5 * 1.4426950408889634
F32, BF16 = jnp.float32, jnp.bfloat16
VMEM = pl.BlockSpec(memory_space=pltpu.VMEM)
SMEM = pl.BlockSpec(memory_space=pltpu.SMEM)


def pack_body(pos_ref, align_ref, q_ref, k_ref, v_ref, kv_out, q_out):
    first = pos_ref[0]
    lane = lax.broadcasted_iota(jnp.int32, (1, GW), 1)
    row = jnp.zeros((1, GW), jnp.int32)
    for i in range(TOK):
        row = jnp.where(lane == first + i, align_ref[i], row)
    high = (row >> 4).astype(F32)
    low = (row & 15).astype(F32)
    which = lax.broadcasted_iota(jnp.int32, (AUX, GW), 0)
    aux = jnp.where(which == 0, high, jnp.where(which == 1, low, 0.0)).astype(BF16)
    for g in range(NZ):
        cols = slice(g * GW, (g + 1) * GW)
        kv_out[g, 0:TOK, :] = k_ref[:, cols]
        kv_out[g, TOK : 2 * TOK, :] = v_ref[:, cols]
        kv_out[g, 2 * TOK :, :] = aux
        q_out[g] = q_ref[:, cols]


def pack(pos, align, q, k, v):
    return pl.pallas_call(
        pack_body,
        out_shape=(
            jax.ShapeDtypeStruct((NZ, 2 * TOK + AUX, GW), BF16),
            jax.ShapeDtypeStruct((NZ, TOK, GW), BF16),
        ),
        in_specs=[SMEM, SMEM, VMEM, VMEM, VMEM],
        out_specs=(VMEM, VMEM),
        name="pack",
    )(pos, align, q, k, v)


def audio_times(start):
    lane = lax.broadcasted_iota(jnp.int32, (AUX, GW), 1) - VID
    which = lax.broadcasted_iota(jnp.int32, (AUX, GW), 0)
    stamp = lane + start
    here = (lane >= 0) & (lane < AUD)
    part = jnp.where(which == 0, stamp >> 4, jnp.where(which == 1, stamp & 15, 0))
    return jnp.where(here, part, 0).astype(F32)


def join_kv_body(pos_ref, kv_ref, aud_ref, out):
    total = audio_times(pos_ref[1])
    for g in range(NZ):
        out[g * TOK : (g + 1) * TOK, :] = kv_ref[g, 0:TOK, :]
        out[VID + g * TOK : VID + (g + 1) * TOK, :] = kv_ref[g, TOK : 2 * TOK, :]
        total = total + kv_ref[g, 2 * TOK :, :].astype(F32)
    out[2 * VID : 2 * VID + AUD, :] = aud_ref[:, GW : 2 * GW]
    out[2 * VID + AUD : 2 * VID + 2 * AUD, :] = aud_ref[:, 2 * GW :]
    out[2 * VID + 2 * AUD :, :] = total.astype(BF16)


def join_kv(pos, kv, aud):
    return pl.pallas_call(
        join_kv_body,
        out_shape=jax.ShapeDtypeStruct((KROWS, GW), BF16),
        in_specs=[SMEM, VMEM, VMEM],
        out_specs=VMEM,
        name="join_kv",
    )(pos, kv, aud)


def join_q_body(pos_ref, q_ref, kv_ref, aud_ref, out):
    total = audio_times(pos_ref[1])
    for g in range(NZ):
        out[g * TOK : (g + 1) * TOK, :] = q_ref[g]
        total = total + kv_ref[g, 2 * TOK :, :].astype(F32)
    out[VID : VID + AUD, :] = aud_ref[:, 0:GW]
    out[VID + AUD :, :] = total.astype(BF16)


def join_q(pos, q, kv, aud):
    return pl.pallas_call(
        join_q_body,
        out_shape=jax.ShapeDtypeStruct((QROWS, GW), BF16),
        in_specs=[SMEM, VMEM, VMEM, VMEM],
        out_specs=VMEM,
        name="join_q",
    )(pos, q, kv, aud)


def times_of(ref, first):
    aux = ref[first : first + AUX, :].astype(F32)
    return aux[0:1, :] * 16.0 + aux[1:2, :]


def as_column(row):
    return jnp.transpose(jnp.broadcast_to(row, (HD, HD)), (1, 0))


def place(rows):
    return sum(
        pltpu.roll(jnp.broadcast_to(row, (8, HD)), i * AUD, 1) if i else jnp.broadcast_to(row, (8, HD))
        for i, row in enumerate(rows)
    )[0:1, :]


def dot_nt(a, b):
    return lax.dot_general(a, b, (((1,), (1,)), ((), ())), preferred_element_type=F32)


def flash_body(*refs):
    q_refs = refs[0:NX]
    k_refs = refs[NX : NX + NKB]
    outs = refs[NX + NKB : NX + NKB + NX]
    ks, vs, s_ref = refs[NX + NKB + NX :]
    nkv = NKB * VID
    for j, k_ref in enumerate(k_refs):
        ks[j * VID : (j + 1) * VID, :] = k_ref[0:VID, :]
        vs[j * VID : (j + 1) * VID, :] = k_ref[VID : 2 * VID, :]
        at = nkv + j * AUD
        ks[at : at + AUD, :] = k_ref[2 * VID : 2 * VID + AUD, :]
        vs[at : at + AUD, :] = k_ref[2 * VID + AUD : 2 * VID + 2 * AUD, :]
    k_times = [times_of(k_ref, 2 * VID + 2 * AUD) for k_ref in k_refs]
    q_times = [times_of(q_ref, VID + AUD) for q_ref in q_refs]
    ka_times = place([t[:, VID:] for t in k_times])
    qa_times = place([t[:, VID:] for t in q_times])
    lane = lax.broadcasted_iota(jnp.int32, (1, HD), 1)

    def emit(out, r0, rows, h, cols, acc, top, total, src=0):
        out[r0 : r0 + rows, cols] = (acc / total).astype(BF16)[src : src + rows]
        lse = top * C2 + jnp.log2(total)
        hi = lse.astype(BF16).astype(F32)
        mid = (lse - hi).astype(BF16).astype(F32)
        lo = lse - hi - mid
        tile = jnp.where(lane == 3 * h, hi, jnp.where(lane == 3 * h + 1, mid, jnp.where(lane == 3 * h + 2, lo, 0.0)))
        old = out[r0 : r0 + rows, GW:].astype(F32)
        out[r0 : r0 + rows, GW:] = (old + tile[src : src + rows]).astype(BF16)

    for out in outs:
        out[:, GW:] = jnp.zeros((VID + AUD, HD), BF16)

    near = []
    for i in range(NX):
        column = jnp.concatenate(
            [as_column(q_times[i][:, a : a + HD]) for a in range(0, VID, HD)], axis=0
        )
        near.append(jnp.abs(column - ka_times) <= WIN)

    def video(i, h):
        cols = pl.ds(pl.multiple_of(h * HD, HD), HD)
        rows = q_refs[i][0:VID, cols]
        top = None
        for j in range(NKB):
            s = dot_nt(rows, ks[j * VID : (j + 1) * VID, cols])
            s_ref[:, j * VID : (j + 1) * VID] = s
            part = jnp.maximum(s[:, 0:HD], s[:, HD:])
            top = part if top is None else jnp.maximum(top, part)
        sa = jnp.where(near[i], dot_nt(rows, ks[nkv:, cols]), NEG)
        top = jnp.max(jnp.maximum(top, sa), axis=1, keepdims=True)
        pa = jnp.exp2((sa - top) * C2)
        total = pa
        acc = jnp.dot(pa.astype(BF16), vs[nkv:, cols], preferred_element_type=F32)
        for j in range(NKB):
            p = jnp.exp2((s_ref[:, j * VID : (j + 1) * VID] - top) * C2)
            total = total + p[:, 0:HD] + p[:, HD:]
            acc = acc + jnp.dot(
                p.astype(BF16), vs[j * VID : (j + 1) * VID, cols], preferred_element_type=F32
            )
        total = jnp.sum(total, axis=1, keepdims=True)
        emit(outs[i], 0, VID, h, cols, acc, top, total)

    def audio(h):
        n = NX * AUD
        cols = pl.ds(pl.multiple_of(h * HD, HD), HD)
        rows = jnp.concatenate([q_ref[VID : VID + AUD, cols] for q_ref in q_refs], axis=0)
        column = as_column(qa_times)[0:n, :]
        column = jnp.concatenate([column, column], axis=1)
        sa = dot_nt(rows, ks[nkv:, cols])
        top = sa
        for j in range(NKB):
            s = dot_nt(rows, ks[j * VID : (j + 1) * VID, cols])
            s = jnp.where(jnp.abs(column - k_times[j][:, 0:VID]) <= WIN, s, NEG)
            s_ref[0:n, j * VID : (j + 1) * VID] = s
            top = jnp.maximum(top, jnp.maximum(s[:, 0:HD], s[:, HD:]))
        top = jnp.max(top, axis=1, keepdims=True)
        pa = jnp.exp2((sa - top) * C2)
        total = pa
        acc = jnp.dot(pa.astype(BF16), vs[nkv:, cols], preferred_element_type=F32)
        for j in range(NKB):
            p = jnp.exp2((s_ref[0:n, j * VID : (j + 1) * VID] - top) * C2)
            total = total + p[:, 0:HD] + p[:, HD:]
            acc = acc + jnp.dot(
                p.astype(BF16), vs[j * VID : (j + 1) * VID, cols], preferred_element_type=F32
            )
        total = jnp.sum(total, axis=1, keepdims=True)
        for i in range(NX):
            emit(outs[i], VID, AUD, h, cols, acc, top, total, i * AUD)

    @pl.loop(0, HPG)
    def _(h):
        for i in range(NX):
            video(i, h)
        audio(h)


def flash(qs, kvs):
    nk = NKB * (VID + AUD)
    area = NX * (VID + AUD) * nk * HPG
    return pl.pallas_call(
        flash_body,
        out_shape=tuple(jax.ShapeDtypeStruct((VID + AUD, GW + HD), BF16) for _ in range(NX)),
        in_specs=[VMEM] * (NX + NKB),
        out_specs=tuple(VMEM for _ in range(NX)),
        scratch_shapes=[
            pltpu.VMEM((nk, GW), BF16),
            pltpu.VMEM((nk, GW), BF16),
            pltpu.VMEM((VID, NKB * VID), F32),
        ],
        compiler_params=pltpu.CompilerParams(vmem_limit_bytes=40 * 2**20),
        cost_estimate=pl.CostEstimate(flops=4 * area * HD, bytes_accessed=8 << 20, transcendentals=area),
        name="flash",
    )(*qs, *kvs)


def combine_body(a_ref, b_ref, c_ref, d_ref, video_out, audio_out):
    refs = (a_ref, b_ref, c_ref, d_ref)
    for h in range(HPG):
        lses = []
        for ref in refs:
            tile = ref[:, GW:].astype(F32)
            lses.append(tile[:, 3 * h : 3 * h + 1] + tile[:, 3 * h + 1 : 3 * h + 2] + tile[:, 3 * h + 2 : 3 * h + 3])
        top = functools.reduce(jnp.maximum, lses)
        weights = [jnp.exp2(x - top) for x in lses]
        scale = 1.0 / sum(weights)
        cols = slice(h * HD, (h + 1) * HD)
        out = sum(ref[:, cols].astype(F32) * (w * scale) for ref, w in zip(refs, weights, strict=True))
        out = out.astype(BF16)
        for g in range(NZ):
            video_out[g, :, cols] = out[g * TOK : (g + 1) * TOK]
        audio_out[:, cols] = out[VID:]


def combine(parts):
    return pl.pallas_call(
        combine_body,
        out_shape=(
            jax.ShapeDtypeStruct((NZ, TOK, GW), BF16),
            jax.ShapeDtypeStruct((AUD, GW), BF16),
        ),
        in_specs=[VMEM] * NX,
        out_specs=(VMEM, VMEM),
        name="combine",
    )(*parts)


def spread_body(in_ref, out_ref):
    for g in range(NZ):
        out_ref[:, g * GW : (g + 1) * GW] = in_ref[g]


def spread(x):
    return pl.pallas_call(
        spread_body,
        out_shape=jax.ShapeDtypeStruct((TOK, NZ * GW), BF16),
        in_specs=[VMEM],
        out_specs=VMEM,
        name="spread",
    )(x)


def shift(x, axis, n, k):
    return lax.ppermute(x, axis, [(i, (i + k) % n) for i in range(n)])


def swap_group(x):
    pairs = [(a * NZ + b, b * NZ + a) for a in range(NZ) for b in range(NZ)]
    return lax.ppermute(x, ("x", "yh", "z"), pairs)


def on_device(video_q, video_k, video_v, audio_q, audio_k, audio_v, align):
    ix, iyh, iyl = lax.axis_index("x"), lax.axis_index("yh"), lax.axis_index("yl")
    iz, ic = lax.axis_index("z"), lax.axis_index("c")
    block = iyl * 16 + (ix * 2 + iyh) * 2 + ic
    pos = jnp.stack([iz * TOK, block * AUD]).astype(jnp.int32)
    aud = swap_group(jnp.concatenate([audio_q, audio_k, audio_v], axis=1))
    kv_packed, q_packed = pack(pos, align, video_q, video_k, video_v)
    kv_got = lax.all_to_all(kv_packed, "z", split_axis=0, concat_axis=0, tiled=True)
    q_got = lax.all_to_all(q_packed, "z", split_axis=0, concat_axis=0, tiled=True)
    kv_own = join_kv(pos, kv_got, aud)
    q_own = join_q(pos, q_got, kv_got, aud)
    y = ("yh", "yl")
    kvs = [kv_own] + [shift(kv_own, y, NY, k) for k in (1, 3, 2)]
    qs = [q_own] + [shift(q_own, "x", NX, k) for k in (1, 3, 2)]
    kvs = kvs + [shift(b, "c", NC, 1) for b in kvs]
    parts = flash(qs, kvs)
    back = [parts[0]] + [shift(p, "x", NX, -k) for p, k in zip(parts[1:], (1, 3, 2), strict=True)]
    video, audio = combine(back)
    video = spread(lax.all_to_all(video, "z", split_axis=0, concat_axis=0, tiled=True))
    return video, swap_group(audio)


def solution(mesh):
    grid = Mesh(np.asarray(mesh.devices).reshape(4, 2, 2, 8, 2), ("x", "yh", "yl", "z", "c"))
    seq, head = ("yl", "z", "c"), ("x", "yh")
    rows = P(seq + head, None)
    audio = P(seq, head)
    return jax.shard_map(
        on_device,
        mesh=grid,
        in_specs=(rows, rows, rows, audio, audio, audio, P(seq + head)),
        out_specs=(rows, audio),
        check_vma=False,
    )
```

time: 221 us -> 135 us (0.61)
  the two profiles are of different devices: /device:TPU:24 before, /device:TPU:36 now
where the time goes in v1:
time: 135 us
  starting transfers between devices  41.5 us (31%)
  waiting for transfers between devices  38.8 us (29%)
  blocking collectives  24 us (18%)
  Pallas kernels  23.9 us (18%)
  local copies, waits for them, and re-layouts  4.91 us (4%)
    ppermute x13, waiting for transfers between devices, shift(): return lax.ppermute(x, axis, [(i, (i + k) % n) for i in range(n)])  30.4 us
    all_to_all x1, blocking collectives, on_device(): lax.all_to_all(kv_packed, 'z', split_axis=0, concat_axis=0, tiled=True)  24 us
    ppermute x2, starting transfers between devices, swap_group(): return lax.ppermute(x, ('x', 'yh', 'z'), pairs)  18.7 us
    pallas_call x1, Pallas kernels, flash(): pl.pallas_call(flash_body, out_shape=tuple((jax.ShapeDtypeStruct((VID + A...  13.3 us
    ppermute x13, starting transfers between devices, shift(): return lax.ppermute(x, axis, [(i, (i + k) % n) for i in range(n)])  10.1 us
    ppermute x2, waiting for transfers between devices, swap_group(): return lax.ppermute(x, ('x', 'yh', 'z'), pairs)  8.37 us
    all_to_all x1, starting transfers between devices, on_device(): lax.all_to_all(video, 'z', split_axis=0, concat_axis=0, tiled=True)  7.86 us
    unnamed x27, local copies, waits for them, and re-layouts  4.91 us
  transfers between devices with their start and end apart: 17, of which 8 were waited for; matrix products, arithmetic and copies ran while one was open for 0% of the time, Pallas kernels for 3%

profile of v1, /device:TPU:36, one launch (start us, length us, event | category | flops | bytes accessed | tf_op | source)
XLA Modules:
  0.0 134.5 jit_solution(7997890216868988133)
XLA Ops:
  1.3 2.1 %pack.1 = (bf16[8,80,384]{2,1,0:T(8,128)(2,1)}, bf16[8,32,384]{2,1,0:T(8,128)(2,1)}) custom-call(s32[2]{0:T(128)} %pad_add_fusion.pos_ref, s32[32]{0:T(128)} %align_ref.1, bf16[32,3072]{1,0:T(8,128)(2,1)} %q_ref.1, bf16[32,3072]{1,0:T(8,128)(2,1)} %k_ref.1, bf16[32,3072]{1,0:T(8,128)(2,1)} %v_ref.1), custom_call_target="tpu_custom_call" | custom-call | tf_op jit(solution)/shard_map/pack/pallas_call | solution.py:50
  3.3 24.0 %all_to_all.15.kv_ref = bf16[8,80,384]{2,1,0:T(8,128)(2,1)} all-to-all(bf16[8,80,384]{2,1,0:T(8,128)(2,1)} %get-tuple-element.11), channel_id=1, replica_groups=mesh['x'=4,'yh'=2,'yl'=2,'z'=8,'c'=2] {'z'}, dimensions={0} | all-to-all | bytes 983040 | tf_op jit(solution)/shard_map/all_to_all | solution.py:307
  27.3 4.9 %all-to-all-start = ((bf16[8,32,384]{2,1,0:T(8,128)(2,1)}), bf16[8,32,384]{2,1,0:T(8,128)(2,1)S(1)}, u32[]{:S(2)}, u32[]{:S(2)}) async-start(bf16[8,32,384]{2,1,0:T(8,128)(2,1)} %get-tuple-element.10), calls=%async_computation | async-start | bytes 393216 | tf_op jit(solution)/shard_map/all_to_all | solution.py:308
  32.2 9.0 %collective-permute-start = (bf16[16,1152]{1,0:T(8,128)(2,1)S(1)}, bf16[16,1152]{1,0:T(8,128)(2,1)S(1)}, u32[]{:S(2)}, u32[]{:S(2)}) collective-permute-start(bf16[16,1152]{1,0:T(8,128)(2,1)S(1)} %pad_maximum_fusion), channel_id=1, source_target_pairs={{0,0},{2,32},{4,64},{6,96},{8,128},{10,160},{12,192},{14,224},{32,... | collective-permute-start | bytes 110600 | tf_op jit(solution)/shard_map/ppermute | solution.py:297
  41.2 4.7 %collective-permute-done.aud_ref = bf16[16,1152]{1,0:T(8,128)(2,1)S(1)} collective-permute-done((bf16[16,1152]{1,0:T(8,128)(2,1)S(1)}, bf16[16,1152]{1,0:T(8,128)(2,1)S(1)}, u32[]{:S(2)}, u32[]{:S(2)}) %collective-permute-start) | collective-permute-done | bytes 36896 | tf_op jit(solution)/shard_map/ppermute | solution.py:297
  46.5 1.9 %join_kv.1.refs_4_ = bf16[560,384]{1,0:T(8,128)(2,1)} custom-call(s32[2]{0:T(128)} %pad_add_fusion.pos_ref, bf16[8,80,384]{2,1,0:T(8,128)(2,1)} %all_to_all.15.kv_ref, bf16[16,1152]{1,0:T(8,128)(2,1)} %copy-done.8), custom_call_target="tpu_custom_call" | custom-call | tf_op jit(solution)/shard_map/join_kv/pallas_call | solution.py:83
  48.4 1.7 %collective-permute-start.6 = (bf16[560,384]{1,0:T(8,128)(2,1)}, bf16[560,384]{1,0:T(8,128)(2,1)S(1)}, u32[]{:S(2)}, u32[]{:S(2)}) collective-permute-start(bf16[560,384]{1,0:T(8,128)(2,1)} %join_kv.1.refs_4_), channel_id=1, source_target_pairs={{0,32},{16,48},{32,0},{48,16},{1,33},{17,49},{33,1},{49,17},{2,34}... | collective-permute-start | bytes 1290248 | tf_op jit(solution)/shard_map/ppermute | solution.py:292
  50.1 3.0 %collective-permute-start.5 = (bf16[560,384]{1,0:T(8,128)(2,1)}, bf16[560,384]{1,0:T(8,128)(2,1)S(1)}, u32[]{:S(2)}, u32[]{:S(2)}) collective-permute-start(bf16[560,384]{1,0:T(8,128)(2,1)} %join_kv.1.refs_4_), channel_id=1, source_target_pairs={{0,48},{16,0},{32,16},{48,32},{1,49},{17,1},{33,17},{49,33},{2,50}... | collective-permute-start | bytes 1290248 | tf_op jit(solution)/shard_map/ppermute | solution.py:292
  53.7 1.8 %join_q.1.refs_0_ = bf16[288,384]{1,0:T(8,128)(2,1)} custom-call(s32[2]{0:T(128)} %pad_add_fusion.pos_ref, bf16[8,32,384]{2,1,0:T(8,128)(2,1)} %copy-done.4, bf16[8,80,384]{2,1,0:T(8,128)(2,1)} %all_to_all.15.kv_ref, bf16[16,1152]{1,0:T(8,128)(2,1)} %copy-done.8), custom_call_target="tpu_custom_call" | custom-call | tf_op jit(solution)/shard_map/join_q/pallas_call | solution.py:102
  55.5 2.0 %collective-permute-start.2 = (bf16[288,384]{1,0:T(8,128)(2,1)}, bf16[288,384]{1,0:T(8,128)(2,1)S(1)}, u32[]{:S(2)}, u32[]{:S(2)}) collective-permute-start(bf16[288,384]{1,0:T(8,128)(2,1)} %join_q.1.refs_0_), channel_id=1, source_target_pairs={{0,192},{64,0},{128,64},{192,128},{1,193},{65,1},{129,65},{193,129... | collective-permute-start | bytes 663560 | tf_op jit(solution)/shard_map/ppermute | solution.py:292
  57.5 5.7 %collective-permute-done.3.refs_3_ = bf16[288,384]{1,0:T(8,128)(2,1)S(1)} collective-permute-done((bf16[288,384]{1,0:T(8,128)(2,1)}, bf16[288,384]{1,0:T(8,128)(2,1)S(1)}, u32[]{:S(2)}, u32[]{:S(2)}) %collective-permute-start.3) | collective-permute-done | bytes 221216 | tf_op jit(solution)/shard_map/ppermute | solution.py:292
  63.7 3.0 %collective-permute-done.5.refs_6_ = bf16[560,384]{1,0:T(8,128)(2,1)S(1)} collective-permute-done((bf16[560,384]{1,0:T(8,128)(2,1)}, bf16[560,384]{1,0:T(8,128)(2,1)S(1)}, u32[]{:S(2)}, u32[]{:S(2)}) %collective-permute-start.5) | collective-permute-done | bytes 430112 | tf_op jit(solution)/shard_map/ppermute | solution.py:292
  66.7 1.8 %collective-permute-done.4.refs_5_ = bf16[560,384]{1,0:T(8,128)(2,1)S(1)} collective-permute-done((bf16[560,384]{1,0:T(8,128)(2,1)}, bf16[560,384]{1,0:T(8,128)(2,1)S(1)}, u32[]{:S(2)}, u32[]{:S(2)}) %collective-permute-start.4) | collective-permute-done | bytes 430112 | tf_op jit(solution)/shard_map/ppermute | solution.py:292
  68.9 7.7 %collective-permute-done.1.refs_1_ = bf16[288,384]{1,0:T(8,128)(2,1)S(1)} collective-permute-done((bf16[288,384]{1,0:T(8,128)(2,1)}, bf16[288,384]{1,0:T(8,128)(2,1)S(1)}, u32[]{:S(2)}, u32[]{:S(2)}) %collective-permute-start.1) | collective-permute-done | bytes 221216 | tf_op jit(solution)/shard_map/ppermute | solution.py:292
  76.7 0.9 copy-done.2
  77.6 13.3 %flash.1 = (bf16[272,512]{1,0:T(8,128)(2,1)S(1)}, bf16[272,512]{1,0:T(8,128)(2,1)S(1)}, bf16[272,512]{1,0:T(8,128)(2,1)S(1)}, bf16[272,512]{1,0:T(8,128)(2,1)S(1)}) custom-call(bf16[288,384]{1,0:T(8,128)(2,1)S(1)} %copy-done.2, bf16[288,384]{1,0:T(8,128)(2,1)S(1)} %collective-permute-done.1.refs_1_, bf16[288,384]{1,0:T(8,128)(2,1)S(1)} %collective-permute-done.2.refs_2_, ...), custom_call_target="tpu_custom_call" | custom-call | flops 3636461568 | bytes 8388608 | tf_op jit(solution)/shard_map/flash/pallas_call | solution.py:229
  91.6 2.0 %collective-permute-start.12 = (bf16[272,512]{1,0:T(8,128)(2,1)S(1)}, bf16[272,512]{1,0:T(8,128)(2,1)S(1)}, u32[]{:S(2)}, u32[]{:S(2)}) collective-permute-start(bf16[272,512]{1,0:T(8,128)(2,1)S(1)} %get-tuple-element.14), channel_id=1, source_target_pairs={{0,64},{64,128},{128,192},{192,0},{1,65},{65,129},{129,193},{193,1... | collective-permute-start | bytes 835592 | tf_op jit(solution)/shard_map/ppermute | solution.py:292
  94.3 6.9 %collective-permute-done.11.b_ref = bf16[272,512]{1,0:T(8,128)(2,1)S(1)} collective-permute-done((bf16[272,512]{1,0:T(8,128)(2,1)S(1)}, bf16[272,512]{1,0:T(8,128)(2,1)S(1)}, u32[]{:S(2)}, u32[]{:S(2)}) %collective-permute-start.11) | collective-permute-done | bytes 278560 | tf_op jit(solution)/shard_map/ppermute | solution.py:292
  101.2 5.2 %collective-permute-done.13.d_ref = bf16[272,512]{1,0:T(8,128)(2,1)S(1)} collective-permute-done((bf16[272,512]{1,0:T(8,128)(2,1)S(1)}, bf16[272,512]{1,0:T(8,128)(2,1)S(1)}, u32[]{:S(2)}, u32[]{:S(2)}) %collective-permute-start.13) | collective-permute-done | bytes 278560 | tf_op jit(solution)/shard_map/ppermute | solution.py:292
  107.1 3.2 %combine.1 = (bf16[8,32,384]{2,1,0:T(8,128)(2,1)}, bf16[16,384]{1,0:T(8,128)(2,1)}) custom-call(bf16[272,512]{1,0:T(8,128)(2,1)} %copy-done.1, bf16[272,512]{1,0:T(8,128)(2,1)} %copy-done.5, bf16[272,512]{1,0:T(8,128)(2,1)} %copy-done.6, bf16[272,512]{1,0:T(8,128)(2,1)} %copy-done.7), custom_call_target="tpu_custom_call" | custom-call | tf_op jit(solution)/shard_map/combine/pallas_call | solution.py:264
  110.4 7.9 %all-to-all-start.2 = ((bf16[8,32,384]{2,1,0:T(8,128)(2,1)}), bf16[8,32,384]{2,1,0:T(8,128)(2,1)S(1)}, u32[]{:S(2)}, u32[]{:S(2)}) async-start(bf16[8,32,384]{2,1,0:T(8,128)(2,1)} %get-tuple-element.16), calls=%async_computation.2 | async-start | bytes 393216 | tf_op jit(solution)/shard_map/all_to_all | solution.py:318
  118.2 9.7 %collective-permute-start.14 = (bf16[16,384]{1,0:T(8,128)(2,1)S(1)}, bf16[16,384]{1,0:T(8,128)(2,1)S(1)}, u32[]{:S(2)}, u32[]{:S(2)}) collective-permute-start(bf16[16,384]{1,0:T(8,128)(2,1)S(1)} %copy-done.12), channel_id=1, source_target_pairs={{0,0},{2,32},{4,64},{6,96},{8,128},{10,160},{12,192},{14,224},{32,... | collective-permute-start | bytes 36872 | tf_op jit(solution)/shard_map/ppermute | solution.py:297
  127.9 3.7 %collective-permute-done.14 = bf16[16,384]{1,0:T(8,128)(2,1)S(1)} collective-permute-done((bf16[16,384]{1,0:T(8,128)(2,1)S(1)}, bf16[16,384]{1,0:T(8,128)(2,1)S(1)}, u32[]{:S(2)}, u32[]{:S(2)}) %collective-permute-start.14) | collective-permute-done | bytes 12320 | tf_op jit(solution)/shard_map/ppermute | solution.py:297
  132.3 1.6 %spread.1 = bf16[32,3072]{1,0:T(8,128)(2,1)} custom-call(bf16[8,32,384]{2,1,0:T(8,128)(2,1)} %copy-done.3), custom_call_target="tpu_custom_call" | custom-call | tf_op jit(solution)/shard_map/spread/pallas_call | solution.py:282
  (46 shorter events, 6.1 us)
Async XLA Ops:
  27.3 4.9 %copy-start.9 = (bf16[16,384]{1,0:T(8,128)(2,1)S(1)}, bf16[16,384]{1,0:T(8,128)(2,1)}, u32[]{:S(2)}) copy-start(bf16[16,384]{1,0:T(8,128)(2,1)} %param.12) | copy-start | bytes 36868
  27.3 4.9 %copy-start.10 = (bf16[16,384]{1,0:T(8,128)(2,1)S(1)}, bf16[16,384]{1,0:T(8,128)(2,1)}, u32[]{:S(2)}) copy-start(bf16[16,384]{1,0:T(8,128)(2,1)} %param.11) | copy-start | bytes 36868
  27.3 4.9 %copy-start.11 = (bf16[16,384]{1,0:T(8,128)(2,1)S(1)}, bf16[16,384]{1,0:T(8,128)(2,1)}, u32[]{:S(2)}) copy-start(bf16[16,384]{1,0:T(8,128)(2,1)} %param.10) | copy-start | bytes 36868
  27.3 25.7 %all-to-all-start = ((bf16[8,32,384]{2,1,0:T(8,128)(2,1)}), bf16[8,32,384]{2,1,0:T(8,128)(2,1)S(1)}, u32[]{:S(2)}, u32[]{:S(2)}) async-start(bf16[8,32,384]{2,1,0:T(8,128)(2,1)} %get-tuple-element.10), calls=%async_computation | async-start | bytes 393216 | tf_op jit(solution)/shard_map/all_to_all | solution.py:308
  32.2 13.7 %collective-permute-start = (bf16[16,1152]{1,0:T(8,128)(2,1)S(1)}, bf16[16,1152]{1,0:T(8,128)(2,1)S(1)}, u32[]{:S(2)}, u32[]{:S(2)}) collective-permute-start(bf16[16,1152]{1,0:T(8,128)(2,1)S(1)} %pad_maximum_fusion), channel_id=1, source_target_pairs={{0,0},{2,32},{4,64},{6,96},{8,128},{10,160},{12,192},{14,224},{32,... | collective-permute-start | bytes 110600 | tf_op jit(solution)/shard_map/ppermute | solution.py:297
  48.4 14.8 %copy-start = (bf16[560,384]{1,0:T(8,128)(2,1)S(1)}, bf16[560,384]{1,0:T(8,128)(2,1)}, u32[]{:S(2)}) copy-start(bf16[560,384]{1,0:T(8,128)(2,1)} %join_kv.1.refs_4_) | copy-start | bytes 1290244
  48.4 14.8 %collective-permute-start.6 = (bf16[560,384]{1,0:T(8,128)(2,1)}, bf16[560,384]{1,0:T(8,128)(2,1)S(1)}, u32[]{:S(2)}, u32[]{:S(2)}) collective-permute-start(bf16[560,384]{1,0:T(8,128)(2,1)} %join_kv.1.refs_4_), channel_id=1, source_target_pairs={{0,32},{16,48},{32,0},{48,16},{1,33},{17,49},{33,1},{49,17},{2,34}... | collective-permute-start | bytes 1290248 | tf_op jit(solution)/shard_map/ppermute | solution.py:292
  50.1 16.6 %collective-permute-start.5 = (bf16[560,384]{1,0:T(8,128)(2,1)}, bf16[560,384]{1,0:T(8,128)(2,1)S(1)}, u32[]{:S(2)}, u32[]{:S(2)}) collective-permute-start(bf16[560,384]{1,0:T(8,128)(2,1)} %join_kv.1.refs_4_), channel_id=1, source_target_pairs={{0,48},{16,0},{32,16},{48,32},{1,49},{17,1},{33,17},{49,33},{2,50}... | collective-permute-start | bytes 1290248 | tf_op jit(solution)/shard_map/ppermute | solution.py:292
  53.0 15.5 %collective-permute-start.4 = (bf16[560,384]{1,0:T(8,128)(2,1)}, bf16[560,384]{1,0:T(8,128)(2,1)S(1)}, u32[]{:S(2)}, u32[]{:S(2)}) collective-permute-start(bf16[560,384]{1,0:T(8,128)(2,1)} %join_kv.1.refs_4_), channel_id=1, source_target_pairs={{0,16},{16,32},{32,48},{48,0},{1,17},{17,33},{33,49},{49,1},{2,18}... | collective-permute-start | bytes 1290248 | tf_op jit(solution)/shard_map/ppermute | solution.py:292
  55.5 7.6 %collective-permute-start.3 = (bf16[288,384]{1,0:T(8,128)(2,1)}, bf16[288,384]{1,0:T(8,128)(2,1)S(1)}, u32[]{:S(2)}, u32[]{:S(2)}) collective-permute-start(bf16[288,384]{1,0:T(8,128)(2,1)} %join_q.1.refs_0_), channel_id=1, source_target_pairs={{0,128},{64,192},{128,0},{192,64},{1,129},{65,193},{129,1},{193,65... | collective-permute-start | bytes 663560 | tf_op jit(solution)/shard_map/ppermute | solution.py:292
  55.5 13.0 %collective-permute-start.2 = (bf16[288,384]{1,0:T(8,128)(2,1)}, bf16[288,384]{1,0:T(8,128)(2,1)S(1)}, u32[]{:S(2)}, u32[]{:S(2)}) collective-permute-start(bf16[288,384]{1,0:T(8,128)(2,1)} %join_q.1.refs_0_), channel_id=1, source_target_pairs={{0,192},{64,0},{128,64},{192,128},{1,193},{65,1},{129,65},{193,129... | collective-permute-start | bytes 663560 | tf_op jit(solution)/shard_map/ppermute | solution.py:292
  63.2 13.5 %collective-permute-start.7 = (bf16[560,384]{1,0:T(8,128)(2,1)S(1)}, bf16[560,384]{1,0:T(8,128)(2,1)S(1)}, u32[]{:S(2)}, u32[]{:S(2)}) collective-permute-start(bf16[560,384]{1,0:T(8,128)(2,1)S(1)} %copy-done), channel_id=1, source_target_pairs={{0,1},{1,0},{2,3},{3,2},{4,5},{5,4},{6,7},{7,6},{8,9},{9,8},{10,11... | collective-permute-start | bytes 1290248 | tf_op jit(solution)/shard_map/ppermute | solution.py:292
  63.2 13.4 %collective-permute-start.10 = (bf16[560,384]{1,0:T(8,128)(2,1)S(1)}, bf16[560,384]{1,0:T(8,128)(2,1)S(1)}, u32[]{:S(2)}, u32[]{:S(2)}) collective-permute-start(bf16[560,384]{1,0:T(8,128)(2,1)S(1)} %collective-permute-done.6.refs_7_), channel_id=1, source_target_pairs={{0,1},{1,0},{2,3},{3,2},{4,5},{5,4},{6,7},{7,6},{8,9},{9,8},{10,11... | collective-permute-start | bytes 1290248 | tf_op jit(solution)/shard_map/ppermute | solution.py:292
  66.7 9.9 %collective-permute-start.9 = (bf16[560,384]{1,0:T(8,128)(2,1)S(1)}, bf16[560,384]{1,0:T(8,128)(2,1)S(1)}, u32[]{:S(2)}, u32[]{:S(2)}) collective-permute-start(bf16[560,384]{1,0:T(8,128)(2,1)S(1)} %collective-permute-done.5.refs_6_), channel_id=1, source_target_pairs={{0,1},{1,0},{2,3},{3,2},{4,5},{5,4},{6,7},{7,6},{8,9},{9,8},{10,11... | collective-permute-start | bytes 1290248 | tf_op jit(solution)/shard_map/ppermute | solution.py:292
  68.6 8.1 %collective-permute-start.8 = (bf16[560,384]{1,0:T(8,128)(2,1)S(1)}, bf16[560,384]{1,0:T(8,128)(2,1)S(1)}, u32[]{:S(2)}, u32[]{:S(2)}) collective-permute-start(bf16[560,384]{1,0:T(8,128)(2,1)S(1)} %collective-permute-done.4.refs_5_), channel_id=1, source_target_pairs={{0,1},{1,0},{2,3},{3,2},{4,5},{5,4},{6,7},{7,6},{8,9},{9,8},{10,11... | collective-permute-start | bytes 1290248 | tf_op jit(solution)/shard_map/ppermute | solution.py:292
  68.6 8.1 %collective-permute-start.1 = (bf16[288,384]{1,0:T(8,128)(2,1)}, bf16[288,384]{1,0:T(8,128)(2,1)S(1)}, u32[]{:S(2)}, u32[]{:S(2)}) collective-permute-start(bf16[288,384]{1,0:T(8,128)(2,1)} %join_q.1.refs_0_), channel_id=1, source_target_pairs={{0,64},{64,128},{128,192},{192,0},{1,65},{65,129},{129,193},{193,1... | collective-permute-start | bytes 663560 | tf_op jit(solution)/shard_map/ppermute | solution.py:292
  91.6 9.6 %collective-permute-start.11 = (bf16[272,512]{1,0:T(8,128)(2,1)S(1)}, bf16[272,512]{1,0:T(8,128)(2,1)S(1)}, u32[]{:S(2)}, u32[]{:S(2)}) collective-permute-start(bf16[272,512]{1,0:T(8,128)(2,1)S(1)} %get-tuple-element.13), channel_id=1, source_target_pairs={{0,192},{64,0},{128,64},{192,128},{1,193},{65,1},{129,65},{193,129... | collective-permute-start | bytes 835592 | tf_op jit(solution)/shard_map/ppermute | solution.py:292
  91.6 9.6 %collective-permute-start.12 = (bf16[272,512]{1,0:T(8,128)(2,1)S(1)}, bf16[272,512]{1,0:T(8,128)(2,1)S(1)}, u32[]{:S(2)}, u32[]{:S(2)}) collective-permute-start(bf16[272,512]{1,0:T(8,128)(2,1)S(1)} %get-tuple-element.14), channel_id=1, source_target_pairs={{0,64},{64,128},{128,192},{192,0},{1,65},{65,129},{129,193},{193,1... | collective-permute-start | bytes 835592 | tf_op jit(solution)/shard_map/ppermute | solution.py:292
  93.7 12.8 %collective-permute-start.13 = (bf16[272,512]{1,0:T(8,128)(2,1)S(1)}, bf16[272,512]{1,0:T(8,128)(2,1)S(1)}, u32[]{:S(2)}, u32[]{:S(2)}) collective-permute-start(bf16[272,512]{1,0:T(8,128)(2,1)S(1)} %get-tuple-element.15), channel_id=1, source_target_pairs={{0,128},{64,192},{128,0},{192,64},{1,129},{65,193},{129,1},{193,65... | collective-permute-start | bytes 835592 | tf_op jit(solution)/shard_map/ppermute | solution.py:292
  101.2 5.3 %copy-start.5 = (bf16[272,512]{1,0:T(8,128)(2,1)}, bf16[272,512]{1,0:T(8,128)(2,1)S(1)}, u32[]{:S(2)}) copy-start(bf16[272,512]{1,0:T(8,128)(2,1)S(1)} %collective-permute-done.11.b_ref) | copy-start | bytes 835588
  101.2 5.3 %copy-start.6 = (bf16[272,512]{1,0:T(8,128)(2,1)}, bf16[272,512]{1,0:T(8,128)(2,1)S(1)}, u32[]{:S(2)}) copy-start(bf16[272,512]{1,0:T(8,128)(2,1)S(1)} %collective-permute-done.12.c_ref) | copy-start | bytes 835588
  110.4 7.9 %copy-start.12 = (bf16[16,384]{1,0:T(8,128)(2,1)S(1)}, bf16[16,384]{1,0:T(8,128)(2,1)}, u32[]{:S(2)}) copy-start(bf16[16,384]{1,0:T(8,128)(2,1)} %get-tuple-element.17) | copy-start | bytes 36868
  110.4 21.3 %all-to-all-start.2 = ((bf16[8,32,384]{2,1,0:T(8,128)(2,1)}), bf16[8,32,384]{2,1,0:T(8,128)(2,1)S(1)}, u32[]{:S(2)}, u32[]{:S(2)}) async-start(bf16[8,32,384]{2,1,0:T(8,128)(2,1)} %get-tuple-element.16), calls=%async_computation.2 | async-start | bytes 393216 | tf_op jit(solution)/shard_map/all_to_all | solution.py:318
  118.2 13.4 %collective-permute-start.14 = (bf16[16,384]{1,0:T(8,128)(2,1)S(1)}, bf16[16,384]{1,0:T(8,128)(2,1)S(1)}, u32[]{:S(2)}, u32[]{:S(2)}) collective-permute-start(bf16[16,384]{1,0:T(8,128)(2,1)S(1)} %copy-done.12), channel_id=1, source_target_pairs={{0,0},{2,32},{4,64},{6,96},{8,128},{10,160},{12,192},{14,224},{32,... | collective-permute-start | bytes 36872 | tf_op jit(solution)/shard_map/ppermute | solution.py:297
  (6 other events, 4.3 us)

commit v2 on v0

v2 whole, which is shorter than its diff:
```python
import functools

import jax
import jax.numpy as jnp
import numpy as np
from jax import lax
from jax.experimental import pallas as pl
from jax.experimental.pallas import tpu as pltpu
from jax.sharding import Mesh
from jax.sharding import PartitionSpec as P

HD = 128
HPG = 3
GW = HPG * HD
NZ, NX, NY, NC = 8, 4, 4, 2
TOK = 32
AUD = 16
VID = NZ * TOK
AUX = 16
QROWS = VID + AUD + AUX
KROWS = 2 * VID + 2 * AUD + AUX
NKB = NY * NC
HALF = NKB // 2
WIN = 64.0
NEG = -1e30
C2 = HD**-0.5 * 1.4426950408889634
F32, BF16 = jnp.float32, jnp.bfloat16
VMEM = pl.BlockSpec(memory_space=pltpu.VMEM)
SMEM = pl.BlockSpec(memory_space=pltpu.SMEM)
SMALL = pltpu.CompilerParams(vmem_limit_bytes=6 * 2**20)


def pack_body(align_ref, q_ref, k_ref, v_ref, out):
    first = lax.axis_index("z") * TOK
    lane = lax.broadcasted_iota(jnp.int32, (1, GW), 1)
    row = jnp.zeros((1, GW), jnp.int32)
    for i in range(TOK):
        row = jnp.where(lane == first + i, align_ref[i], row)
    high = (row >> 4).astype(F32)
    low = (row & 15).astype(F32)
    which = lax.broadcasted_iota(jnp.int32, (AUX, GW), 0)
    aux = jnp.where(which == 0, high, jnp.where(which == 1, low, 0.0)).astype(BF16)
    for g in range(NZ):
        cols = slice(g * GW, (g + 1) * GW)
        out[g, 0:TOK, :] = q_ref[:, cols]
        out[g, TOK : 2 * TOK, :] = k_ref[:, cols]
        out[g, 2 * TOK : 3 * TOK, :] = v_ref[:, cols]
        out[g, 3 * TOK :, :] = aux


def pack(align, q, k, v):
    return pl.pallas_call(
        pack_body,
        out_shape=jax.ShapeDtypeStruct((NZ, 3 * TOK + AUX, GW), BF16),
        in_specs=[SMEM, VMEM, VMEM, VMEM],
        out_specs=VMEM,
        name="pack",
    )(align, q, k, v)


def audio_times(start):
    lane = lax.broadcasted_iota(jnp.int32, (AUX, GW), 1) - VID
    which = lax.broadcasted_iota(jnp.int32, (AUX, GW), 0)
    stamp = lane + start
    here = (lane >= 0) & (lane < AUD)
    part = jnp.where(which == 0, stamp >> 4, jnp.where(which == 1, stamp & 15, 0))
    return jnp.where(here, part, 0).astype(F32)


def join_body(got_ref, aud_ref, q_out, kv_out):
    block = lax.axis_index("yl") * 16 + (lax.axis_index("x") * 2 + lax.axis_index("yh")) * 2 + lax.axis_index("c")
    total = audio_times(block * AUD)
    for g in range(NZ):
        at = g * TOK
        q_out[at : at + TOK, :] = got_ref[g, 0:TOK, :]
        kv_out[at : at + TOK, :] = got_ref[g, TOK : 2 * TOK, :]
        kv_out[VID + at : VID + at + TOK, :] = got_ref[g, 2 * TOK : 3 * TOK, :]
        total = total + got_ref[g, 3 * TOK :, :].astype(F32)
    q_out[VID : VID + AUD, :] = aud_ref[:, 0:GW]
    kv_out[2 * VID : 2 * VID + AUD, :] = aud_ref[:, GW : 2 * GW]
    kv_out[2 * VID + AUD : 2 * VID + 2 * AUD, :] = aud_ref[:, 2 * GW :]
    q_out[VID + AUD :, :] = total.astype(BF16)
    kv_out[2 * VID + 2 * AUD :, :] = total.astype(BF16)


def join(got, aud):
    return pl.pallas_call(
        join_body,
        out_shape=(
            jax.ShapeDtypeStruct((QROWS, GW), BF16),
            jax.ShapeDtypeStruct((KROWS, GW), BF16),
        ),
        in_specs=[VMEM, VMEM],
        out_specs=(VMEM, VMEM),
        compiler_params=SMALL,
        name="join",
    )(got, aud)


def place(rows):
    return sum(
        pltpu.roll(jnp.broadcast_to(row, (8, HD)), i * AUD, 1) if i else jnp.broadcast_to(row, (8, HD))
        for i, row in enumerate(rows)
    )[0:1, :]


def dot_nt(a, b):
    return lax.dot_general(a, b, (((1,), (1,)), ((), ())), preferred_element_type=F32)


def dot_tn(a, b):
    return lax.dot_general(a, b, (((0,), (0,)), ((), ())), preferred_element_type=F32)


def times_of(ref, first):
    aux = ref[first : first + AUX, :].astype(F32)
    return aux[0:1, :] * 16.0 + aux[1:2, :]


def column_times(q_ref):
    which = lax.broadcasted_iota(jnp.int32, (AUX, HD), 0)
    pick = jnp.where(which == 0, 16.0, jnp.where(which == 1, 1.0, 0.0)).astype(BF16)
    return dot_tn(q_ref[VID + AUD :, :], pick)


def side_by_side(x):
    return jnp.concatenate([x, x], axis=1)


def scores(q, k_refs, cols, near_audio, s_ref, h):
    top = None
    for j, k_ref in enumerate(k_refs):
        s = dot_nt(q, k_ref[0:VID, cols])
        s = jnp.concatenate([s[0:VID], jnp.where(near_audio[j], s[VID:], NEG)], axis=0)
        s_ref[h, :, j * VID : (j + 1) * VID] = s
        part = jnp.maximum(s[:, 0:HD], s[:, HD:])
        top = part if top is None else jnp.maximum(top, part)
    return top


def weigh(s, top, v, ones):
    p = jnp.exp2((s - top) * C2).astype(BF16)
    v = jnp.concatenate([v, ones[0 : v.shape[0]]], axis=1)
    return jnp.dot(p, v, preferred_element_type=F32)


def early_body(*refs):
    q_refs, k_refs = refs[0:NX], refs[NX : NX + HALF]
    outs, s_ref = refs[NX + HALF : NX + HALF + 2 * NX], refs[-1]
    k_times = [times_of(k_ref, 2 * VID + 2 * AUD) for k_ref in k_refs]
    ones = jnp.ones((VID, HD), BF16)

    def start(i, h):
        q_ref = q_refs[i]
        cols = slice(h * HD, (h + 1) * HD)
        column = side_by_side(column_times(q_ref)[VID : VID + AUD])
        near_audio = [jnp.abs(column - t[:, 0:VID]) <= WIN for t in k_times]
        top = scores(q_ref[0 : VID + AUD, cols], k_refs, cols, near_audio, s_ref, (i * HPG + h) % 3)
        return jnp.max(top, axis=1, keepdims=True)

    def end(i, h, top):
        cols = slice(h * HD, (h + 1) * HD)
        acc = 0.0
        for j, k_ref in enumerate(k_refs):
            s = s_ref[(i * HPG + h) % 3, :, j * VID : (j + 1) * VID]
            acc = acc + weigh(s, top, k_ref[VID : 2 * VID, cols], ones)
        total = acc[:, HD:]
        outs[2 * i][:, cols] = acc[:, 0:HD] / total
        outs[2 * i + 1][:, cols] = top * C2 + jnp.log2(total)

    work = [(i, h) for i in range(NX) for h in range(HPG)]
    tops = {}
    for n, item in enumerate(work):
        tops[item] = start(*item)
        if n >= 2:
            end(*work[n - 2], tops[work[n - 2]])
    for item in work[-2:]:
        end(*item, tops[item])


def early(qs, kvs):
    rows, nk = VID + AUD, HALF * VID
    area = NX * rows * nk * HPG
    return pl.pallas_call(
        early_body,
        out_shape=tuple(jax.ShapeDtypeStruct((rows, GW), F32) for _ in range(2 * NX)),
        in_specs=[VMEM] * (NX + HALF),
        out_specs=tuple(VMEM for _ in range(2 * NX)),
        scratch_shapes=[pltpu.VMEM((3, rows, nk), F32)],
        compiler_params=pltpu.CompilerParams(vmem_limit_bytes=16 * 2**20),
        cost_estimate=pl.CostEstimate(flops=6 * area * HD, bytes_accessed=4 << 20, transcendentals=area),
        name="early",
    )(*qs, *kvs)


def late_body(q_ref, o_ref, l_ref, *refs):
    k_refs, out, s_ref = refs[0:NKB], refs[NKB], refs[NKB + 1]
    rows = VID + AUD
    half = k_refs[HALF:]
    ka_times = place([times_of(k_ref, 2 * VID + 2 * AUD)[:, VID:] for k_ref in k_refs])
    k_times = [times_of(k_ref, 2 * VID + 2 * AUD) for k_ref in half]
    column = column_times(q_ref)
    near_video = jnp.abs(column[0:VID] - ka_times) <= WIN
    column = side_by_side(column[VID:rows])
    near_audio = [jnp.abs(column - t[:, 0:VID]) <= WIN for t in k_times]
    ones = jnp.ones((VID, HD), BF16)
    eye = lax.broadcasted_iota(jnp.int32, (HD, HD), 0) == lax.broadcasted_iota(jnp.int32, (HD, HD), 1)
    which = lax.broadcasted_iota(jnp.int32, (AUX, GW), 0)
    first = HALF * VID

    def start(h):
        cols = slice(h * HD, (h + 1) * HD)
        q = q_ref[0:rows, cols]
        top = scores(q, half, cols, near_audio, s_ref, h)
        s = dot_nt(q, jnp.concatenate([k[2 * VID : 2 * VID + AUD, cols] for k in k_refs], axis=0))
        s = jnp.concatenate([jnp.where(near_video, s[0:VID], NEG), s[VID:]], axis=0)
        s_ref[h, :, first:] = s
        return jnp.max(jnp.maximum(top, s), axis=1, keepdims=True)

    def end(h, top):
        cols = slice(h * HD, (h + 1) * HD)
        at = 2 * VID + AUD
        acc = weigh(s_ref[h, :, first:], top, jnp.concatenate([k[at : at + AUD, cols] for k in k_refs], axis=0), ones)
        for j, k_ref in enumerate(half):
            acc = acc + weigh(s_ref[h, :, j * VID : (j + 1) * VID], top, k_ref[VID : 2 * VID, cols], ones)
        base = top * C2
        before = l_ref[:, cols]
        most = jnp.maximum(base, before)
        w_here, w_before = jnp.exp2(base - most), jnp.exp2(before - most)
        total = acc[:, HD:] * w_here + w_before
        out[0:rows, cols] = ((acc[:, 0:HD] * w_here + o_ref[:, cols] * w_before) / total).astype(BF16)
        lse = most + jnp.log2(total)
        row = jnp.concatenate(
            [
                jnp.sum(jnp.where(eye[0:n], lse[a : a + n], 0.0), axis=0, keepdims=True)
                for a, n in ((0, HD), (HD, HD), (VID, AUD))
            ],
            axis=1,
        )
        hi = row.astype(BF16).astype(F32)
        mid = (row - hi).astype(BF16).astype(F32)
        low = row - hi - mid
        return jnp.where(which == 3 * h, hi, jnp.where(which == 3 * h + 1, mid, jnp.where(which == 3 * h + 2, low, 0.0)))

    tops = [start(h) for h in range(HPG)]
    out[rows:, :] = sum(end(h, tops[h]) for h in range(HPG)).astype(BF16)


def late(q, state, kvs):
    rows, nk = VID + AUD, HALF * VID + NKB * AUD
    area = rows * nk * HPG
    return pl.pallas_call(
        late_body,
        out_shape=jax.ShapeDtypeStruct((QROWS, GW), BF16),
        in_specs=[VMEM] * (3 + NKB),
        out_specs=VMEM,
        scratch_shapes=[pltpu.VMEM((HPG, rows, nk), F32)],
        compiler_params=pltpu.CompilerParams(vmem_limit_bytes=16 * 2**20),
        cost_estimate=pl.CostEstimate(flops=6 * area * HD, bytes_accessed=5 << 20, transcendentals=area),
        name="late",
    )(q, *state, *kvs)


def combine_body(a_ref, b_ref, c_ref, d_ref, video_out, audio_out):
    refs = (a_ref, b_ref, c_ref, d_ref)
    rows = VID + AUD
    which = lax.broadcasted_iota(jnp.int32, (AUX, HD), 0)
    for h in range(HPG):
        pick = jnp.where((which >= 3 * h) & (which < 3 * h + 3), 1.0, 0.0).astype(BF16)
        lses = [dot_tn(ref[rows:, :], pick)[0:rows] for ref in refs]
        top = functools.reduce(jnp.maximum, lses)
        weights = [jnp.exp2(x - top) for x in lses]
        scale = 1.0 / sum(weights)
        cols = slice(h * HD, (h + 1) * HD)
        out = sum(ref[0:rows, cols].astype(F32) * (w * scale) for ref, w in zip(refs, weights, strict=True))
        out = out.astype(BF16)
        for g in range(NZ):
            video_out[g, :, cols] = out[g * TOK : (g + 1) * TOK]
        audio_out[:, cols] = out[VID:]


def combine(parts):
    return pl.pallas_call(
        combine_body,
        out_shape=(
            jax.ShapeDtypeStruct((NZ, TOK, GW), BF16),
            jax.ShapeDtypeStruct((AUD, GW), BF16),
        ),
        in_specs=[VMEM] * NX,
        out_specs=(VMEM, VMEM),
        compiler_params=SMALL,
        name="combine",
    )(*parts)


def shift(x, axis, n, k):
    return lax.ppermute(x, axis, [(i, (i + k) % n) for i in range(n)])


def swap_group(x):
    pairs = [(a * NZ + b, b * NZ + a) for a in range(NZ) for b in range(NZ)]
    return lax.ppermute(x, ("x", "yh", "z"), pairs)


def on_device(video_q, video_k, video_v, audio_q, audio_k, audio_v, align):
    aud = swap_group(jnp.concatenate([audio_q, audio_k, audio_v], axis=1))
    got = lax.all_to_all(
        pack(align, video_q, video_k, video_v), "z", split_axis=0, concat_axis=0, tiled=True
    )
    q_own, kv_own = join(got, aud)
    y = ("yh", "yl")
    core = functools.partial(shift, axis="c", n=NC, k=1)
    far, near = shift(kv_own, y, NY, 2), core(kv_own)
    qs = [shift(q_own, "x", NX, k) for k in (2, 1, 3)]
    right, left = [shift(kv_own, y, NY, k) for k in (1, 3)]
    qs = qs + [q_own]
    first = [kv_own, far, near, core(far)]
    state = early(qs, first)
    kvs = first + [right, left, core(right), core(left)]
    parts = [late(q, state[2 * i : 2 * i + 2], kvs) for i, q in enumerate(qs)]
    back = [shift(p, "x", NX, -k) for p, k in zip(parts, (2, 1, 3))]
    video, audio = combine(parts[3:] + back)
    video = lax.all_to_all(video, "z", split_axis=0, concat_axis=0, tiled=True)
    return video.transpose(1, 0, 2).reshape(TOK, NZ * GW), swap_group(audio)


def solution(mesh):
    grid = Mesh(np.asarray(mesh.devices).reshape(4, 2, 2, 8, 2), ("x", "yh", "yl", "z", "c"))
    seq, head = ("yl", "z", "c"), ("x", "yh")
    rows = P(seq + head, None)
    audio = P(seq, head)
    return jax.shard_map(
        on_device,
        mesh=grid,
        in_specs=(rows, rows, rows, audio, audio, audio, P(seq + head)),
        out_specs=(rows, audio),
        check_vma=False,
    )
```

time: 221 us -> 101 us (0.46)
  the two profiles are of different devices: /device:TPU:24 before, /device:TPU:152 now
where the time goes in v2:
time: 101 us; the launch traced here: 100 us
  waiting for transfers between devices  47.7 us (47%)
  starting transfers between devices  34.9 us (35%)
  Pallas kernels  15.5 us (15%)
  local copies, waits for them, and re-layouts  1.31 us (1%)
    ppermute x2, waiting for transfers between devices, swap_group(): return lax.ppermute(x, ('x', 'yh', 'z'), pairs)  25.6 us
    ppermute x13, waiting for transfers between devices, shift(): return lax.ppermute(x, axis, [(i, (i + k) % n) for i in range(n)])  22.1 us
    ppermute x13, starting transfers between devices, shift(): return lax.ppermute(x, axis, [(i, (i + k) % n) for i in range(n)])  12.4 us
    ppermute x2, starting transfers between devices, swap_group(): return lax.ppermute(x, ('x', 'yh', 'z'), pairs)  7.93 us
    all_to_all x1, starting transfers between devices, on_device(): lax.all_to_all(pack(align, video_q, video_k, video_v), 'z', split_axis=0,...  7.35 us
    all_to_all x1, starting transfers between devices, on_device(): video = lax.all_to_all(video, 'z', split_axis=0, concat_axis=0, tiled=True)  7.21 us
    pallas_call x4, Pallas kernels, late(): pl.pallas_call(late_body, out_shape=jax.ShapeDtypeStruct((QROWS, GW), BF1...  7.13 us
    pallas_call x1, Pallas kernels, early(): pl.pallas_call(early_body, out_shape=tuple((jax.ShapeDtypeStruct((rows, G...  4.81 us
  transfers between devices with their start and end apart: 17, of which 8 were waited for; matrix products, arithmetic and copies ran while one was open for 0% of the time, Pallas kernels for 10%

profile of v2, /device:TPU:152, one launch (start us, length us, event | category | flops | bytes accessed | tf_op | source)
XLA Modules:
  0.0 100.3 jit_solution(5307115542024141838)
XLA Ops:
  0.6 2.1 %pack.1 = bf16[8,112,384]{2,1,0:T(8,128)(2,1)} custom-call(s32[32]{0:T(128)} %align_ref.1, bf16[32,3072]{1,0:T(8,128)(2,1)} %q_ref.1, bf16[32,3072]{1,0:T(8,128)(2,1)} %k_ref.1, bf16[32,3072]{1,0:T(8,128)(2,1)} %v_ref.1), custom_call_target="tpu_custom_call" | custom-call | tf_op jit(solution)/shard_map/pack/pallas_call | solution.py:52
  2.7 7.3 %all-to-all-start = ((bf16[8,112,384]{2,1,0:T(8,128)(2,1)}), bf16[8,112,384]{2,1,0:T(8,128)(2,1)S(1)}, u32[]{:S(2)}, u32[]{:S(2)}) async-start(bf16[8,112,384]{2,1,0:T(8,128)(2,1)} %pack.1), calls=%async_computation | async-start | bytes 1376256 | tf_op jit(solution)/shard_map/all_to_all | solution.py:307
  10.1 5.6 %collective-permute-start = (bf16[16,1152]{1,0:T(8,128)(2,1)S(1)}, bf16[16,1152]{1,0:T(8,128)(2,1)S(1)}, u32[]{:S(2)}, u32[]{:S(2)}) collective-permute-start(bf16[16,1152]{1,0:T(8,128)(2,1)S(1)} %pad_maximum_fusion), channel_id=1, source_target_pairs={{0,0},{2,32},{4,64},{6,96},{8,128},{10,160},{12,192},{14,224},{32,... | collective-permute-start | bytes 110600 | tf_op jit(solution)/shard_map/ppermute | solution.py:302
  15.7 14.5 %collective-permute-done.aud_ref = bf16[16,1152]{1,0:T(8,128)(2,1)S(1)} collective-permute-done((bf16[16,1152]{1,0:T(8,128)(2,1)S(1)}, bf16[16,1152]{1,0:T(8,128)(2,1)S(1)}, u32[]{:S(2)}, u32[]{:S(2)}) %collective-permute-start) | collective-permute-done | bytes 36896 | tf_op jit(solution)/shard_map/ppermute | solution.py:302
  30.4 1.4 %collective-permute-start.3 = (bf16[288,384]{1,0:T(8,128)(2,1)S(1)}, bf16[288,384]{1,0:T(8,128)(2,1)S(1)}, u32[]{:S(2)}, u32[]{:S(2)}) collective-permute-start(bf16[288,384]{1,0:T(8,128)(2,1)S(1)} %get-tuple-element.14.refs_3_.q_ref), channel_id=1, source_target_pairs={{0,192},{64,0},{128,64},{192,128},{1,193},{65,1},{129,65},{193,129... | collective-permute-start | bytes 663560 | tf_op jit(solution)/shard_map/ppermute | solution.py:297
  31.8 3.2 %collective-permute-start.7 = (bf16[560,384]{1,0:T(8,128)(2,1)S(1)}, bf16[560,384]{1,0:T(8,128)(2,1)S(1)}, u32[]{:S(2)}, u32[]{:S(2)}) collective-permute-start(bf16[560,384]{1,0:T(8,128)(2,1)S(1)} %get-tuple-element.15.refs_4_.refs_0_), channel_id=1, source_target_pairs={{0,16},{16,32},{32,48},{48,0},{1,17},{17,33},{33,49},{49,1},{2,18}... | collective-permute-start | bytes 1290248 | tf_op jit(solution)/shard_map/ppermute | solution.py:297
  35.7 1.9 %collective-permute-done.3.refs_2_.q_ref = bf16[288,384]{1,0:T(8,128)(2,1)S(1)} collective-permute-done((bf16[288,384]{1,0:T(8,128)(2,1)S(1)}, bf16[288,384]{1,0:T(8,128)(2,1)S(1)}, u32[]{:S(2)}, u32[]{:S(2)}) %collective-permute-start.3) | collective-permute-done | bytes 221216 | tf_op jit(solution)/shard_map/ppermute | solution.py:297
  37.6 7.1 %collective-permute-done.4.refs_5_.refs_1_ = bf16[560,384]{1,0:T(8,128)(2,1)S(1)} collective-permute-done((bf16[560,384]{1,0:T(8,128)(2,1)S(1)}, bf16[560,384]{1,0:T(8,128)(2,1)S(1)}, u32[]{:S(2)}, u32[]{:S(2)}) %collective-permute-start.4) | collective-permute-done | bytes 430112 | tf_op jit(solution)/shard_map/ppermute | solution.py:297
  44.7 1.6 %collective-permute-start.1 = (bf16[288,384]{1,0:T(8,128)(2,1)S(1)}, bf16[288,384]{1,0:T(8,128)(2,1)S(1)}, u32[]{:S(2)}, u32[]{:S(2)}) collective-permute-start(bf16[288,384]{1,0:T(8,128)(2,1)S(1)} %get-tuple-element.14.refs_3_.q_ref), channel_id=1, source_target_pairs={{0,128},{64,192},{128,0},{192,64},{1,129},{65,193},{129,1},{193,65... | collective-permute-start | bytes 663560 | tf_op jit(solution)/shard_map/ppermute | solution.py:297
  46.3 6.4 %collective-permute-done.8.refs_5_ = bf16[560,384]{1,0:T(8,128)(2,1)S(1)} collective-permute-done((bf16[560,384]{1,0:T(8,128)(2,1)S(1)}, bf16[560,384]{1,0:T(8,128)(2,1)S(1)}, u32[]{:S(2)}, u32[]{:S(2)}) %collective-permute-start.8) | collective-permute-done | bytes 430112 | tf_op jit(solution)/shard_map/ppermute | solution.py:297
  53.2 0.9 collective-permute-done.1.refs_0_.q_ref
  54.1 4.8 %early.1 = (f32[272,384]{1,0:T(8,128)S(1)}, f32[272,384]{1,0:T(8,128)S(1)}, f32[272,384]{1,0:T(8,128)S(1)}, f32[272,384]{1,0:T(8,128)S(1)}, f32[272,384]{1,0:T(8...) custom-call(bf16[288,384]{1,0:T(8,128)(2,1)S(1)} %collective-permute-done.1.refs_0_.q_ref, ...), custom_call_target="tpu_custom_call" | custom-call | flops 2566914048 | bytes 4194304 | tf_op jit(solution)/shard_map/early/pallas_call | solution.py:184
  58.9 1.8 %late.5 = bf16[288,384]{1,0:T(8,128)(2,1)S(1)} custom-call(bf16[288,384]{1,0:T(8,128)(2,1)S(1)} %collective-permute-done.1.refs_0_.q_ref, f32[272,384]{1,0:T(8,128)S(1)} %get-tuple-element.18.o_ref, f32[272,384]{1,0:T(8,128)S(1)} %get-tuple-element.19.l_ref, bf16[560,384]{1,0:T(8,128)(2,1)S(1)} %get-tuple-element.15.refs_4_.refs_0_, ...), custom_call_target="tpu_custom_call" | custom-call | flops 721944576 | bytes 5242880 | tf_op jit(solution)/shard_map/late/pallas_call | solution.py:252
  60.7 1.7 %collective-permute-start.11 = (bf16[288,384]{1,0:T(8,128)(2,1)S(1)}, bf16[288,384]{1,0:T(8,128)(2,1)S(1)}, u32[]{:S(2)}, u32[]{:S(2)}) collective-permute-start(bf16[288,384]{1,0:T(8,128)(2,1)S(1)} %late.5), channel_id=1, source_target_pairs={{0,128},{64,192},{128,0},{192,64},{1,129},{65,193},{129,1},{193,65... | collective-permute-start | bytes 663560 | tf_op jit(solution)/shard_map/ppermute | solution.py:297
  62.4 1.8 %late.6 = bf16[288,384]{1,0:T(8,128)(2,1)S(1)} custom-call(bf16[288,384]{1,0:T(8,128)(2,1)S(1)} %collective-permute-done.2.refs_1_.q_ref, f32[272,384]{1,0:T(8,128)S(1)} %get-tuple-element.20.o_ref, f32[272,384]{1,0:T(8,128)S(1)} %get-tuple-element.21.l_ref, bf16[560,384]{1,0:T(8,128)(2,1)S(1)} %get-tuple-element.15.refs_4_.refs_0_, ...), custom_call_target="tpu_custom_call" | custom-call | flops 721944576 | bytes 5242880 | tf_op jit(solution)/shard_map/late/pallas_call | solution.py:252
  64.2 2.9 %collective-permute-start.12 = (bf16[288,384]{1,0:T(8,128)(2,1)S(1)}, bf16[288,384]{1,0:T(8,128)(2,1)S(1)}, u32[]{:S(2)}, u32[]{:S(2)}) collective-permute-start(bf16[288,384]{1,0:T(8,128)(2,1)S(1)} %late.6), channel_id=1, source_target_pairs={{0,192},{64,0},{128,64},{192,128},{1,193},{65,1},{129,65},{193,129... | collective-permute-start | bytes 663560 | tf_op jit(solution)/shard_map/ppermute | solution.py:297
  67.1 1.8 %late.7 = bf16[288,384]{1,0:T(8,128)(2,1)S(1)} custom-call(bf16[288,384]{1,0:T(8,128)(2,1)S(1)} %collective-permute-done.3.refs_2_.q_ref, f32[272,384]{1,0:T(8,128)S(1)} %get-tuple-element.22.o_ref, f32[272,384]{1,0:T(8,128)S(1)} %get-tuple-element.23.l_ref, bf16[560,384]{1,0:T(8,128)(2,1)S(1)} %get-tuple-element.15.refs_4_.refs_0_, ...), custom_call_target="tpu_custom_call" | custom-call | flops 721944576 | bytes 5242880 | tf_op jit(solution)/shard_map/late/pallas_call | solution.py:252
  69.2 1.8 %late.4.a_ref = bf16[288,384]{1,0:T(8,128)(2,1)S(1)} custom-call(bf16[288,384]{1,0:T(8,128)(2,1)S(1)} %get-tuple-element.14.refs_3_.q_ref, f32[272,384]{1,0:T(8,128)S(1)} %get-tuple-element.16.o_ref, f32[272,384]{1,0:T(8,128)S(1)} %get-tuple-element.17.l_ref, bf16[560,384]{1,0:T(8,128)(2,1)S(1)} %get-tuple-element.15.refs_4_.refs_0_, ...), custom_call_target="tpu_custom_call" | custom-call | flops 721944576 | bytes 5242880 | tf_op jit(solution)/shard_map/late/pallas_call | solution.py:252
  71.0 1.8 %collective-permute-done.12.c_ref = bf16[288,384]{1,0:T(8,128)(2,1)S(1)} collective-permute-done((bf16[288,384]{1,0:T(8,128)(2,1)S(1)}, bf16[288,384]{1,0:T(8,128)(2,1)S(1)}, u32[]{:S(2)}, u32[]{:S(2)}) %collective-permute-start.12) | collective-permute-done | bytes 221216 | tf_op jit(solution)/shard_map/ppermute | solution.py:297
  72.8 4.1 %collective-permute-done.13.d_ref = bf16[288,384]{1,0:T(8,128)(2,1)S(1)} collective-permute-done((bf16[288,384]{1,0:T(8,128)(2,1)S(1)}, bf16[288,384]{1,0:T(8,128)(2,1)S(1)}, u32[]{:S(2)}, u32[]{:S(2)}) %collective-permute-start.13) | collective-permute-done | bytes 221216 | tf_op jit(solution)/shard_map/ppermute | solution.py:297
  76.9 1.4 %combine.1 = (bf16[8,32,384]{2,1,0:T(8,128)(2,1)}, bf16[16,384]{1,0:T(8,128)(2,1)S(1)}) custom-call(bf16[288,384]{1,0:T(8,128)(2,1)S(1)} %late.4.a_ref, bf16[288,384]{1,0:T(8,128)(2,1)S(1)} %collective-permute-done.11.b_ref, bf16[288,384]{1,0:T(8,128)(2,1)S(1)} %collective-permute-done.12.c_ref, bf16[288,384]{1,0:T(8,128)(2,1)S(1)} %collective-permute-done.13.d_ref), custom_call_target="tpu_custom_call" | custom-call | tf_op jit(solution)/shard_map/combine/pallas_call | solution.py:283
  78.4 7.2 %all-to-all-start.1 = ((bf16[8,32,384]{2,1,0:T(8,128)(2,1)}), bf16[8,32,384]{2,1,0:T(8,128)(2,1)S(1)}, u32[]{:S(2)}, u32[]{:S(2)}) async-start(bf16[8,32,384]{2,1,0:T(8,128)(2,1)} %get-tuple-element.24), calls=%async_computation.1 | async-start | bytes 393216 | tf_op jit(solution)/shard_map/all_to_all | solution.py:323
  85.6 2.3 %collective-permute-start.14 = (bf16[16,384]{1,0:T(8,128)(2,1)S(1)}, bf16[16,384]{1,0:T(8,128)(2,1)S(1)}, u32[]{:S(2)}, u32[]{:S(2)}) collective-permute-start(bf16[16,384]{1,0:T(8,128)(2,1)S(1)} %get-tuple-element.25), channel_id=1, source_target_pairs={{0,0},{2,32},{4,64},{6,96},{8,128},{10,160},{12,192},{14,224},{32,... | collective-permute-start | bytes 36872 | tf_op jit(solution)/shard_map/ppermute | solution.py:302
  87.9 11.1 %collective-permute-done.14 = bf16[16,384]{1,0:T(8,128)(2,1)S(1)} collective-permute-done((bf16[16,384]{1,0:T(8,128)(2,1)S(1)}, bf16[16,384]{1,0:T(8,128)(2,1)S(1)}, u32[]{:S(2)}, u32[]{:S(2)}) %collective-permute-start.14) | collective-permute-done | bytes 12320 | tf_op jit(solution)/shard_map/ppermute | solution.py:302
  (27 shorter events, 3.1 us)
Async XLA Ops:
  2.7 7.4 %copy-start = (bf16[16,384]{1,0:T(8,128)(2,1)S(1)}, bf16[16,384]{1,0:T(8,128)(2,1)}, u32[]{:S(2)}) copy-start(bf16[16,384]{1,0:T(8,128)(2,1)} %param.12) | copy-start | bytes 36868
  2.7 7.4 %copy-start.1 = (bf16[16,384]{1,0:T(8,128)(2,1)S(1)}, bf16[16,384]{1,0:T(8,128)(2,1)}, u32[]{:S(2)}) copy-start(bf16[16,384]{1,0:T(8,128)(2,1)} %param.11) | copy-start | bytes 36868
  2.7 7.4 %copy-start.2 = (bf16[16,384]{1,0:T(8,128)(2,1)S(1)}, bf16[16,384]{1,0:T(8,128)(2,1)}, u32[]{:S(2)}) copy-start(bf16[16,384]{1,0:T(8,128)(2,1)} %param.10) | copy-start | bytes 36868
  2.7 27.5 %all-to-all-start = ((bf16[8,112,384]{2,1,0:T(8,128)(2,1)}), bf16[8,112,384]{2,1,0:T(8,128)(2,1)S(1)}, u32[]{:S(2)}, u32[]{:S(2)}) async-start(bf16[8,112,384]{2,1,0:T(8,128)(2,1)} %pack.1), calls=%async_computation | async-start | bytes 1376256 | tf_op jit(solution)/shard_map/all_to_all | solution.py:307
  10.1 20.1 %collective-permute-start = (bf16[16,1152]{1,0:T(8,128)(2,1)S(1)}, bf16[16,1152]{1,0:T(8,128)(2,1)S(1)}, u32[]{:S(2)}, u32[]{:S(2)}) collective-permute-start(bf16[16,1152]{1,0:T(8,128)(2,1)S(1)} %pad_maximum_fusion), channel_id=1, source_target_pairs={{0,0},{2,32},{4,64},{6,96},{8,128},{10,160},{12,192},{14,224},{32,... | collective-permute-start | bytes 110600 | tf_op jit(solution)/shard_map/ppermute | solution.py:302
  30.3 14.4 %collective-permute-start.4 = (bf16[560,384]{1,0:T(8,128)(2,1)S(1)}, bf16[560,384]{1,0:T(8,128)(2,1)S(1)}, u32[]{:S(2)}, u32[]{:S(2)}) collective-permute-start(bf16[560,384]{1,0:T(8,128)(2,1)S(1)} %get-tuple-element.15.refs_4_.refs_0_), channel_id=1, source_target_pairs={{0,32},{16,48},{32,0},{48,16},{1,33},{17,49},{33,1},{49,17},{2,34}... | collective-permute-start | bytes 1290248 | tf_op jit(solution)/shard_map/ppermute | solution.py:297
  30.4 7.2 %collective-permute-start.3 = (bf16[288,384]{1,0:T(8,128)(2,1)S(1)}, bf16[288,384]{1,0:T(8,128)(2,1)S(1)}, u32[]{:S(2)}, u32[]{:S(2)}) collective-permute-start(bf16[288,384]{1,0:T(8,128)(2,1)S(1)} %get-tuple-element.14.refs_3_.q_ref), channel_id=1, source_target_pairs={{0,192},{64,0},{128,64},{192,128},{1,193},{65,1},{129,65},{193,129... | collective-permute-start | bytes 663560 | tf_op jit(solution)/shard_map/ppermute | solution.py:297
  31.8 21.0 %collective-permute-start.8 = (bf16[560,384]{1,0:T(8,128)(2,1)S(1)}, bf16[560,384]{1,0:T(8,128)(2,1)S(1)}, u32[]{:S(2)}, u32[]{:S(2)}) collective-permute-start(bf16[560,384]{1,0:T(8,128)(2,1)S(1)} %get-tuple-element.15.refs_4_.refs_0_), channel_id=1, source_target_pairs={{0,48},{16,0},{32,16},{48,32},{1,49},{17,1},{33,17},{49,33},{2,50}... | collective-permute-start | bytes 1290248 | tf_op jit(solution)/shard_map/ppermute | solution.py:297
  31.8 21.0 %collective-permute-start.7 = (bf16[560,384]{1,0:T(8,128)(2,1)S(1)}, bf16[560,384]{1,0:T(8,128)(2,1)S(1)}, u32[]{:S(2)}, u32[]{:S(2)}) collective-permute-start(bf16[560,384]{1,0:T(8,128)(2,1)S(1)} %get-tuple-element.15.refs_4_.refs_0_), channel_id=1, source_target_pairs={{0,16},{16,32},{32,48},{48,0},{1,17},{17,33},{33,49},{49,1},{2,18}... | collective-permute-start | bytes 1290248 | tf_op jit(solution)/shard_map/ppermute | solution.py:297
  35.0 9.7 %collective-permute-start.2 = (bf16[288,384]{1,0:T(8,128)(2,1)S(1)}, bf16[288,384]{1,0:T(8,128)(2,1)S(1)}, u32[]{:S(2)}, u32[]{:S(2)}) collective-permute-start(bf16[288,384]{1,0:T(8,128)(2,1)S(1)} %get-tuple-element.14.refs_3_.q_ref), channel_id=1, source_target_pairs={{0,64},{64,128},{128,192},{192,0},{1,65},{65,129},{129,193},{193,1... | collective-permute-start | bytes 663560 | tf_op jit(solution)/shard_map/ppermute | solution.py:297
  37.6 16.5 %collective-permute-start.5 = (bf16[560,384]{1,0:T(8,128)(2,1)S(1)}, bf16[560,384]{1,0:T(8,128)(2,1)S(1)}, u32[]{:S(2)}, u32[]{:S(2)}) collective-permute-start(bf16[560,384]{1,0:T(8,128)(2,1)S(1)} %get-tuple-element.15.refs_4_.refs_0_), channel_id=1, source_target_pairs={{0,1},{1,0},{2,3},{3,2},{4,5},{5,4},{6,7},{7,6},{8,9},{9,8},{10,11... | collective-permute-start | bytes 1290248 | tf_op jit(solution)/shard_map/ppermute | solution.py:297
  44.7 9.4 %collective-permute-start.6 = (bf16[560,384]{1,0:T(8,128)(2,1)S(1)}, bf16[560,384]{1,0:T(8,128)(2,1)S(1)}, u32[]{:S(2)}, u32[]{:S(2)}) collective-permute-start(bf16[560,384]{1,0:T(8,128)(2,1)S(1)} %collective-permute-done.4.refs_5_.refs_1_), channel_id=1, source_target_pairs={{0,1},{1,0},{2,3},{3,2},{4,5},{5,4},{6,7},{7,6},{8,9},{9,8},{10,11... | collective-permute-start | bytes 1290248 | tf_op jit(solution)/shard_map/ppermute | solution.py:297
  44.7 9.3 %collective-permute-start.1 = (bf16[288,384]{1,0:T(8,128)(2,1)S(1)}, bf16[288,384]{1,0:T(8,128)(2,1)S(1)}, u32[]{:S(2)}, u32[]{:S(2)}) collective-permute-start(bf16[288,384]{1,0:T(8,128)(2,1)S(1)} %get-tuple-element.14.refs_3_.q_ref), channel_id=1, source_target_pairs={{0,128},{64,192},{128,0},{192,64},{1,129},{65,193},{129,1},{193,65... | collective-permute-start | bytes 663560 | tf_op jit(solution)/shard_map/ppermute | solution.py:297
  52.7 6.2 %collective-permute-start.10 = (bf16[560,384]{1,0:T(8,128)(2,1)S(1)}, bf16[560,384]{1,0:T(8,128)(2,1)S(1)}, u32[]{:S(2)}, u32[]{:S(2)}) collective-permute-start(bf16[560,384]{1,0:T(8,128)(2,1)S(1)} %collective-permute-done.8.refs_5_), channel_id=1, source_target_pairs={{0,1},{1,0},{2,3},{3,2},{4,5},{5,4},{6,7},{7,6},{8,9},{9,8},{10,11... | collective-permute-start | bytes 1290248 | tf_op jit(solution)/shard_map/ppermute | solution.py:297
  52.7 6.2 %collective-permute-start.9 = (bf16[560,384]{1,0:T(8,128)(2,1)S(1)}, bf16[560,384]{1,0:T(8,128)(2,1)S(1)}, u32[]{:S(2)}, u32[]{:S(2)}) collective-permute-start(bf16[560,384]{1,0:T(8,128)(2,1)S(1)} %collective-permute-done.7.refs_4_), channel_id=1, source_target_pairs={{0,1},{1,0},{2,3},{3,2},{4,5},{5,4},{6,7},{7,6},{8,9},{9,8},{10,11... | collective-permute-start | bytes 1290248 | tf_op jit(solution)/shard_map/ppermute | solution.py:297
  60.7 10.3 %collective-permute-start.11 = (bf16[288,384]{1,0:T(8,128)(2,1)S(1)}, bf16[288,384]{1,0:T(8,128)(2,1)S(1)}, u32[]{:S(2)}, u32[]{:S(2)}) collective-permute-start(bf16[288,384]{1,0:T(8,128)(2,1)S(1)} %late.5), channel_id=1, source_target_pairs={{0,128},{64,192},{128,0},{192,64},{1,129},{65,193},{129,1},{193,65... | collective-permute-start | bytes 663560 | tf_op jit(solution)/shard_map/ppermute | solution.py:297
  64.2 8.7 %collective-permute-start.12 = (bf16[288,384]{1,0:T(8,128)(2,1)S(1)}, bf16[288,384]{1,0:T(8,128)(2,1)S(1)}, u32[]{:S(2)}, u32[]{:S(2)}) collective-permute-start(bf16[288,384]{1,0:T(8,128)(2,1)S(1)} %late.6), channel_id=1, source_target_pairs={{0,192},{64,0},{128,64},{192,128},{1,193},{65,1},{129,65},{193,129... | collective-permute-start | bytes 663560 | tf_op jit(solution)/shard_map/ppermute | solution.py:297
  68.9 8.0 %collective-permute-start.13 = (bf16[288,384]{1,0:T(8,128)(2,1)S(1)}, bf16[288,384]{1,0:T(8,128)(2,1)S(1)}, u32[]{:S(2)}, u32[]{:S(2)}) collective-permute-start(bf16[288,384]{1,0:T(8,128)(2,1)S(1)} %late.7), channel_id=1, source_target_pairs={{0,64},{64,128},{128,192},{192,0},{1,65},{65,129},{129,193},{193,1... | collective-permute-start | bytes 663560 | tf_op jit(solution)/shard_map/ppermute | solution.py:297
  78.4 20.6 %all-to-all-start.1 = ((bf16[8,32,384]{2,1,0:T(8,128)(2,1)}), bf16[8,32,384]{2,1,0:T(8,128)(2,1)S(1)}, u32[]{:S(2)}, u32[]{:S(2)}) async-start(bf16[8,32,384]{2,1,0:T(8,128)(2,1)} %get-tuple-element.24), calls=%async_computation.1 | async-start | bytes 393216 | tf_op jit(solution)/shard_map/all_to_all | solution.py:323
  85.6 13.4 %collective-permute-start.14 = (bf16[16,384]{1,0:T(8,128)(2,1)S(1)}, bf16[16,384]{1,0:T(8,128)(2,1)S(1)}, u32[]{:S(2)}, u32[]{:S(2)}) collective-permute-start(bf16[16,384]{1,0:T(8,128)(2,1)S(1)} %get-tuple-element.25), channel_id=1, source_target_pairs={{0,0},{2,32},{4,64},{6,96},{8,128},{10,160},{12,192},{14,224},{32,... | collective-permute-start | bytes 36872 | tf_op jit(solution)/shard_map/ppermute | solution.py:302

commit v3 on v2

--- a/solution.py
+++ b/solution.py
@@ -20,7 +20,7 @@
 QROWS = VID + AUD + AUX
 KROWS = 2 * VID + 2 * AUD + AUX
 NKB = NY * NC
-HALF = NKB // 2
+EARLY = 6
 WIN = 64.0
 NEG = -1e30
 C2 = HD**-0.5 * 1.4426950408889634
@@ -68,7 +68,7 @@
 
 
 def join_body(got_ref, aud_ref, q_out, kv_out):
-    block = lax.axis_index("yl") * 16 + (lax.axis_index("x") * 2 + lax.axis_index("yh")) * 2 + lax.axis_index("c")
+    block = lax.axis_index("yl") * 16 + audio_z() * 2 + lax.axis_index("c")
     total = audio_times(block * AUD)
     for g in range(NZ):
         at = g * TOK
@@ -87,8 +87,8 @@
     return pl.pallas_call(
         join_body,
         out_shape=(
-            jax.ShapeDtypeStruct((QROWS, GW), BF16),
-            jax.ShapeDtypeStruct((KROWS, GW), BF16),
+            pltpu.VMEM((QROWS, GW), BF16),
+            pltpu.VMEM((KROWS, GW), BF16),
         ),
         in_specs=[VMEM, VMEM],
         out_specs=(VMEM, VMEM),
@@ -120,7 +120,7 @@
 def column_times(q_ref):
     which = lax.broadcasted_iota(jnp.int32, (AUX, HD), 0)
     pick = jnp.where(which == 0, 16.0, jnp.where(which == 1, 1.0, 0.0)).astype(BF16)
-    return dot_tn(q_ref[VID + AUD :, :], pick)
+    return dot_tn(q_ref[VID + AUD : QROWS, :], pick)
 
 
 def side_by_side(x):
@@ -145,8 +145,9 @@
 
 
 def early_body(*refs):
-    q_refs, k_refs = refs[0:NX], refs[NX : NX + HALF]
-    outs, s_ref = refs[NX + HALF : NX + HALF + 2 * NX], refs[-1]
+    n = (len(refs) - EARLY - 1) // 3
+    q_refs, k_refs = refs[0:n], refs[n : n + EARLY]
+    outs, s_ref = refs[n + EARLY : -1], refs[-1]
     k_times = [times_of(k_ref, 2 * VID + 2 * AUD) for k_ref in k_refs]
     ones = jnp.ones((VID, HD), BF16)
 
@@ -168,24 +169,24 @@
         outs[2 * i][:, cols] = acc[:, 0:HD] / total
         outs[2 * i + 1][:, cols] = top * C2 + jnp.log2(total)
 
-    work = [(i, h) for i in range(NX) for h in range(HPG)]
+    work = [(i, h) for i in range(n) for h in range(HPG)]
     tops = {}
-    for n, item in enumerate(work):
+    for m, item in enumerate(work):
         tops[item] = start(*item)
-        if n >= 2:
-            end(*work[n - 2], tops[work[n - 2]])
+        if m >= 2:
+            end(*work[m - 2], tops[work[m - 2]])
     for item in work[-2:]:
         end(*item, tops[item])
 
 
 def early(qs, kvs):
-    rows, nk = VID + AUD, HALF * VID
-    area = NX * rows * nk * HPG
+    n, rows, nk = len(qs), VID + AUD, EARLY * VID
+    area = n * rows * nk * HPG
     return pl.pallas_call(
         early_body,
-        out_shape=tuple(jax.ShapeDtypeStruct((rows, GW), F32) for _ in range(2 * NX)),
-        in_specs=[VMEM] * (NX + HALF),
-        out_specs=tuple(VMEM for _ in range(2 * NX)),
+        out_shape=tuple(jax.ShapeDtypeStruct((rows, GW), F32) for _ in range(2 * n)),
+        in_specs=[VMEM] * (n + EARLY),
+        out_specs=tuple(VMEM for _ in range(2 * n)),
         scratch_shapes=[pltpu.VMEM((3, rows, nk), F32)],
         compiler_params=pltpu.CompilerParams(vmem_limit_bytes=16 * 2**20),
         cost_estimate=pl.CostEstimate(flops=6 * area * HD, bytes_accessed=4 << 20, transcendentals=area),
@@ -194,11 +195,15 @@
 
 
 def late_body(q_ref, o_ref, l_ref, *refs):
-    k_refs, out, s_ref = refs[0:NKB], refs[NKB], refs[NKB + 1]
+    out, s_ref, far_ref, twin_ref = refs[EARLY + 4 :]
     rows = VID + AUD
-    half = k_refs[HALF:]
+    for n, ref in enumerate((far_ref, twin_ref)):
+        ref[0:VID, :] = refs[EARLY + 2 * n][...]
+        ref[VID:, :] = refs[EARLY + 2 * n + 1][...]
+    rest = (far_ref, twin_ref)
+    k_refs = refs[0:EARLY] + rest
     ka_times = place([times_of(k_ref, 2 * VID + 2 * AUD)[:, VID:] for k_ref in k_refs])
-    k_times = [times_of(k_ref, 2 * VID + 2 * AUD) for k_ref in half]
+    k_times = [times_of(k_ref, 2 * VID + 2 * AUD) for k_ref in rest]
     column = column_times(q_ref)
     near_video = jnp.abs(column[0:VID] - ka_times) <= WIN
     column = side_by_side(column[VID:rows])
@@ -206,12 +211,12 @@
     ones = jnp.ones((VID, HD), BF16)
     eye = lax.broadcasted_iota(jnp.int32, (HD, HD), 0) == lax.broadcasted_iota(jnp.int32, (HD, HD), 1)
     which = lax.broadcasted_iota(jnp.int32, (AUX, GW), 0)
-    first = HALF * VID
+    first = len(rest) * VID
 
     def start(h):
         cols = slice(h * HD, (h + 1) * HD)
         q = q_ref[0:rows, cols]
-        top = scores(q, half, cols, near_audio, s_ref, h)
+        top = scores(q, rest, cols, near_audio, s_ref, h)
         s = dot_nt(q, jnp.concatenate([k[2 * VID : 2 * VID + AUD, cols] for k in k_refs], axis=0))
         s = jnp.concatenate([jnp.where(near_video, s[0:VID], NEG), s[VID:]], axis=0)
         s_ref[h, :, first:] = s
@@ -221,7 +226,7 @@
         cols = slice(h * HD, (h + 1) * HD)
         at = 2 * VID + AUD
         acc = weigh(s_ref[h, :, first:], top, jnp.concatenate([k[at : at + AUD, cols] for k in k_refs], axis=0), ones)
-        for j, k_ref in enumerate(half):
+        for j, k_ref in enumerate(rest):
             acc = acc + weigh(s_ref[h, :, j * VID : (j + 1) * VID], top, k_ref[VID : 2 * VID, cols], ones)
         base = top * C2
         before = l_ref[:, cols]
@@ -247,14 +252,18 @@
 
 
 def late(q, state, kvs):
-    rows, nk = VID + AUD, HALF * VID + NKB * AUD
+    rows, nk = VID + AUD, (NKB - EARLY) * VID + NKB * AUD
     area = rows * nk * HPG
     return pl.pallas_call(
         late_body,
         out_shape=jax.ShapeDtypeStruct((QROWS, GW), BF16),
-        in_specs=[VMEM] * (3 + NKB),
+        in_specs=[VMEM] * (3 + EARLY + 4),
         out_specs=VMEM,
-        scratch_shapes=[pltpu.VMEM((HPG, rows, nk), F32)],
+        scratch_shapes=[
+            pltpu.VMEM((HPG, rows, nk), F32),
+            pltpu.VMEM((KROWS, GW), BF16),
+            pltpu.VMEM((KROWS, GW), BF16),
+        ],
         compiler_params=pltpu.CompilerParams(vmem_limit_bytes=16 * 2**20),
         cost_estimate=pl.CostEstimate(flops=6 * area * HD, bytes_accessed=5 << 20, transcendentals=area),
         name="late",
@@ -297,31 +306,62 @@
     return lax.ppermute(x, axis, [(i, (i + k) % n) for i in range(n)])
 
 
-def swap_group(x):
-    pairs = [(a * NZ + b, b * NZ + a) for a in range(NZ) for b in range(NZ)]
-    return lax.ppermute(x, ("x", "yh", "z"), pairs)
+PLACES = ((2, 1), (1, 1), (2, 0), (1, 0), (0, 0), (3, 0), (0, 1), (3, 1))
+
+
+def audio_pairs():
+    pairs = []
+    for group in range(NZ):
+        for ahead, (dx, dy) in enumerate(PLACES):
+            there = ((group // 2 + dx) % NX) * 2 + (group % 2 + dy) % 2
+            pairs.append((group * NZ + (group + ahead) % NZ, there * NZ + group))
+    return pairs
+
+
+def audio_z():
+    group = lax.axis_index("z")
+    dx = lax.rem(lax.axis_index("x") + NX - group // 2, NX)
+    dy = lax.rem(lax.axis_index("yh") + 2 - lax.rem(group, 2), 2)
+    ahead = 0
+    for n, (px, py) in enumerate(PLACES):
+        ahead = jnp.where((dx == px) & (dy == py), n, ahead)
+    return lax.rem(group + ahead, NZ)
+
+
+def to_group(x):
+    return lax.ppermute(x, ("x", "yh", "z"), audio_pairs())
+
+
+def from_group(x):
+    return lax.ppermute(x, ("x", "yh", "z"), [(b, a) for a, b in audio_pairs()])
 
 
 def on_device(video_q, video_k, video_v, audio_q, audio_k, audio_v, align):
-    aud = swap_group(jnp.concatenate([audio_q, audio_k, audio_v], axis=1))
+    aud = to_group(jnp.concatenate([audio_q, audio_k, audio_v], axis=1))
     got = lax.all_to_all(
         pack(align, video_q, video_k, video_v), "z", split_axis=0, concat_axis=0, tiled=True
     )
     q_own, kv_own = join(got, aud)
     y = ("yh", "yl")
     core = functools.partial(shift, axis="c", n=NC, k=1)
-    far, near = shift(kv_own, y, NY, 2), core(kv_own)
-    qs = [shift(q_own, "x", NX, k) for k in (2, 1, 3)]
     right, left = [shift(kv_own, y, NY, k) for k in (1, 3)]
-    qs = qs + [q_own]
-    first = [kv_own, far, near, core(far)]
-    state = early(qs, first)
-    kvs = first + [right, left, core(right), core(left)]
-    parts = [late(q, state[2 * i : 2 * i + 2], kvs) for i, q in enumerate(qs)]
+    q_right, q_left = [shift(q_own, "x", NX, k) for k in (1, 3)]
+    got = lax.optimization_barrier([left, right, q_left, q_right, q_own, kv_own])
+    left, right, q_left, q_right, q_own, kv_own = got
+    far = [shift(right[0:VID], y, NY, 1), shift(left[VID:], y, NY, 3)]
+    q_far = shift(q_right, "x", NX, 1)
+    kvs = [kv_own, right, left] + [core(b) for b in (kv_own, right, left)]
+    state = early([q_right, q_left, q_own], kvs)
+    q_far, state = lax.optimization_barrier((q_far, state))
+    state_far = early([q_far], kvs)
+    far, state_far = lax.optimization_barrier((far, state_far))
+    kvs = kvs + far + [core(b) for b in far]
+    states = [state_far, state[0:2], state[2:4], state[4:6]]
+    parts = [late(q, st, kvs) for q, st in zip([q_far, q_right, q_left, q_own], states)]
     back = [shift(p, "x", NX, -k) for p, k in zip(parts, (2, 1, 3))]
     video, audio = combine(parts[3:] + back)
     video = lax.all_to_all(video, "z", split_axis=0, concat_axis=0, tiled=True)
-    return video.transpose(1, 0, 2).reshape(TOK, NZ * GW), swap_group(audio)
+    return video.transpose(1, 0, 2).reshape(TOK, NZ * GW), from_group(audio)
 
 
 def solution(mesh):

time: 101 us -> 96 us (0.950)
  the two profiles are of different devices: /device:TPU:152 before, /device:TPU:24 now
where the time goes in v3:
time: 96 us; the launch traced here: 94.9 us
  waiting for transfers between devices  39.6 us (41%)
  starting transfers between devices  37.7 us (39%)
  Pallas kernels  15.6 us (16%)
  local copies, waits for them, and re-layouts  1.35 us (1%)
    ppermute x15, waiting for transfers between devices, shift(): return lax.ppermute(x, axis, [(i, (i + k) % n) for i in range(n)])  17.7 us
    ppermute x1, waiting for transfers between devices, to_group(): return lax.ppermute(x, ('x', 'yh', 'z'), audio_pairs())  16.3 us
    ppermute x15, starting transfers between devices, shift(): return lax.ppermute(x, axis, [(i, (i + k) % n) for i in range(n)])  14.1 us
    all_to_all x1, starting transfers between devices, on_device(): lax.all_to_all(pack(align, video_q, video_k, video_v), 'z', split_axis=0,...  8.6 us
    pallas_call x2, Pallas kernels, early(): pl.pallas_call(early_body, out_shape=tuple((jax.ShapeDtypeStruct((rows, G...  6.8 us
    all_to_all x1, starting transfers between devices, on_device(): video = lax.all_to_all(video, 'z', split_axis=0, concat_axis=0, tiled=True)  5.86 us
    pallas_call x4, Pallas kernels, late(): pl.pallas_call(late_body, out_shape=jax.ShapeDtypeStruct((QROWS, GW), BF1...  5.18 us
    ppermute x1, starting transfers between devices, to_group(): return lax.ppermute(x, ('x', 'yh', 'z'), audio_pairs())  4.96 us
  transfers between devices with their start and end apart: 19, of which 13 were waited for; matrix products, arithmetic and copies ran while one was open for 0% of the time, Pallas kernels for 11%

profile of v3, /device:TPU:24, one launch (start us, length us, event | category | flops | bytes accessed | tf_op | source)
XLA Modules:
  0.0 94.9 jit_solution(4783740922958824771)
XLA Ops:
  0.6 2.1 %pack.1 = bf16[8,112,384]{2,1,0:T(8,128)(2,1)} custom-call(s32[32]{0:T(128)} %align_ref.1, bf16[32,3072]{1,0:T(8,128)(2,1)} %q_ref.1, bf16[32,3072]{1,0:T(8,128)(2,1)} %k_ref.1, bf16[32,3072]{1,0:T(8,128)(2,1)} %v_ref.1), custom_call_target="tpu_custom_call" | custom-call | tf_op jit(solution)/shard_map/pack/pallas_call | solution.py:52
  2.7 8.6 %all-to-all-start = ((bf16[8,112,384]{2,1,0:T(8,128)(2,1)}), bf16[8,112,384]{2,1,0:T(8,128)(2,1)S(1)}, u32[]{:S(2)}, u32[]{:S(2)}) async-start(bf16[8,112,384]{2,1,0:T(8,128)(2,1)} %pack.1), calls=%async_computation | async-start | bytes 1376256 | tf_op jit(solution)/shard_map/all_to_all | solution.py:341
  11.3 5.0 %collective-permute-start = (bf16[16,1152]{1,0:T(8,128)(2,1)S(1)}, bf16[16,1152]{1,0:T(8,128)(2,1)S(1)}, u32[]{:S(2)}, u32[]{:S(2)}) collective-permute-start(bf16[16,1152]{1,0:T(8,128)(2,1)S(1)} %pad_maximum_fusion), channel_id=1, source_target_pairs={{0,160},{2,96},{4,128},{6,64},{8,0},{10,192},{12,32},{14,224},{34,... | collective-permute-start | bytes 110600 | tf_op jit(solution)/shard_map/ppermute | solution.py:332
  16.3 16.3 %collective-permute-done.aud_ref = bf16[16,1152]{1,0:T(8,128)(2,1)S(1)} collective-permute-done((bf16[16,1152]{1,0:T(8,128)(2,1)S(1)}, bf16[16,1152]{1,0:T(8,128)(2,1)S(1)}, u32[]{:S(2)}, u32[]{:S(2)}) %collective-permute-start) | collective-permute-done | bytes 36896 | tf_op jit(solution)/shard_map/ppermute | solution.py:332
  35.1 2.9 %collective-permute-start.3 = (bf16[288,384]{1,0:T(8,128)(2,1)S(1)}, bf16[288,384]{1,0:T(8,128)(2,1)S(1)}, u32[]{:S(2)}, u32[]{:S(2)}) collective-permute-start(bf16[288,384]{1,0:T(8,128)(2,1)S(1)} %get-tuple-element.33.refs_2_.q_ref), channel_id=1, source_target_pairs={{0,192},{64,0},{128,64},{192,128},{1,193},{65,1},{129,65},{193,129... | collective-permute-start | bytes 663560 | tf_op jit(solution)/shard_map/ppermute | solution.py:306
  38.0 4.5 %collective-permute-done.4.refs_0_.q_ref = bf16[288,384]{1,0:T(8,128)(2,1)S(1)} collective-permute-done((bf16[288,384]{1,0:T(8,128)(2,1)S(1)}, bf16[288,384]{1,0:T(8,128)(2,1)S(1)}, u32[]{:S(2)}, u32[]{:S(2)}) %collective-permute-start.4) | collective-permute-done | bytes 221216 | tf_op jit(solution)/shard_map/ppermute | solution.py:306
  44.3 1.9 %collective-permute-done.1.refs_5_.refs_3_.refs_2_ = bf16[560,384]{1,0:T(8,128)(2,1)S(1)} collective-permute-done((bf16[560,384]{1,0:T(8,128)(2,1)S(1)}, bf16[560,384]{1,0:T(8,128)(2,1)S(1)}, u32[]{:S(2)}, u32[]{:S(2)}) %collective-permute-start.1) | collective-permute-done | bytes 430112 | tf_op jit(solution)/shard_map/ppermute | solution.py:306
  48.0 1.6 %collective-permute-start.10 = (bf16[304,384]{1,0:T(8,128)(2,1)S(1)}, bf16[304,384]{1,0:T(8,128)(2,1)S(1)}, u32[]{:S(2)}, u32[]{:S(2)}) collective-permute-start(bf16[304,384]{1,0:T(8,128)(2,1)S(1)} %slice.7), channel_id=1, source_target_pairs={{0,48},{16,0},{32,16},{48,32},{1,49},{17,1},{33,17},{49,33},{2,50}... | collective-permute-start | bytes 700424 | tf_op jit(solution)/shard_map/ppermute | solution.py:306
  49.6 4.9 %early.2 = (f32[272,384]{1,0:T(8,128)S(1)}, f32[272,384]{1,0:T(8,128)S(1)}, f32[272,384]{1,0:T(8,128)S(1)}, f32[272,384]{1,0:T(8,128)S(1)}, f32[272,384]{1,0:T(8,128)S(1)}, /*index=5*/f32[272,384]{1,0:T(8,128)S(1)}) custom-call(bf16[288,384]{1,0:T(8,128)(2,1)S(1)} %collective-permute-done.4.refs_0_.q_ref, ...), custom_call_target="tpu_custom_call" | custom-call | flops 2887778304 | bytes 4194304 | tf_op jit(solution)/shard_map/early/pallas_call | solution.py:185
  54.6 1.7 %collective-permute-done.5.refs_0_.q_ref = bf16[288,384]{1,0:T(8,128)(2,1)S(1)} collective-permute-done((bf16[288,384]{1,0:T(8,128)(2,1)S(1)}, bf16[288,384]{1,0:T(8,128)(2,1)S(1)}, u32[]{:S(2)}, u32[]{:S(2)}) %collective-permute-start.5) | collective-permute-done | bytes 221216 | tf_op jit(solution)/shard_map/ppermute | solution.py:306
  56.2 1.9 %early.3 = (f32[272,384]{1,0:T(8,128)S(1)}, f32[272,384]{1,0:T(8,128)S(1)}) custom-call(bf16[288,384]{1,0:T(8,128)(2,1)S(1)} %collective-permute-done.5.refs_0_.q_ref, bf16[560,384]{1,0:T(8,128)(2,1)S(1)} %get-tuple-element.36.refs_3_.refs_1_.refs_0_, bf16[560,384]{1,0:T(8,128)(2,1)S(1)} %collective-permute-done.2.refs_4_.refs_2_.refs_1_, ...), custom_call_target="tpu_custom_call" | custom-call | flops 962592768 | bytes 4194304 | tf_op jit(solution)/shard_map/early/pallas_call | solution.py:185
  60.0 1.3 %late.5 = bf16[288,384]{1,0:T(8,128)(2,1)S(1)} custom-call(bf16[288,384]{1,0:T(8,128)(2,1)S(1)} %collective-permute-done.5.refs_0_.q_ref, f32[272,384]{1,0:T(8,128)S(1)} %get-tuple-element.52.o_ref, f32[272,384]{1,0:T(8,128)S(1)} %get-tuple-element.53.l_ref, bf16[560,384]{1,0:T(8,128)(2,1)S(1)} %get-tuple-element.36.refs_3_.refs_1_.refs_0_, ...), custom_call_target="tpu_custom_call" | custom-call | flops 401080320 | bytes 5242880 | tf_op jit(solution)/shard_map/late/pallas_call | solution.py:257
  61.3 2.5 %collective-permute-start.13 = (bf16[288,384]{1,0:T(8,128)(2,1)S(1)}, bf16[288,384]{1,0:T(8,128)(2,1)S(1)}, u32[]{:S(2)}, u32[]{:S(2)}) collective-permute-start(bf16[288,384]{1,0:T(8,128)(2,1)S(1)} %late.5), channel_id=1, source_target_pairs={{0,128},{64,192},{128,0},{192,64},{1,129},{65,193},{129,1},{193,65... | collective-permute-start | bytes 663560 | tf_op jit(solution)/shard_map/ppermute | solution.py:306
  63.8 1.3 %late.6 = bf16[288,384]{1,0:T(8,128)(2,1)S(1)} custom-call(bf16[288,384]{1,0:T(8,128)(2,1)S(1)} %collective-permute-done.4.refs_0_.q_ref, f32[272,384]{1,0:T(8,128)S(1)} %get-tuple-element.54.o_ref, f32[272,384]{1,0:T(8,128)S(1)} %get-tuple-element.55.l_ref, bf16[560,384]{1,0:T(8,128)(2,1)S(1)} %get-tuple-element.36.refs_3_.refs_1_.refs_0_, ...), custom_call_target="tpu_custom_call" | custom-call | flops 401080320 | bytes 5242880 | tf_op jit(solution)/shard_map/late/pallas_call | solution.py:257
  65.1 1.9 %collective-permute-start.14 = (bf16[288,384]{1,0:T(8,128)(2,1)S(1)}, bf16[288,384]{1,0:T(8,128)(2,1)S(1)}, u32[]{:S(2)}, u32[]{:S(2)}) collective-permute-start(bf16[288,384]{1,0:T(8,128)(2,1)S(1)} %late.6), channel_id=1, source_target_pairs={{0,192},{64,0},{128,64},{192,128},{1,193},{65,1},{129,65},{193,129... | collective-permute-start | bytes 663560 | tf_op jit(solution)/shard_map/ppermute | solution.py:306
  67.0 1.3 %late.7 = bf16[288,384]{1,0:T(8,128)(2,1)S(1)} custom-call(bf16[288,384]{1,0:T(8,128)(2,1)S(1)} %collective-permute-done.3.refs_1_.q_ref, f32[272,384]{1,0:T(8,128)S(1)} %get-tuple-element.56.o_ref, f32[272,384]{1,0:T(8,128)S(1)} %get-tuple-element.57.l_ref, bf16[560,384]{1,0:T(8,128)(2,1)S(1)} %get-tuple-element.36.refs_3_.refs_1_.refs_0_, ...), custom_call_target="tpu_custom_call" | custom-call | flops 401080320 | bytes 5242880 | tf_op jit(solution)/shard_map/late/pallas_call | solution.py:257
  68.8 1.3 %late.4.a_ref = bf16[288,384]{1,0:T(8,128)(2,1)S(1)} custom-call(bf16[288,384]{1,0:T(8,128)(2,1)S(1)} %get-tuple-element.33.refs_2_.q_ref, f32[272,384]{1,0:T(8,128)S(1)} %get-tuple-element.45.o_ref, f32[272,384]{1,0:T(8,128)S(1)} %get-tuple-element.46.l_ref, bf16[560,384]{1,0:T(8,128)(2,1)S(1)} %get-tuple-element.36.refs_3_.refs_1_.refs_0_, ...), custom_call_target="tpu_custom_call" | custom-call | flops 401080320 | bytes 5242880 | tf_op jit(solution)/shard_map/late/pallas_call | solution.py:257
  70.4 4.0 %collective-permute-done.14.c_ref = bf16[288,384]{1,0:T(8,128)(2,1)S(1)} collective-permute-done((bf16[288,384]{1,0:T(8,128)(2,1)S(1)}, bf16[288,384]{1,0:T(8,128)(2,1)S(1)}, u32[]{:S(2)}, u32[]{:S(2)}) %collective-permute-start.14) | collective-permute-done | bytes 221216 | tf_op jit(solution)/shard_map/ppermute | solution.py:306
  74.4 2.2 %collective-permute-done.15.d_ref = bf16[288,384]{1,0:T(8,128)(2,1)S(1)} collective-permute-done((bf16[288,384]{1,0:T(8,128)(2,1)S(1)}, bf16[288,384]{1,0:T(8,128)(2,1)S(1)}, u32[]{:S(2)}, u32[]{:S(2)}) %collective-permute-start.15) | collective-permute-done | bytes 221216 | tf_op jit(solution)/shard_map/ppermute | solution.py:306
  76.5 1.4 %combine.1 = (bf16[8,32,384]{2,1,0:T(8,128)(2,1)}, bf16[16,384]{1,0:T(8,128)(2,1)S(1)}) custom-call(bf16[288,384]{1,0:T(8,128)(2,1)S(1)} %late.4.a_ref, bf16[288,384]{1,0:T(8,128)(2,1)S(1)} %collective-permute-done.13.b_ref, bf16[288,384]{1,0:T(8,128)(2,1)S(1)} %collective-permute-done.14.c_ref, bf16[288,384]{1,0:T(8,128)(2,1)S(1)} %collective-permute-done.15.d_ref), custom_call_target="tpu_custom_call" | custom-call | tf_op jit(solution)/shard_map/combine/pallas_call | solution.py:292
  78.0 5.9 %all-to-all-start.1 = ((bf16[8,32,384]{2,1,0:T(8,128)(2,1)}), bf16[8,32,384]{2,1,0:T(8,128)(2,1)S(1)}, u32[]{:S(2)}, u32[]{:S(2)}) async-start(bf16[8,32,384]{2,1,0:T(8,128)(2,1)} %get-tuple-element.58), calls=%async_computation.1 | async-start | bytes 393216 | tf_op jit(solution)/shard_map/all_to_all | solution.py:363
  83.9 4.2 %collective-permute-start.16 = (bf16[16,384]{1,0:T(8,128)(2,1)S(1)}, bf16[16,384]{1,0:T(8,128)(2,1)S(1)}, u32[]{:S(2)}, u32[]{:S(2)}) collective-permute-start(bf16[16,384]{1,0:T(8,128)(2,1)S(1)} %get-tuple-element.59), channel_id=1, source_target_pairs={{160,0},{96,2},{128,4},{64,6},{0,8},{192,10},{32,12},{224,14},{130... | collective-permute-start | bytes 36872 | tf_op jit(solution)/shard_map/ppermute | solution.py:336
  88.0 4.0 %collective-permute-done.16 = bf16[16,384]{1,0:T(8,128)(2,1)S(1)} collective-permute-done((bf16[16,384]{1,0:T(8,128)(2,1)S(1)}, bf16[16,384]{1,0:T(8,128)(2,1)S(1)}, u32[]{:S(2)}, u32[]{:S(2)}) %collective-permute-start.16) | collective-permute-done | bytes 12320 | tf_op jit(solution)/shard_map/ppermute | solution.py:336
  92.1 1.6 %all-to-all-done.1 = bf16[8,32,384]{2,1,0:T(8,128)(2,1)S(1)} async-done(((bf16[8,32,384]{2,1,0:T(8,128)(2,1)}), bf16[8,32,384]{2,1,0:T(8,128)(2,1)S(1)}, u32[]{:S(2)}, u32[]{:S(2)}) %all-to-all-start.1) | async-done | bytes 196640 | tf_op jit(solution)/shard_map/all_to_all | solution.py:363
  (34 shorter events, 10.0 us)
Async XLA Ops:
  2.7 8.6 %copy-start = (bf16[16,384]{1,0:T(8,128)(2,1)S(1)}, bf16[16,384]{1,0:T(8,128)(2,1)}, u32[]{:S(2)}) copy-start(bf16[16,384]{1,0:T(8,128)(2,1)} %param.12) | copy-start | bytes 36868
  2.7 8.6 %copy-start.1 = (bf16[16,384]{1,0:T(8,128)(2,1)S(1)}, bf16[16,384]{1,0:T(8,128)(2,1)}, u32[]{:S(2)}) copy-start(bf16[16,384]{1,0:T(8,128)(2,1)} %param.11) | copy-start | bytes 36868
  2.7 8.6 %copy-start.2 = (bf16[16,384]{1,0:T(8,128)(2,1)S(1)}, bf16[16,384]{1,0:T(8,128)(2,1)}, u32[]{:S(2)}) copy-start(bf16[16,384]{1,0:T(8,128)(2,1)} %param.10) | copy-start | bytes 36868
  2.7 29.9 %all-to-all-start = ((bf16[8,112,384]{2,1,0:T(8,128)(2,1)}), bf16[8,112,384]{2,1,0:T(8,128)(2,1)S(1)}, u32[]{:S(2)}, u32[]{:S(2)}) async-start(bf16[8,112,384]{2,1,0:T(8,128)(2,1)} %pack.1), calls=%async_computation | async-start | bytes 1376256 | tf_op jit(solution)/shard_map/all_to_all | solution.py:341
  11.3 21.2 %collective-permute-start = (bf16[16,1152]{1,0:T(8,128)(2,1)S(1)}, bf16[16,1152]{1,0:T(8,128)(2,1)S(1)}, u32[]{:S(2)}, u32[]{:S(2)}) collective-permute-start(bf16[16,1152]{1,0:T(8,128)(2,1)S(1)} %pad_maximum_fusion), channel_id=1, source_target_pairs={{0,160},{2,96},{4,128},{6,64},{8,0},{10,192},{12,32},{14,224},{34,... | collective-permute-start | bytes 110600 | tf_op jit(solution)/shard_map/ppermute | solution.py:332
  32.7 11.6 %collective-permute-start.2 = (bf16[560,384]{1,0:T(8,128)(2,1)S(1)}, bf16[560,384]{1,0:T(8,128)(2,1)S(1)}, u32[]{:S(2)}, u32[]{:S(2)}) collective-permute-start(bf16[560,384]{1,0:T(8,128)(2,1)S(1)} %get-tuple-element.36.refs_3_.refs_1_.refs_0_), channel_id=1, source_target_pairs={{0,16},{16,32},{32,48},{48,0},{1,17},{17,33},{33,49},{49,1},{2,18}... | collective-permute-start | bytes 1290248 | tf_op jit(solution)/shard_map/ppermute | solution.py:306
  33.5 12.8 %collective-permute-start.1 = (bf16[560,384]{1,0:T(8,128)(2,1)S(1)}, bf16[560,384]{1,0:T(8,128)(2,1)S(1)}, u32[]{:S(2)}, u32[]{:S(2)}) collective-permute-start(bf16[560,384]{1,0:T(8,128)(2,1)S(1)} %get-tuple-element.36.refs_3_.refs_1_.refs_0_), channel_id=1, source_target_pairs={{0,48},{16,0},{32,16},{48,32},{1,49},{17,1},{33,17},{49,33},{2,50}... | collective-permute-start | bytes 1290248 | tf_op jit(solution)/shard_map/ppermute | solution.py:306
  34.8 7.7 %collective-permute-start.4 = (bf16[288,384]{1,0:T(8,128)(2,1)S(1)}, bf16[288,384]{1,0:T(8,128)(2,1)S(1)}, u32[]{:S(2)}, u32[]{:S(2)}) collective-permute-start(bf16[288,384]{1,0:T(8,128)(2,1)S(1)} %get-tuple-element.33.refs_2_.q_ref), channel_id=1, source_target_pairs={{0,64},{64,128},{128,192},{192,0},{1,65},{65,129},{129,193},{193,1... | collective-permute-start | bytes 663560 | tf_op jit(solution)/shard_map/ppermute | solution.py:306
  35.1 8.3 %collective-permute-start.3 = (bf16[288,384]{1,0:T(8,128)(2,1)S(1)}, bf16[288,384]{1,0:T(8,128)(2,1)S(1)}, u32[]{:S(2)}, u32[]{:S(2)}) collective-permute-start(bf16[288,384]{1,0:T(8,128)(2,1)S(1)} %get-tuple-element.33.refs_2_.q_ref), channel_id=1, source_target_pairs={{0,192},{64,0},{128,64},{192,128},{1,193},{65,1},{129,65},{193,129... | collective-permute-start | bytes 663560 | tf_op jit(solution)/shard_map/ppermute | solution.py:306
  46.2 1.8 %collective-permute-start.6 = (bf16[560,384]{1,0:T(8,128)(2,1)S(1)}, bf16[560,384]{1,0:T(8,128)(2,1)S(1)}, u32[]{:S(2)}, u32[]{:S(2)}) collective-permute-start(bf16[560,384]{1,0:T(8,128)(2,1)S(1)} %get-tuple-element.36.refs_3_.refs_1_.refs_0_), channel_id=1, source_target_pairs={{0,1},{1,0},{2,3},{3,2},{4,5},{5,4},{6,7},{7,6},{8,9},{9,8},{10,11... | collective-permute-start | bytes 1290248 | tf_op jit(solution)/shard_map/ppermute | solution.py:306
  46.2 3.4 %collective-permute-start.7 = (bf16[560,384]{1,0:T(8,128)(2,1)S(1)}, bf16[560,384]{1,0:T(8,128)(2,1)S(1)}, u32[]{:S(2)}, u32[]{:S(2)}) collective-permute-start(bf16[560,384]{1,0:T(8,128)(2,1)S(1)} %collective-permute-done.2.refs_4_.refs_2_.refs_1_), channel_id=1, source_target_pairs={{0,1},{1,0},{2,3},{3,2},{4,5},{5,4},{6,7},{7,6},{8,9},{9,8},{10,11... | collective-permute-start | bytes 1290248 | tf_op jit(solution)/shard_map/ppermute | solution.py:306
  46.7 2.9 %collective-permute-start.8 = (bf16[560,384]{1,0:T(8,128)(2,1)S(1)}, bf16[560,384]{1,0:T(8,128)(2,1)S(1)}, u32[]{:S(2)}, u32[]{:S(2)}) collective-permute-start(bf16[560,384]{1,0:T(8,128)(2,1)S(1)} %collective-permute-done.1.refs_5_.refs_3_.refs_2_), channel_id=1, source_target_pairs={{0,1},{1,0},{2,3},{3,2},{4,5},{5,4},{6,7},{7,6},{8,9},{9,8},{10,11... | collective-permute-start | bytes 1290248 | tf_op jit(solution)/shard_map/ppermute | solution.py:306
  46.8 11.3 %collective-permute-start.9 = (bf16[256,384]{1,0:T(8,128)(2,1)S(1)}, bf16[256,384]{1,0:T(8,128)(2,1)S(1)}, u32[]{:S(2)}, u32[]{:S(2)}) collective-permute-start(bf16[256,384]{1,0:T(8,128)(2,1)S(1)} %slice.6), channel_id=1, source_target_pairs={{0,16},{16,32},{32,48},{48,0},{1,17},{17,33},{33,49},{49,1},{2,18}... | collective-permute-start | bytes 589832 | tf_op jit(solution)/shard_map/ppermute | solution.py:306
  47.3 9.0 %collective-permute-start.5 = (bf16[288,384]{1,0:T(8,128)(2,1)S(1)}, bf16[288,384]{1,0:T(8,128)(2,1)S(1)}, u32[]{:S(2)}, u32[]{:S(2)}) collective-permute-start(bf16[288,384]{1,0:T(8,128)(2,1)S(1)} %collective-permute-done.4.refs_0_.q_ref), channel_id=1, source_target_pairs={{0,64},{64,128},{128,192},{192,0},{1,65},{65,129},{129,193},{193,1... | collective-permute-start | bytes 663560 | tf_op jit(solution)/shard_map/ppermute | solution.py:306
  48.0 10.1 %collective-permute-start.10 = (bf16[304,384]{1,0:T(8,128)(2,1)S(1)}, bf16[304,384]{1,0:T(8,128)(2,1)S(1)}, u32[]{:S(2)}, u32[]{:S(2)}) collective-permute-start(bf16[304,384]{1,0:T(8,128)(2,1)S(1)} %slice.7), channel_id=1, source_target_pairs={{0,48},{16,0},{32,16},{48,32},{1,49},{17,1},{33,17},{49,33},{2,50}... | collective-permute-start | bytes 700424 | tf_op jit(solution)/shard_map/ppermute | solution.py:306
  58.1 1.9 %collective-permute-start.12 = (bf16[304,384]{1,0:T(8,128)(2,1)S(1)}, bf16[304,384]{1,0:T(8,128)(2,1)S(1)}, u32[]{:S(2)}, u32[]{:S(2)}) collective-permute-start(bf16[304,384]{1,0:T(8,128)(2,1)S(1)} %collective-permute-done.10.refs_7_), channel_id=1, source_target_pairs={{0,1},{1,0},{2,3},{3,2},{4,5},{5,4},{6,7},{7,6},{8,9},{9,8},{10,11... | collective-permute-start | bytes 700424 | tf_op jit(solution)/shard_map/ppermute | solution.py:306
  58.2 1.8 %collective-permute-start.11 = (bf16[256,384]{1,0:T(8,128)(2,1)S(1)}, bf16[256,384]{1,0:T(8,128)(2,1)S(1)}, u32[]{:S(2)}, u32[]{:S(2)}) collective-permute-start(bf16[256,384]{1,0:T(8,128)(2,1)S(1)} %collective-permute-done.9.refs_6_), channel_id=1, source_target_pairs={{0,1},{1,0},{2,3},{3,2},{4,5},{5,4},{6,7},{7,6},{8,9},{9,8},{10,11... | collective-permute-start | bytes 589832 | tf_op jit(solution)/shard_map/ppermute | solution.py:306
  61.3 9.1 %collective-permute-start.13 = (bf16[288,384]{1,0:T(8,128)(2,1)S(1)}, bf16[288,384]{1,0:T(8,128)(2,1)S(1)}, u32[]{:S(2)}, u32[]{:S(2)}) collective-permute-start(bf16[288,384]{1,0:T(8,128)(2,1)S(1)} %late.5), channel_id=1, source_target_pairs={{0,128},{64,192},{128,0},{192,64},{1,129},{65,193},{129,1},{193,65... | collective-permute-start | bytes 663560 | tf_op jit(solution)/shard_map/ppermute | solution.py:306
  65.1 9.3 %collective-permute-start.14 = (bf16[288,384]{1,0:T(8,128)(2,1)S(1)}, bf16[288,384]{1,0:T(8,128)(2,1)S(1)}, u32[]{:S(2)}, u32[]{:S(2)}) collective-permute-start(bf16[288,384]{1,0:T(8,128)(2,1)S(1)} %late.6), channel_id=1, source_target_pairs={{0,192},{64,0},{128,64},{192,128},{1,193},{65,1},{129,65},{193,129... | collective-permute-start | bytes 663560 | tf_op jit(solution)/shard_map/ppermute | solution.py:306
  68.3 8.2 %collective-permute-start.15 = (bf16[288,384]{1,0:T(8,128)(2,1)S(1)}, bf16[288,384]{1,0:T(8,128)(2,1)S(1)}, u32[]{:S(2)}, u32[]{:S(2)}) collective-permute-start(bf16[288,384]{1,0:T(8,128)(2,1)S(1)} %late.7), channel_id=1, source_target_pairs={{0,64},{64,128},{128,192},{192,0},{1,65},{65,129},{129,193},{193,1... | collective-permute-start | bytes 663560 | tf_op jit(solution)/shard_map/ppermute | solution.py:306
  78.0 15.6 %all-to-all-start.1 = ((bf16[8,32,384]{2,1,0:T(8,128)(2,1)}), bf16[8,32,384]{2,1,0:T(8,128)(2,1)S(1)}, u32[]{:S(2)}, u32[]{:S(2)}) async-start(bf16[8,32,384]{2,1,0:T(8,128)(2,1)} %get-tuple-element.58), calls=%async_computation.1 | async-start | bytes 393216 | tf_op jit(solution)/shard_map/all_to_all | solution.py:363
  83.9 8.2 %collective-permute-start.16 = (bf16[16,384]{1,0:T(8,128)(2,1)S(1)}, bf16[16,384]{1,0:T(8,128)(2,1)S(1)}, u32[]{:S(2)}, u32[]{:S(2)}) collective-permute-start(bf16[16,384]{1,0:T(8,128)(2,1)S(1)} %get-tuple-element.59), channel_id=1, source_target_pairs={{160,0},{96,2},{128,4},{64,6},{0,8},{192,10},{32,12},{224,14},{130... | collective-permute-start | bytes 36872 | tf_op jit(solution)/shard_map/ppermute | solution.py:336

commit v4 on v3

--- a/solution.py
+++ b/solution.py
@@ -16,6 +16,7 @@
 TOK = 32
 AUD = 16
 VID = NZ * TOK
+STAMPS = 8
 AUX = 16
 QROWS = VID + AUD + AUX
 KROWS = 2 * VID + 2 * AUD + AUX
@@ -27,6 +28,7 @@
 F32, BF16 = jnp.float32, jnp.bfloat16
 VMEM = pl.BlockSpec(memory_space=pltpu.VMEM)
 SMEM = pl.BlockSpec(memory_space=pltpu.SMEM)
+ANY = pl.BlockSpec(memory_space=pl.ANY)
 SMALL = pltpu.CompilerParams(vmem_limit_bytes=6 * 2**20)
 
 
@@ -38,20 +40,20 @@
         row = jnp.where(lane == first + i, align_ref[i], row)
     high = (row >> 4).astype(F32)
     low = (row & 15).astype(F32)
-    which = lax.broadcasted_iota(jnp.int32, (AUX, GW), 0)
-    aux = jnp.where(which == 0, high, jnp.where(which == 1, low, 0.0)).astype(BF16)
+    which = lax.broadcasted_iota(jnp.int32, (STAMPS, GW), 0)
+    stamps = jnp.where(which == 0, high, jnp.where(which == 1, low, 0.0)).astype(BF16)
     for g in range(NZ):
         cols = slice(g * GW, (g + 1) * GW)
         out[g, 0:TOK, :] = q_ref[:, cols]
         out[g, TOK : 2 * TOK, :] = k_ref[:, cols]
         out[g, 2 * TOK : 3 * TOK, :] = v_ref[:, cols]
-        out[g, 3 * TOK :, :] = aux
+        out[g, 3 * TOK :, :] = stamps
 
 
 def pack(align, q, k, v):
     return pl.pallas_call(
         pack_body,
-        out_shape=jax.ShapeDtypeStruct((NZ, 3 * TOK + AUX, GW), BF16),
+        out_shape=jax.ShapeDtypeStruct((NZ, 3 * TOK + STAMPS, GW), BF16),
         in_specs=[SMEM, VMEM, VMEM, VMEM],
         out_specs=VMEM,
         name="pack",
@@ -59,8 +61,8 @@
 
 
 def audio_times(start):
-    lane = lax.broadcasted_iota(jnp.int32, (AUX, GW), 1) - VID
-    which = lax.broadcasted_iota(jnp.int32, (AUX, GW), 0)
+    lane = lax.broadcasted_iota(jnp.int32, (STAMPS, GW), 1) - VID
+    which = lax.broadcasted_iota(jnp.int32, (STAMPS, GW), 0)
     stamp = lane + start
     here = (lane >= 0) & (lane < AUD)
     part = jnp.where(which == 0, stamp >> 4, jnp.where(which == 1, stamp & 15, 0))
@@ -76,6 +78,7 @@
         kv_out[at : at + TOK, :] = got_ref[g, TOK : 2 * TOK, :]
         kv_out[VID + at : VID + at + TOK, :] = got_ref[g, 2 * TOK : 3 * TOK, :]
         total = total + got_ref[g, 3 * TOK :, :].astype(F32)
+    total = jnp.concatenate([total, jnp.zeros((AUX - STAMPS, GW), F32)], axis=0)
     q_out[VID : VID + AUD, :] = aud_ref[:, 0:GW]
     kv_out[2 * VID : 2 * VID + AUD, :] = aud_ref[:, GW : 2 * GW]
     kv_out[2 * VID + AUD : 2 * VID + 2 * AUD, :] = aud_ref[:, 2 * GW :]
@@ -302,6 +305,32 @@
     )(*parts)
 
 
+def spread_body(video_ref, audio_ref, video_out, audio_out, rows_ref, sems):
+    audio_copy = pltpu.make_async_copy(audio_ref, audio_out, sems.at[0])
+    audio_copy.start()
+    for g in range(NZ):
+        rows_ref[:, g * GW : (g + 1) * GW] = video_ref[g]
+    video_copy = pltpu.make_async_copy(rows_ref, video_out, sems.at[1])
+    video_copy.start()
+    audio_copy.wait()
+    video_copy.wait()
+
+
+def spread(video, audio):
+    return pl.pallas_call(
+        spread_body,
+        out_shape=(
+            jax.ShapeDtypeStruct((TOK, NZ * GW), BF16),
+            jax.ShapeDtypeStruct((AUD, GW), BF16),
+        ),
+        in_specs=[VMEM, VMEM],
+        out_specs=(ANY, ANY),
+        scratch_shapes=[pltpu.VMEM((TOK, NZ * GW), BF16), pltpu.SemaphoreType.DMA((2,))],
+        compiler_params=SMALL,
+        name="spread",
+    )(video, audio)
+
+
 def shift(x, axis, n, k):
     return lax.ppermute(x, axis, [(i, (i + k) % n) for i in range(n)])
 
@@ -352,16 +381,16 @@
     q_far = shift(q_right, "x", NX, 1)
     kvs = [kv_own, right, left] + [core(b) for b in (kv_own, right, left)]
     state = early([q_right, q_left, q_own], kvs)
-    q_far, state = lax.optimization_barrier((q_far, state))
+    far, q_far, state = lax.optimization_barrier((far, q_far, state))
+    others = [core(b) for b in far]
     state_far = early([q_far], kvs)
-    far, state_far = lax.optimization_barrier((far, state_far))
-    kvs = kvs + far + [core(b) for b in far]
-    states = [state_far, state[0:2], state[2:4], state[4:6]]
-    parts = [late(q, st, kvs) for q, st in zip([q_far, q_right, q_left, q_own], states)]
+    kvs = kvs + far + others
+    part_far, state = lax.optimization_barrier((late(q_far, state_far, kvs), state))
+    parts = [part_far] + [late(q, state[2 * i : 2 * i + 2], kvs) for i, q in enumerate([q_right, q_left, q_own])]
     back = [shift(p, "x", NX, -k) for p, k in zip(parts, (2, 1, 3))]
     video, audio = combine(parts[3:] + back)
     video = lax.all_to_all(video, "z", split_axis=0, concat_axis=0, tiled=True)
-    return video.transpose(1, 0, 2).reshape(TOK, NZ * GW), from_group(audio)
+    return spread(video, from_group(audio))
 
 
 def solution(mesh):

time: 96 us -> 94.2 us (0.981)
  waiting for transfers between devices: 39.6 us -> 38.2 us
  local copies, waits for them, and re-layouts: 1.35 us -> 0.06 us
    ppermute x15, starting transfers between devices: 14.1 us -> 15.3 us  [shift(): return lax.ppermute(x, axis, [(i, (i + k) % n) for i in range(n)])]
    ppermute x1, waiting for transfers between devices: 16.3 us -> 15.2 us  [to_group(): return lax.ppermute(x, ('x', 'yh', 'z'), audio_pairs())]
    pallas_call x1 -> x2, Pallas kernels: 2.06 us -> 2.76 us  [the longest x1 2.05 us: pack(): pl.pallas_call(pack_body, out_shape=jax.ShapeDtypeStruct((NZ, 3 * TOK + S...]
  transfers between devices with their start and end apart: 19 -> 19, of which waited for: 13 -> 12; matrix products, arithmetic and copies ran while one was open for 0% -> 0% of each run, Pallas kernels for 11% -> 11%
where the time goes in v4:
time: 94.2 us; the launch traced here: 93.9 us
  starting transfers between devices  38.4 us (41%)
  waiting for transfers between devices  38.2 us (41%)
  Pallas kernels  16.3 us (17%)
    ppermute x15, waiting for transfers between devices, shift(): return lax.ppermute(x, axis, [(i, (i + k) % n) for i in range(n)])  16.9 us
    ppermute x15, starting transfers between devices, shift(): return lax.ppermute(x, axis, [(i, (i + k) % n) for i in range(n)])  15.3 us
    ppermute x1, waiting for transfers between devices, to_group(): return lax.ppermute(x, ('x', 'yh', 'z'), audio_pairs())  15.2 us
    all_to_all x1, starting transfers between devices, on_device(): lax.all_to_all(pack(align, video_q, video_k, video_v), 'z', split_axis=0,...  8.6 us
    pallas_call x2, Pallas kernels, early(): pl.pallas_call(early_body, out_shape=tuple((jax.ShapeDtypeStruct((rows, G...  6.87 us
    all_to_all x1, starting transfers between devices, on_device(): video = lax.all_to_all(video, 'z', split_axis=0, concat_axis=0, tiled=True)  5.85 us
    pallas_call x4, Pallas kernels, late(): pl.pallas_call(late_body, out_shape=jax.ShapeDtypeStruct((QROWS, GW), BF1...  5.17 us
    ppermute x1, starting transfers between devices, to_group(): return lax.ppermute(x, ('x', 'yh', 'z'), audio_pairs())  4.96 us
  transfers between devices with their start and end apart: 19, of which 12 were waited for; matrix products, arithmetic and copies ran while one was open for 0% of the time, Pallas kernels for 11%

profile of v4, /device:TPU:24, one launch (start us, length us, event | category | flops | bytes accessed | tf_op | source)
XLA Modules:
  0.0 93.9 jit_solution(15805992517268026643)
XLA Ops:
  0.6 2.1 %pack.1 = bf16[8,104,384]{2,1,0:T(8,128)(2,1)} custom-call(s32[32]{0:T(128)} %align_ref.1, bf16[32,3072]{1,0:T(8,128)(2,1)} %q_ref.1, bf16[32,3072]{1,0:T(8,128)(2,1)} %k_ref.1, bf16[32,3072]{1,0:T(8,128)(2,1)} %v_ref.1), custom_call_target="tpu_custom_call" | custom-call | tf_op jit(solution)/shard_map/pack/pallas_call | solution.py:54
  2.7 8.6 %all-to-all-start = ((bf16[8,104,384]{2,1,0:T(8,128)(2,1)}), bf16[8,104,384]{2,1,0:T(8,128)(2,1)S(1)}, u32[]{:S(2)}, u32[]{:S(2)}) async-start(bf16[8,104,384]{2,1,0:T(8,128)(2,1)} %pack.1), calls=%async_computation | async-start | bytes 1277952 | tf_op jit(solution)/shard_map/all_to_all | solution.py:370
  11.3 5.0 %collective-permute-start = (bf16[16,1152]{1,0:T(8,128)(2,1)S(1)}, bf16[16,1152]{1,0:T(8,128)(2,1)S(1)}, u32[]{:S(2)}, u32[]{:S(2)}) collective-permute-start(bf16[16,1152]{1,0:T(8,128)(2,1)S(1)} %pad_maximum_fusion), channel_id=1, source_target_pairs={{0,160},{2,96},{4,128},{6,64},{8,0},{10,192},{12,32},{14,224},{34,... | collective-permute-start | bytes 110600 | tf_op jit(solution)/shard_map/ppermute | solution.py:361
  16.3 15.2 %collective-permute-done.aud_ref = bf16[16,1152]{1,0:T(8,128)(2,1)S(1)} collective-permute-done((bf16[16,1152]{1,0:T(8,128)(2,1)S(1)}, bf16[16,1152]{1,0:T(8,128)(2,1)S(1)}, u32[]{:S(2)}, u32[]{:S(2)}) %collective-permute-start) | collective-permute-done | bytes 36896 | tf_op jit(solution)/shard_map/ppermute | solution.py:361
  32.4 1.3 %collective-permute-start.1 = (bf16[560,384]{1,0:T(8,128)(2,1)S(1)}, bf16[560,384]{1,0:T(8,128)(2,1)S(1)}, u32[]{:S(2)}, u32[]{:S(2)}) collective-permute-start(bf16[560,384]{1,0:T(8,128)(2,1)S(1)} %get-tuple-element.43.refs_3_.refs_1_.refs_0_), channel_id=1, source_target_pairs={{0,48},{16,0},{32,16},{48,32},{1,49},{17,1},{33,17},{49,33},{2,50}... | collective-permute-start | bytes 1290248 | tf_op jit(solution)/shard_map/ppermute | solution.py:335
  34.0 2.9 %collective-permute-start.3 = (bf16[288,384]{1,0:T(8,128)(2,1)S(1)}, bf16[288,384]{1,0:T(8,128)(2,1)S(1)}, u32[]{:S(2)}, u32[]{:S(2)}) collective-permute-start(bf16[288,384]{1,0:T(8,128)(2,1)S(1)} %get-tuple-element.38.refs_2_.q_ref), channel_id=1, source_target_pairs={{0,192},{64,0},{128,64},{192,128},{1,193},{65,1},{129,65},{193,129... | collective-permute-start | bytes 663560 | tf_op jit(solution)/shard_map/ppermute | solution.py:335
  37.0 4.5 %collective-permute-done.4.refs_0_.q_ref = bf16[288,384]{1,0:T(8,128)(2,1)S(1)} collective-permute-done((bf16[288,384]{1,0:T(8,128)(2,1)S(1)}, bf16[288,384]{1,0:T(8,128)(2,1)S(1)}, u32[]{:S(2)}, u32[]{:S(2)}) %collective-permute-start.4) | collective-permute-done | bytes 221216 | tf_op jit(solution)/shard_map/ppermute | solution.py:335
  43.2 1.9 %collective-permute-done.1.refs_5_.refs_3_.refs_2_ = bf16[560,384]{1,0:T(8,128)(2,1)S(1)} collective-permute-done((bf16[560,384]{1,0:T(8,128)(2,1)S(1)}, bf16[560,384]{1,0:T(8,128)(2,1)S(1)}, u32[]{:S(2)}, u32[]{:S(2)}) %collective-permute-start.1) | collective-permute-done | bytes 430112 | tf_op jit(solution)/shard_map/ppermute | solution.py:335
  47.0 1.6 %collective-permute-start.6 = (bf16[304,384]{1,0:T(8,128)(2,1)S(1)}, bf16[304,384]{1,0:T(8,128)(2,1)S(1)}, u32[]{:S(2)}, u32[]{:S(2)}) collective-permute-start(bf16[304,384]{1,0:T(8,128)(2,1)S(1)} %slice.7), channel_id=1, source_target_pairs={{0,48},{16,0},{32,16},{48,32},{1,49},{17,1},{33,17},{49,33},{2,50}... | collective-permute-start | bytes 700424 | tf_op jit(solution)/shard_map/ppermute | solution.py:335
  48.6 5.0 %early.2 = (f32[272,384]{1,0:T(8,128)S(1)}, f32[272,384]{1,0:T(8,128)S(1)}, f32[272,384]{1,0:T(8,128)S(1)}, f32[272,384]{1,0:T(8,128)S(1)}, f32[272,384]{1,0:T(8,128)S(1)}, /*index=5*/f32[272,384]{1,0:T(8,128)S(1)}) custom-call(bf16[288,384]{1,0:T(8,128)(2,1)S(1)} %collective-permute-done.4.refs_0_.q_ref, ...), custom_call_target="tpu_custom_call" | custom-call | flops 2887778304 | bytes 4194304 | tf_op jit(solution)/shard_map/early/pallas_call | solution.py:188
  53.6 1.6 %collective-permute-done.7.refs_0_.q_ref = bf16[288,384]{1,0:T(8,128)(2,1)S(1)} collective-permute-done((bf16[288,384]{1,0:T(8,128)(2,1)S(1)}, bf16[288,384]{1,0:T(8,128)(2,1)S(1)}, u32[]{:S(2)}, u32[]{:S(2)}) %collective-permute-start.7) | collective-permute-done | bytes 221216 | tf_op jit(solution)/shard_map/ppermute | solution.py:335
  56.4 1.9 %early.3 = (f32[272,384]{1,0:T(8,128)S(1)}, f32[272,384]{1,0:T(8,128)S(1)}) custom-call(bf16[288,384]{1,0:T(8,128)(2,1)S(1)} %collective-permute-done.7.refs_0_.q_ref, bf16[560,384]{1,0:T(8,128)(2,1)S(1)} %get-tuple-element.43.refs_3_.refs_1_.refs_0_, bf16[560,384]{1,0:T(8,128)(2,1)S(1)} %collective-permute-done.2.refs_4_.refs_2_.refs_1_, ...), custom_call_target="tpu_custom_call" | custom-call | flops 962592768 | bytes 4194304 | tf_op jit(solution)/shard_map/early/pallas_call | solution.py:188
  59.6 3.8 %collective-permute-start.13 = (bf16[288,384]{1,0:T(8,128)(2,1)S(1)}, bf16[288,384]{1,0:T(8,128)(2,1)S(1)}, u32[]{:S(2)}, u32[]{:S(2)}) collective-permute-start(bf16[288,384]{1,0:T(8,128)(2,1)S(1)} %late.4), channel_id=1, source_target_pairs={{0,128},{64,192},{128,0},{192,64},{1,129},{65,193},{129,1},{193,65... | collective-permute-start | bytes 663560 | tf_op jit(solution)/shard_map/ppermute | solution.py:335
  63.4 1.3 %late.6 = bf16[288,384]{1,0:T(8,128)(2,1)S(1)} custom-call(bf16[288,384]{1,0:T(8,128)(2,1)S(1)} %collective-permute-done.4.refs_0_.q_ref, f32[272,384]{1,0:T(8,128)S(1)} %get-tuple-element.64.o_ref, f32[272,384]{1,0:T(8,128)S(1)} %get-tuple-element.65.l_ref, bf16[560,384]{1,0:T(8,128)(2,1)S(1)} %get-tuple-element.43.refs_3_.refs_1_.refs_0_, ...), custom_call_target="tpu_custom_call" | custom-call | flops 401080320 | bytes 5242880 | tf_op jit(solution)/shard_map/late/pallas_call | solution.py:260
  64.7 1.9 %collective-permute-start.14 = (bf16[288,384]{1,0:T(8,128)(2,1)S(1)}, bf16[288,384]{1,0:T(8,128)(2,1)S(1)}, u32[]{:S(2)}, u32[]{:S(2)}) collective-permute-start(bf16[288,384]{1,0:T(8,128)(2,1)S(1)} %late.6), channel_id=1, source_target_pairs={{0,192},{64,0},{128,64},{192,128},{1,193},{65,1},{129,65},{193,129... | collective-permute-start | bytes 663560 | tf_op jit(solution)/shard_map/ppermute | solution.py:335
  66.6 1.3 %late.7 = bf16[288,384]{1,0:T(8,128)(2,1)S(1)} custom-call(bf16[288,384]{1,0:T(8,128)(2,1)S(1)} %collective-permute-done.3.refs_1_.q_ref, f32[272,384]{1,0:T(8,128)S(1)} %get-tuple-element.66.o_ref, f32[272,384]{1,0:T(8,128)S(1)} %get-tuple-element.67.l_ref, bf16[560,384]{1,0:T(8,128)(2,1)S(1)} %get-tuple-element.43.refs_3_.refs_1_.refs_0_, ...), custom_call_target="tpu_custom_call" | custom-call | flops 401080320 | bytes 5242880 | tf_op jit(solution)/shard_map/late/pallas_call | solution.py:260
  68.4 1.3 %late.5.a_ref = bf16[288,384]{1,0:T(8,128)(2,1)S(1)} custom-call(bf16[288,384]{1,0:T(8,128)(2,1)S(1)} %get-tuple-element.38.refs_2_.q_ref, f32[272,384]{1,0:T(8,128)S(1)} %get-tuple-element.61.o_ref, f32[272,384]{1,0:T(8,128)S(1)} %get-tuple-element.62.l_ref, bf16[560,384]{1,0:T(8,128)(2,1)S(1)} %get-tuple-element.43.refs_3_.refs_1_.refs_0_, ...), custom_call_target="tpu_custom_call" | custom-call | flops 401080320 | bytes 5242880 | tf_op jit(solution)/shard_map/late/pallas_call | solution.py:260
  69.7 4.1 %collective-permute-done.14.c_ref = bf16[288,384]{1,0:T(8,128)(2,1)S(1)} collective-permute-done((bf16[288,384]{1,0:T(8,128)(2,1)S(1)}, bf16[288,384]{1,0:T(8,128)(2,1)S(1)}, u32[]{:S(2)}, u32[]{:S(2)}) %collective-permute-start.14) | collective-permute-done | bytes 221216 | tf_op jit(solution)/shard_map/ppermute | solution.py:335
  73.7 2.2 %collective-permute-done.15.d_ref = bf16[288,384]{1,0:T(8,128)(2,1)S(1)} collective-permute-done((bf16[288,384]{1,0:T(8,128)(2,1)S(1)}, bf16[288,384]{1,0:T(8,128)(2,1)S(1)}, u32[]{:S(2)}, u32[]{:S(2)}) %collective-permute-start.15) | collective-permute-done | bytes 221216 | tf_op jit(solution)/shard_map/ppermute | solution.py:335
  75.9 1.4 %combine.1 = (bf16[8,32,384]{2,1,0:T(8,128)(2,1)}, bf16[16,384]{1,0:T(8,128)(2,1)S(1)}) custom-call(bf16[288,384]{1,0:T(8,128)(2,1)S(1)} %late.5.a_ref, bf16[288,384]{1,0:T(8,128)(2,1)S(1)} %collective-permute-done.13.b_ref, bf16[288,384]{1,0:T(8,128)(2,1)S(1)} %collective-permute-done.14.c_ref, bf16[288,384]{1,0:T(8,128)(2,1)S(1)} %collective-permute-done.15.d_ref), custom_call_target="tpu_custom_call" | custom-call | tf_op jit(solution)/shard_map/combine/pallas_call | solution.py:295
  77.4 5.8 %all-to-all-start.1 = ((bf16[8,32,384]{2,1,0:T(8,128)(2,1)}), bf16[8,32,384]{2,1,0:T(8,128)(2,1)S(1)}, u32[]{:S(2)}, u32[]{:S(2)}) async-start(bf16[8,32,384]{2,1,0:T(8,128)(2,1)} %get-tuple-element.68), calls=%async_computation.1 | async-start | bytes 393216 | tf_op jit(solution)/shard_map/all_to_all | solution.py:392
  83.2 3.7 %collective-permute-start.16 = (bf16[16,384]{1,0:T(8,128)(2,1)S(1)}, bf16[16,384]{1,0:T(8,128)(2,1)S(1)}, u32[]{:S(2)}, u32[]{:S(2)}) collective-permute-start(bf16[16,384]{1,0:T(8,128)(2,1)S(1)} %get-tuple-element.69), channel_id=1, source_target_pairs={{160,0},{96,2},{128,4},{64,6},{0,8},{192,10},{32,12},{224,14},{130... | collective-permute-start | bytes 36872 | tf_op jit(solution)/shard_map/ppermute | solution.py:365
  86.9 4.5 %collective-permute-done.16.audio_ref = bf16[16,384]{1,0:T(8,128)(2,1)S(1)} collective-permute-done((bf16[16,384]{1,0:T(8,128)(2,1)S(1)}, bf16[16,384]{1,0:T(8,128)(2,1)S(1)}, u32[]{:S(2)}, u32[]{:S(2)}) %collective-permute-start.16) | collective-permute-done | bytes 12320 | tf_op jit(solution)/shard_map/ppermute | solution.py:365
  91.4 1.6 %all-to-all-done.1.video_ref = bf16[8,32,384]{2,1,0:T(8,128)(2,1)S(1)} async-done(((bf16[8,32,384]{2,1,0:T(8,128)(2,1)}), bf16[8,32,384]{2,1,0:T(8,128)(2,1)S(1)}, u32[]{:S(2)}, u32[]{:S(2)}) %all-to-all-start.1) | async-done | bytes 196640 | tf_op jit(solution)/shard_map/all_to_all | solution.py:392
  (33 shorter events, 8.5 us)
Async XLA Ops:
  2.7 8.6 %copy-start = (bf16[16,384]{1,0:T(8,128)(2,1)S(1)}, bf16[16,384]{1,0:T(8,128)(2,1)}, u32[]{:S(2)}) copy-start(bf16[16,384]{1,0:T(8,128)(2,1)} %param.12) | copy-start | bytes 36868
  2.7 8.6 %copy-start.1 = (bf16[16,384]{1,0:T(8,128)(2,1)S(1)}, bf16[16,384]{1,0:T(8,128)(2,1)}, u32[]{:S(2)}) copy-start(bf16[16,384]{1,0:T(8,128)(2,1)} %param.11) | copy-start | bytes 36868
  2.7 8.6 %copy-start.2 = (bf16[16,384]{1,0:T(8,128)(2,1)S(1)}, bf16[16,384]{1,0:T(8,128)(2,1)}, u32[]{:S(2)}) copy-start(bf16[16,384]{1,0:T(8,128)(2,1)} %param.10) | copy-start | bytes 36868
  2.7 28.8 %all-to-all-start = ((bf16[8,104,384]{2,1,0:T(8,128)(2,1)}), bf16[8,104,384]{2,1,0:T(8,128)(2,1)S(1)}, u32[]{:S(2)}, u32[]{:S(2)}) async-start(bf16[8,104,384]{2,1,0:T(8,128)(2,1)} %pack.1), calls=%async_computation | async-start | bytes 1277952 | tf_op jit(solution)/shard_map/all_to_all | solution.py:370
  11.3 20.2 %collective-permute-start = (bf16[16,1152]{1,0:T(8,128)(2,1)S(1)}, bf16[16,1152]{1,0:T(8,128)(2,1)S(1)}, u32[]{:S(2)}, u32[]{:S(2)}) collective-permute-start(bf16[16,1152]{1,0:T(8,128)(2,1)S(1)} %pad_maximum_fusion), channel_id=1, source_target_pairs={{0,160},{2,96},{4,128},{6,64},{8,0},{10,192},{12,32},{14,224},{34,... | collective-permute-start | bytes 110600 | tf_op jit(solution)/shard_map/ppermute | solution.py:361
  31.6 11.6 %collective-permute-start.2 = (bf16[560,384]{1,0:T(8,128)(2,1)S(1)}, bf16[560,384]{1,0:T(8,128)(2,1)S(1)}, u32[]{:S(2)}, u32[]{:S(2)}) collective-permute-start(bf16[560,384]{1,0:T(8,128)(2,1)S(1)} %get-tuple-element.43.refs_3_.refs_1_.refs_0_), channel_id=1, source_target_pairs={{0,16},{16,32},{32,48},{48,0},{1,17},{17,33},{33,49},{49,1},{2,18}... | collective-permute-start | bytes 1290248 | tf_op jit(solution)/shard_map/ppermute | solution.py:335
  32.4 12.8 %collective-permute-start.1 = (bf16[560,384]{1,0:T(8,128)(2,1)S(1)}, bf16[560,384]{1,0:T(8,128)(2,1)S(1)}, u32[]{:S(2)}, u32[]{:S(2)}) collective-permute-start(bf16[560,384]{1,0:T(8,128)(2,1)S(1)} %get-tuple-element.43.refs_3_.refs_1_.refs_0_), channel_id=1, source_target_pairs={{0,48},{16,0},{32,16},{48,32},{1,49},{17,1},{33,17},{49,33},{2,50}... | collective-permute-start | bytes 1290248 | tf_op jit(solution)/shard_map/ppermute | solution.py:335
  33.7 7.7 %collective-permute-start.4 = (bf16[288,384]{1,0:T(8,128)(2,1)S(1)}, bf16[288,384]{1,0:T(8,128)(2,1)S(1)}, u32[]{:S(2)}, u32[]{:S(2)}) collective-permute-start(bf16[288,384]{1,0:T(8,128)(2,1)S(1)} %get-tuple-element.38.refs_2_.q_ref), channel_id=1, source_target_pairs={{0,64},{64,128},{128,192},{192,0},{1,65},{65,129},{129,193},{193,1... | collective-permute-start | bytes 663560 | tf_op jit(solution)/shard_map/ppermute | solution.py:335
  34.0 8.3 %collective-permute-start.3 = (bf16[288,384]{1,0:T(8,128)(2,1)S(1)}, bf16[288,384]{1,0:T(8,128)(2,1)S(1)}, u32[]{:S(2)}, u32[]{:S(2)}) collective-permute-start(bf16[288,384]{1,0:T(8,128)(2,1)S(1)} %get-tuple-element.38.refs_2_.q_ref), channel_id=1, source_target_pairs={{0,192},{64,0},{128,64},{192,128},{1,193},{65,1},{129,65},{193,129... | collective-permute-start | bytes 663560 | tf_op jit(solution)/shard_map/ppermute | solution.py:335
  45.2 1.8 %collective-permute-start.8 = (bf16[560,384]{1,0:T(8,128)(2,1)S(1)}, bf16[560,384]{1,0:T(8,128)(2,1)S(1)}, u32[]{:S(2)}, u32[]{:S(2)}) collective-permute-start(bf16[560,384]{1,0:T(8,128)(2,1)S(1)} %get-tuple-element.43.refs_3_.refs_1_.refs_0_), channel_id=1, source_target_pairs={{0,1},{1,0},{2,3},{3,2},{4,5},{5,4},{6,7},{7,6},{8,9},{9,8},{10,11... | collective-permute-start | bytes 1290248 | tf_op jit(solution)/shard_map/ppermute | solution.py:335
  45.2 3.4 %collective-permute-start.9 = (bf16[560,384]{1,0:T(8,128)(2,1)S(1)}, bf16[560,384]{1,0:T(8,128)(2,1)S(1)}, u32[]{:S(2)}, u32[]{:S(2)}) collective-permute-start(bf16[560,384]{1,0:T(8,128)(2,1)S(1)} %collective-permute-done.2.refs_4_.refs_2_.refs_1_), channel_id=1, source_target_pairs={{0,1},{1,0},{2,3},{3,2},{4,5},{5,4},{6,7},{7,6},{8,9},{9,8},{10,11... | collective-permute-start | bytes 1290248 | tf_op jit(solution)/shard_map/ppermute | solution.py:335
  45.7 2.9 %collective-permute-start.10 = (bf16[560,384]{1,0:T(8,128)(2,1)S(1)}, bf16[560,384]{1,0:T(8,128)(2,1)S(1)}, u32[]{:S(2)}, u32[]{:S(2)}) collective-permute-start(bf16[560,384]{1,0:T(8,128)(2,1)S(1)} %collective-permute-done.1.refs_5_.refs_3_.refs_2_), channel_id=1, source_target_pairs={{0,1},{1,0},{2,3},{3,2},{4,5},{5,4},{6,7},{7,6},{8,9},{9,8},{10,11... | collective-permute-start | bytes 1290248 | tf_op jit(solution)/shard_map/ppermute | solution.py:335
  45.8 7.8 %collective-permute-start.5 = (bf16[256,384]{1,0:T(8,128)(2,1)S(1)}, bf16[256,384]{1,0:T(8,128)(2,1)S(1)}, u32[]{:S(2)}, u32[]{:S(2)}) collective-permute-start(bf16[256,384]{1,0:T(8,128)(2,1)S(1)} %slice.6), channel_id=1, source_target_pairs={{0,16},{16,32},{32,48},{48,0},{1,17},{17,33},{33,49},{49,1},{2,18}... | collective-permute-start | bytes 589832 | tf_op jit(solution)/shard_map/ppermute | solution.py:335
  46.2 9.0 %collective-permute-start.7 = (bf16[288,384]{1,0:T(8,128)(2,1)S(1)}, bf16[288,384]{1,0:T(8,128)(2,1)S(1)}, u32[]{:S(2)}, u32[]{:S(2)}) collective-permute-start(bf16[288,384]{1,0:T(8,128)(2,1)S(1)} %collective-permute-done.4.refs_0_.q_ref), channel_id=1, source_target_pairs={{0,64},{64,128},{128,192},{192,0},{1,65},{65,129},{129,193},{193,1... | collective-permute-start | bytes 663560 | tf_op jit(solution)/shard_map/ppermute | solution.py:335
  47.0 8.9 %collective-permute-start.6 = (bf16[304,384]{1,0:T(8,128)(2,1)S(1)}, bf16[304,384]{1,0:T(8,128)(2,1)S(1)}, u32[]{:S(2)}, u32[]{:S(2)}) collective-permute-start(bf16[304,384]{1,0:T(8,128)(2,1)S(1)} %slice.7), channel_id=1, source_target_pairs={{0,48},{16,0},{32,16},{48,32},{1,49},{17,1},{33,17},{49,33},{2,50}... | collective-permute-start | bytes 700424 | tf_op jit(solution)/shard_map/ppermute | solution.py:335
  55.9 2.4 %collective-permute-start.12 = (bf16[304,384]{1,0:T(8,128)(2,1)S(1)}, bf16[304,384]{1,0:T(8,128)(2,1)S(1)}, u32[]{:S(2)}, u32[]{:S(2)}) collective-permute-start(bf16[304,384]{1,0:T(8,128)(2,1)S(1)} %collective-permute-done.6.refs_7_), channel_id=1, source_target_pairs={{0,1},{1,0},{2,3},{3,2},{4,5},{5,4},{6,7},{7,6},{8,9},{9,8},{10,11... | collective-permute-start | bytes 700424 | tf_op jit(solution)/shard_map/ppermute | solution.py:335
  55.9 2.4 %collective-permute-start.11 = (bf16[256,384]{1,0:T(8,128)(2,1)S(1)}, bf16[256,384]{1,0:T(8,128)(2,1)S(1)}, u32[]{:S(2)}, u32[]{:S(2)}) collective-permute-start(bf16[256,384]{1,0:T(8,128)(2,1)S(1)} %collective-permute-done.5.refs_6_), channel_id=1, source_target_pairs={{0,1},{1,0},{2,3},{3,2},{4,5},{5,4},{6,7},{7,6},{8,9},{9,8},{10,11... | collective-permute-start | bytes 589832 | tf_op jit(solution)/shard_map/ppermute | solution.py:335
  59.6 10.1 %collective-permute-start.13 = (bf16[288,384]{1,0:T(8,128)(2,1)S(1)}, bf16[288,384]{1,0:T(8,128)(2,1)S(1)}, u32[]{:S(2)}, u32[]{:S(2)}) collective-permute-start(bf16[288,384]{1,0:T(8,128)(2,1)S(1)} %late.4), channel_id=1, source_target_pairs={{0,128},{64,192},{128,0},{192,64},{1,129},{65,193},{129,1},{193,65... | collective-permute-start | bytes 663560 | tf_op jit(solution)/shard_map/ppermute | solution.py:335
  64.7 9.1 %collective-permute-start.14 = (bf16[288,384]{1,0:T(8,128)(2,1)S(1)}, bf16[288,384]{1,0:T(8,128)(2,1)S(1)}, u32[]{:S(2)}, u32[]{:S(2)}) collective-permute-start(bf16[288,384]{1,0:T(8,128)(2,1)S(1)} %late.6), channel_id=1, source_target_pairs={{0,192},{64,0},{128,64},{192,128},{1,193},{65,1},{129,65},{193,129... | collective-permute-start | bytes 663560 | tf_op jit(solution)/shard_map/ppermute | solution.py:335
  67.9 8.1 %collective-permute-start.15 = (bf16[288,384]{1,0:T(8,128)(2,1)S(1)}, bf16[288,384]{1,0:T(8,128)(2,1)S(1)}, u32[]{:S(2)}, u32[]{:S(2)}) collective-permute-start(bf16[288,384]{1,0:T(8,128)(2,1)S(1)} %late.7), channel_id=1, source_target_pairs={{0,64},{64,128},{128,192},{192,0},{1,65},{65,129},{129,193},{193,1... | collective-permute-start | bytes 663560 | tf_op jit(solution)/shard_map/ppermute | solution.py:335
  77.4 15.6 %all-to-all-start.1 = ((bf16[8,32,384]{2,1,0:T(8,128)(2,1)}), bf16[8,32,384]{2,1,0:T(8,128)(2,1)S(1)}, u32[]{:S(2)}, u32[]{:S(2)}) async-start(bf16[8,32,384]{2,1,0:T(8,128)(2,1)} %get-tuple-element.68), calls=%async_computation.1 | async-start | bytes 393216 | tf_op jit(solution)/shard_map/all_to_all | solution.py:392
  83.2 8.2 %collective-permute-start.16 = (bf16[16,384]{1,0:T(8,128)(2,1)S(1)}, bf16[16,384]{1,0:T(8,128)(2,1)S(1)}, u32[]{:S(2)}, u32[]{:S(2)}) collective-permute-start(bf16[16,384]{1,0:T(8,128)(2,1)S(1)} %get-tuple-element.69), channel_id=1, source_target_pairs={{160,0},{96,2},{128,4},{64,6},{0,8},{192,10},{32,12},{224,14},{130... | collective-permute-start | bytes 36872 | tf_op jit(solution)/shard_map/ppermute | solution.py:365

commit v5 on v4

--- a/solution.py
+++ b/solution.py
@@ -276,15 +276,28 @@
 def combine_body(a_ref, b_ref, c_ref, d_ref, video_out, audio_out):
     refs = (a_ref, b_ref, c_ref, d_ref)
     rows = VID + AUD
-    which = lax.broadcasted_iota(jnp.int32, (AUX, HD), 0)
+    auxes = [ref[rows:, :].astype(F32) for ref in refs]
+    which = lax.broadcasted_iota(jnp.int32, (2 * AUX, GW), 0)
+    table = jnp.zeros((2 * AUX, GW), F32)
     for h in range(HPG):
-        pick = jnp.where((which >= 3 * h) & (which < 3 * h + 3), 1.0, 0.0).astype(BF16)
-        lses = [dot_tn(ref[rows:, :], pick)[0:rows] for ref in refs]
+        lses = [x[3 * h : 3 * h + 1] + x[3 * h + 1 : 3 * h + 2] + x[3 * h + 2 : 3 * h + 3] for x in auxes]
         top = functools.reduce(jnp.maximum, lses)
         weights = [jnp.exp2(x - top) for x in lses]
         scale = 1.0 / sum(weights)
+        for i, w in enumerate(weights):
+            w = w * scale
+            hi = w.astype(BF16).astype(F32)
+            at = 2 * (NX * h + i)
+            table = jnp.where(which == at, hi, jnp.where(which == at + 1, w - hi, table))
+    table = table.astype(BF16)
+    which = lax.broadcasted_iota(jnp.int32, (2 * AUX, HD), 0)
+    for h in range(HPG):
         cols = slice(h * HD, (h + 1) * HD)
-        out = sum(ref[0:rows, cols].astype(F32) * (w * scale) for ref, w in zip(refs, weights, strict=True))
+        out = 0.0
+        for i, ref in enumerate(refs):
+            at = 2 * (NX * h + i)
+            pick = jnp.where((which == at) | (which == at + 1), 1.0, 0.0).astype(BF16)
+            out = out + ref[0:rows, cols].astype(F32) * dot_tn(table, pick)[0:rows]
         out = out.astype(BF16)
         for g in range(NZ):
             video_out[g, :, cols] = out[g * TOK : (g + 1) * TOK]
@@ -375,10 +388,10 @@
     core = functools.partial(shift, axis="c", n=NC, k=1)
     right, left = [shift(kv_own, y, NY, k) for k in (1, 3)]
     q_right, q_left = [shift(q_own, "x", NX, k) for k in (1, 3)]
+    q_far = shift(q_right, "x", NX, 1)
     got = lax.optimization_barrier([left, right, q_left, q_right, q_own, kv_own])
     left, right, q_left, q_right, q_own, kv_own = got
     far = [shift(right[0:VID], y, NY, 1), shift(left[VID:], y, NY, 3)]
-    q_far = shift(q_right, "x", NX, 1)
     kvs = [kv_own, right, left] + [core(b) for b in (kv_own, right, left)]
     state = early([q_right, q_left, q_own], kvs)
     far, q_far, state = lax.optimization_barrier((far, q_far, state))

time: 94.2 us -> 94 us (level)
  no operation moved by 1% of the time
where the time goes in v5:
time: 94 us; the launch traced here: 93.7 us
  starting transfers between devices  38.4 us (41%)
  waiting for transfers between devices  38.2 us (41%)
  Pallas kernels  16.1 us (17%)
    ppermute x15, waiting for transfers between devices, shift(): return lax.ppermute(x, axis, [(i, (i + k) % n) for i in range(n)])  16.9 us
    ppermute x15, starting transfers between devices, shift(): return lax.ppermute(x, axis, [(i, (i + k) % n) for i in range(n)])  15.5 us
    ppermute x1, waiting for transfers between devices, to_group(): return lax.ppermute(x, ('x', 'yh', 'z'), audio_pairs())  15.2 us
    all_to_all x1, starting transfers between devices, on_device(): lax.all_to_all(pack(align, video_q, video_k, video_v), 'z', split_axis=0,...  8.6 us
    pallas_call x2, Pallas kernels, early(): pl.pallas_call(early_body, out_shape=tuple((jax.ShapeDtypeStruct((rows, G...  6.87 us
    all_to_all x1, starting transfers between devices, on_device(): video = lax.all_to_all(video, 'z', split_axis=0, concat_axis=0, tiled=True)  5.69 us
    pallas_call x4, Pallas kernels, late(): pl.pallas_call(late_body, out_shape=jax.ShapeDtypeStruct((QROWS, GW), BF1...  5.18 us
    ppermute x1, starting transfers between devices, to_group(): return lax.ppermute(x, ('x', 'yh', 'z'), audio_pairs())  4.96 us
  transfers between devices with their start and end apart: 19, of which 12 were waited for; matrix products, arithmetic and copies ran while one was open for 0% of the time, Pallas kernels for 11%

profile of v5, /device:TPU:24, one launch (start us, length us, event | category | flops | bytes accessed | tf_op | source)
XLA Modules:
  0.0 93.7 jit_solution(13549776709457289489)
XLA Ops:
  0.6 2.1 %pack.1 = bf16[8,104,384]{2,1,0:T(8,128)(2,1)} custom-call(s32[32]{0:T(128)} %align_ref.1, bf16[32,3072]{1,0:T(8,128)(2,1)} %q_ref.1, bf16[32,3072]{1,0:T(8,128)(2,1)} %k_ref.1, bf16[32,3072]{1,0:T(8,128)(2,1)} %v_ref.1), custom_call_target="tpu_custom_call" | custom-call | tf_op jit(solution)/shard_map/pack/pallas_call | solution.py:54
  2.7 8.6 %all-to-all-start = ((bf16[8,104,384]{2,1,0:T(8,128)(2,1)}), bf16[8,104,384]{2,1,0:T(8,128)(2,1)S(1)}, u32[]{:S(2)}, u32[]{:S(2)}) async-start(bf16[8,104,384]{2,1,0:T(8,128)(2,1)} %pack.1), calls=%async_computation | async-start | bytes 1277952 | tf_op jit(solution)/shard_map/all_to_all | solution.py:383
  11.3 5.0 %collective-permute-start = (bf16[16,1152]{1,0:T(8,128)(2,1)S(1)}, bf16[16,1152]{1,0:T(8,128)(2,1)S(1)}, u32[]{:S(2)}, u32[]{:S(2)}) collective-permute-start(bf16[16,1152]{1,0:T(8,128)(2,1)S(1)} %pad_maximum_fusion), channel_id=1, source_target_pairs={{0,160},{2,96},{4,128},{6,64},{8,0},{10,192},{12,32},{14,224},{34,... | collective-permute-start | bytes 110600 | tf_op jit(solution)/shard_map/ppermute | solution.py:374
  16.3 15.2 %collective-permute-done.aud_ref = bf16[16,1152]{1,0:T(8,128)(2,1)S(1)} collective-permute-done((bf16[16,1152]{1,0:T(8,128)(2,1)S(1)}, bf16[16,1152]{1,0:T(8,128)(2,1)S(1)}, u32[]{:S(2)}, u32[]{:S(2)}) %collective-permute-start) | collective-permute-done | bytes 36896 | tf_op jit(solution)/shard_map/ppermute | solution.py:374
  32.4 1.3 %collective-permute-start.1 = (bf16[560,384]{1,0:T(8,128)(2,1)S(1)}, bf16[560,384]{1,0:T(8,128)(2,1)S(1)}, u32[]{:S(2)}, u32[]{:S(2)}) collective-permute-start(bf16[560,384]{1,0:T(8,128)(2,1)S(1)} %get-tuple-element.43.refs_3_.refs_1_.refs_0_), channel_id=1, source_target_pairs={{0,48},{16,0},{32,16},{48,32},{1,49},{17,1},{33,17},{49,33},{2,50}... | collective-permute-start | bytes 1290248 | tf_op jit(solution)/shard_map/ppermute | solution.py:348
  34.0 2.9 %collective-permute-start.3 = (bf16[288,384]{1,0:T(8,128)(2,1)S(1)}, bf16[288,384]{1,0:T(8,128)(2,1)S(1)}, u32[]{:S(2)}, u32[]{:S(2)}) collective-permute-start(bf16[288,384]{1,0:T(8,128)(2,1)S(1)} %get-tuple-element.38.refs_2_.q_ref), channel_id=1, source_target_pairs={{0,192},{64,0},{128,64},{192,128},{1,193},{65,1},{129,65},{193,129... | collective-permute-start | bytes 663560 | tf_op jit(solution)/shard_map/ppermute | solution.py:348
  37.0 4.5 %collective-permute-done.4.refs_0_.q_ref = bf16[288,384]{1,0:T(8,128)(2,1)S(1)} collective-permute-done((bf16[288,384]{1,0:T(8,128)(2,1)S(1)}, bf16[288,384]{1,0:T(8,128)(2,1)S(1)}, u32[]{:S(2)}, u32[]{:S(2)}) %collective-permute-start.4) | collective-permute-done | bytes 221216 | tf_op jit(solution)/shard_map/ppermute | solution.py:348
  43.2 1.9 %collective-permute-done.1.refs_5_.refs_3_.refs_2_ = bf16[560,384]{1,0:T(8,128)(2,1)S(1)} collective-permute-done((bf16[560,384]{1,0:T(8,128)(2,1)S(1)}, bf16[560,384]{1,0:T(8,128)(2,1)S(1)}, u32[]{:S(2)}, u32[]{:S(2)}) %collective-permute-start.1) | collective-permute-done | bytes 430112 | tf_op jit(solution)/shard_map/ppermute | solution.py:348
  47.0 1.6 %collective-permute-start.6 = (bf16[304,384]{1,0:T(8,128)(2,1)S(1)}, bf16[304,384]{1,0:T(8,128)(2,1)S(1)}, u32[]{:S(2)}, u32[]{:S(2)}) collective-permute-start(bf16[304,384]{1,0:T(8,128)(2,1)S(1)} %slice.7), channel_id=1, source_target_pairs={{0,48},{16,0},{32,16},{48,32},{1,49},{17,1},{33,17},{49,33},{2,50}... | collective-permute-start | bytes 700424 | tf_op jit(solution)/shard_map/ppermute | solution.py:348
  48.6 5.0 %early.2 = (f32[272,384]{1,0:T(8,128)S(1)}, f32[272,384]{1,0:T(8,128)S(1)}, f32[272,384]{1,0:T(8,128)S(1)}, f32[272,384]{1,0:T(8,128)S(1)}, f32[272,384]{1,0:T(8,128)S(1)}, /*index=5*/f32[272,384]{1,0:T(8,128)S(1)}) custom-call(bf16[288,384]{1,0:T(8,128)(2,1)S(1)} %collective-permute-done.4.refs_0_.q_ref, ...), custom_call_target="tpu_custom_call" | custom-call | flops 2887778304 | bytes 4194304 | tf_op jit(solution)/shard_map/early/pallas_call | solution.py:188
  53.6 1.4 %collective-permute-done.7.refs_0_.q_ref = bf16[288,384]{1,0:T(8,128)(2,1)S(1)} collective-permute-done((bf16[288,384]{1,0:T(8,128)(2,1)S(1)}, bf16[288,384]{1,0:T(8,128)(2,1)S(1)}, u32[]{:S(2)}, u32[]{:S(2)}) %collective-permute-start.7) | collective-permute-done | bytes 221216 | tf_op jit(solution)/shard_map/ppermute | solution.py:348
  56.4 1.9 %early.3 = (f32[272,384]{1,0:T(8,128)S(1)}, f32[272,384]{1,0:T(8,128)S(1)}) custom-call(bf16[288,384]{1,0:T(8,128)(2,1)S(1)} %collective-permute-done.7.refs_0_.q_ref, bf16[560,384]{1,0:T(8,128)(2,1)S(1)} %get-tuple-element.43.refs_3_.refs_1_.refs_0_, bf16[560,384]{1,0:T(8,128)(2,1)S(1)} %collective-permute-done.2.refs_4_.refs_2_.refs_1_, ...), custom_call_target="tpu_custom_call" | custom-call | flops 962592768 | bytes 4194304 | tf_op jit(solution)/shard_map/early/pallas_call | solution.py:188
  58.3 1.3 %late.4 = bf16[288,384]{1,0:T(8,128)(2,1)S(1)} custom-call(bf16[288,384]{1,0:T(8,128)(2,1)S(1)} %collective-permute-done.7.refs_0_.q_ref, f32[272,384]{1,0:T(8,128)S(1)} %get-tuple-element.51.o_ref, f32[272,384]{1,0:T(8,128)S(1)} %get-tuple-element.52.l_ref, bf16[560,384]{1,0:T(8,128)(2,1)S(1)} %get-tuple-element.43.refs_3_.refs_1_.refs_0_, ...), custom_call_target="tpu_custom_call" | custom-call | flops 401080320 | bytes 5242880 | tf_op jit(solution)/shard_map/late/pallas_call | solution.py:260
  59.6 3.9 %collective-permute-start.13 = (bf16[288,384]{1,0:T(8,128)(2,1)S(1)}, bf16[288,384]{1,0:T(8,128)(2,1)S(1)}, u32[]{:S(2)}, u32[]{:S(2)}) collective-permute-start(bf16[288,384]{1,0:T(8,128)(2,1)S(1)} %late.4), channel_id=1, source_target_pairs={{0,128},{64,192},{128,0},{192,64},{1,129},{65,193},{129,1},{193,65... | collective-permute-start | bytes 663560 | tf_op jit(solution)/shard_map/ppermute | solution.py:348
  63.5 1.3 %late.6 = bf16[288,384]{1,0:T(8,128)(2,1)S(1)} custom-call(bf16[288,384]{1,0:T(8,128)(2,1)S(1)} %collective-permute-done.4.refs_0_.q_ref, f32[272,384]{1,0:T(8,128)S(1)} %get-tuple-element.64.o_ref, f32[272,384]{1,0:T(8,128)S(1)} %get-tuple-element.65.l_ref, bf16[560,384]{1,0:T(8,128)(2,1)S(1)} %get-tuple-element.43.refs_3_.refs_1_.refs_0_, ...), custom_call_target="tpu_custom_call" | custom-call | flops 401080320 | bytes 5242880 | tf_op jit(solution)/shard_map/late/pallas_call | solution.py:260
  64.8 1.9 %collective-permute-start.14 = (bf16[288,384]{1,0:T(8,128)(2,1)S(1)}, bf16[288,384]{1,0:T(8,128)(2,1)S(1)}, u32[]{:S(2)}, u32[]{:S(2)}) collective-permute-start(bf16[288,384]{1,0:T(8,128)(2,1)S(1)} %late.6), channel_id=1, source_target_pairs={{0,192},{64,0},{128,64},{192,128},{1,193},{65,1},{129,65},{193,129... | collective-permute-start | bytes 663560 | tf_op jit(solution)/shard_map/ppermute | solution.py:348
  66.7 1.3 %late.7 = bf16[288,384]{1,0:T(8,128)(2,1)S(1)} custom-call(bf16[288,384]{1,0:T(8,128)(2,1)S(1)} %collective-permute-done.3.refs_1_.q_ref, f32[272,384]{1,0:T(8,128)S(1)} %get-tuple-element.66.o_ref, f32[272,384]{1,0:T(8,128)S(1)} %get-tuple-element.67.l_ref, bf16[560,384]{1,0:T(8,128)(2,1)S(1)} %get-tuple-element.43.refs_3_.refs_1_.refs_0_, ...), custom_call_target="tpu_custom_call" | custom-call | flops 401080320 | bytes 5242880 | tf_op jit(solution)/shard_map/late/pallas_call | solution.py:260
  68.6 1.3 %late.5.a_ref = bf16[288,384]{1,0:T(8,128)(2,1)S(1)} custom-call(bf16[288,384]{1,0:T(8,128)(2,1)S(1)} %get-tuple-element.38.refs_2_.q_ref, f32[272,384]{1,0:T(8,128)S(1)} %get-tuple-element.61.o_ref, f32[272,384]{1,0:T(8,128)S(1)} %get-tuple-element.62.l_ref, bf16[560,384]{1,0:T(8,128)(2,1)S(1)} %get-tuple-element.43.refs_3_.refs_1_.refs_0_, ...), custom_call_target="tpu_custom_call" | custom-call | flops 401080320 | bytes 5242880 | tf_op jit(solution)/shard_map/late/pallas_call | solution.py:260
  69.9 3.9 %collective-permute-done.14.c_ref = bf16[288,384]{1,0:T(8,128)(2,1)S(1)} collective-permute-done((bf16[288,384]{1,0:T(8,128)(2,1)S(1)}, bf16[288,384]{1,0:T(8,128)(2,1)S(1)}, u32[]{:S(2)}, u32[]{:S(2)}) %collective-permute-start.14) | collective-permute-done | bytes 221216 | tf_op jit(solution)/shard_map/ppermute | solution.py:348
  73.7 2.4 %collective-permute-done.15.d_ref = bf16[288,384]{1,0:T(8,128)(2,1)S(1)} collective-permute-done((bf16[288,384]{1,0:T(8,128)(2,1)S(1)}, bf16[288,384]{1,0:T(8,128)(2,1)S(1)}, u32[]{:S(2)}, u32[]{:S(2)}) %collective-permute-start.15) | collective-permute-done | bytes 221216 | tf_op jit(solution)/shard_map/ppermute | solution.py:348
  77.3 5.7 %all-to-all-start.1 = ((bf16[8,32,384]{2,1,0:T(8,128)(2,1)}), bf16[8,32,384]{2,1,0:T(8,128)(2,1)S(1)}, u32[]{:S(2)}, u32[]{:S(2)}) async-start(bf16[8,32,384]{2,1,0:T(8,128)(2,1)} %get-tuple-element.68), calls=%async_computation.1 | async-start | bytes 393216 | tf_op jit(solution)/shard_map/all_to_all | solution.py:405
  83.0 3.7 %collective-permute-start.16 = (bf16[16,384]{1,0:T(8,128)(2,1)S(1)}, bf16[16,384]{1,0:T(8,128)(2,1)S(1)}, u32[]{:S(2)}, u32[]{:S(2)}) collective-permute-start(bf16[16,384]{1,0:T(8,128)(2,1)S(1)} %get-tuple-element.69), channel_id=1, source_target_pairs={{160,0},{96,2},{128,4},{64,6},{0,8},{192,10},{32,12},{224,14},{130... | collective-permute-start | bytes 36872 | tf_op jit(solution)/shard_map/ppermute | solution.py:378
  86.7 4.5 %collective-permute-done.16.audio_ref = bf16[16,384]{1,0:T(8,128)(2,1)S(1)} collective-permute-done((bf16[16,384]{1,0:T(8,128)(2,1)S(1)}, bf16[16,384]{1,0:T(8,128)(2,1)S(1)}, u32[]{:S(2)}, u32[]{:S(2)}) %collective-permute-start.16) | collective-permute-done | bytes 12320 | tf_op jit(solution)/shard_map/ppermute | solution.py:378
  91.2 1.6 %all-to-all-done.1.video_ref = bf16[8,32,384]{2,1,0:T(8,128)(2,1)S(1)} async-done(((bf16[8,32,384]{2,1,0:T(8,128)(2,1)}), bf16[8,32,384]{2,1,0:T(8,128)(2,1)S(1)}, u32[]{:S(2)}, u32[]{:S(2)}) %all-to-all-start.1) | async-done | bytes 196640 | tf_op jit(solution)/shard_map/all_to_all | solution.py:405
  (33 shorter events, 8.7 us)
Async XLA Ops:
  2.7 8.6 %copy-start = (bf16[16,384]{1,0:T(8,128)(2,1)S(1)}, bf16[16,384]{1,0:T(8,128)(2,1)}, u32[]{:S(2)}) copy-start(bf16[16,384]{1,0:T(8,128)(2,1)} %param.12) | copy-start | bytes 36868
  2.7 8.6 %copy-start.1 = (bf16[16,384]{1,0:T(8,128)(2,1)S(1)}, bf16[16,384]{1,0:T(8,128)(2,1)}, u32[]{:S(2)}) copy-start(bf16[16,384]{1,0:T(8,128)(2,1)} %param.11) | copy-start | bytes 36868
  2.7 8.6 %copy-start.2 = (bf16[16,384]{1,0:T(8,128)(2,1)S(1)}, bf16[16,384]{1,0:T(8,128)(2,1)}, u32[]{:S(2)}) copy-start(bf16[16,384]{1,0:T(8,128)(2,1)} %param.10) | copy-start | bytes 36868
  2.7 28.8 %all-to-all-start = ((bf16[8,104,384]{2,1,0:T(8,128)(2,1)}), bf16[8,104,384]{2,1,0:T(8,128)(2,1)S(1)}, u32[]{:S(2)}, u32[]{:S(2)}) async-start(bf16[8,104,384]{2,1,0:T(8,128)(2,1)} %pack.1), calls=%async_computation | async-start | bytes 1277952 | tf_op jit(solution)/shard_map/all_to_all | solution.py:383
  11.3 20.2 %collective-permute-start = (bf16[16,1152]{1,0:T(8,128)(2,1)S(1)}, bf16[16,1152]{1,0:T(8,128)(2,1)S(1)}, u32[]{:S(2)}, u32[]{:S(2)}) collective-permute-start(bf16[16,1152]{1,0:T(8,128)(2,1)S(1)} %pad_maximum_fusion), channel_id=1, source_target_pairs={{0,160},{2,96},{4,128},{6,64},{8,0},{10,192},{12,32},{14,224},{34,... | collective-permute-start | bytes 110600 | tf_op jit(solution)/shard_map/ppermute | solution.py:374
  31.6 11.6 %collective-permute-start.2 = (bf16[560,384]{1,0:T(8,128)(2,1)S(1)}, bf16[560,384]{1,0:T(8,128)(2,1)S(1)}, u32[]{:S(2)}, u32[]{:S(2)}) collective-permute-start(bf16[560,384]{1,0:T(8,128)(2,1)S(1)} %get-tuple-element.43.refs_3_.refs_1_.refs_0_), channel_id=1, source_target_pairs={{0,16},{16,32},{32,48},{48,0},{1,17},{17,33},{33,49},{49,1},{2,18}... | collective-permute-start | bytes 1290248 | tf_op jit(solution)/shard_map/ppermute | solution.py:348
  32.4 12.8 %collective-permute-start.1 = (bf16[560,384]{1,0:T(8,128)(2,1)S(1)}, bf16[560,384]{1,0:T(8,128)(2,1)S(1)}, u32[]{:S(2)}, u32[]{:S(2)}) collective-permute-start(bf16[560,384]{1,0:T(8,128)(2,1)S(1)} %get-tuple-element.43.refs_3_.refs_1_.refs_0_), channel_id=1, source_target_pairs={{0,48},{16,0},{32,16},{48,32},{1,49},{17,1},{33,17},{49,33},{2,50}... | collective-permute-start | bytes 1290248 | tf_op jit(solution)/shard_map/ppermute | solution.py:348
  33.7 7.7 %collective-permute-start.4 = (bf16[288,384]{1,0:T(8,128)(2,1)S(1)}, bf16[288,384]{1,0:T(8,128)(2,1)S(1)}, u32[]{:S(2)}, u32[]{:S(2)}) collective-permute-start(bf16[288,384]{1,0:T(8,128)(2,1)S(1)} %get-tuple-element.38.refs_2_.q_ref), channel_id=1, source_target_pairs={{0,64},{64,128},{128,192},{192,0},{1,65},{65,129},{129,193},{193,1... | collective-permute-start | bytes 663560 | tf_op jit(solution)/shard_map/ppermute | solution.py:348
  34.0 8.3 %collective-permute-start.3 = (bf16[288,384]{1,0:T(8,128)(2,1)S(1)}, bf16[288,384]{1,0:T(8,128)(2,1)S(1)}, u32[]{:S(2)}, u32[]{:S(2)}) collective-permute-start(bf16[288,384]{1,0:T(8,128)(2,1)S(1)} %get-tuple-element.38.refs_2_.q_ref), channel_id=1, source_target_pairs={{0,192},{64,0},{128,64},{192,128},{1,193},{65,1},{129,65},{193,129... | collective-permute-start | bytes 663560 | tf_op jit(solution)/shard_map/ppermute | solution.py:348
  45.2 1.8 %collective-permute-start.8 = (bf16[560,384]{1,0:T(8,128)(2,1)S(1)}, bf16[560,384]{1,0:T(8,128)(2,1)S(1)}, u32[]{:S(2)}, u32[]{:S(2)}) collective-permute-start(bf16[560,384]{1,0:T(8,128)(2,1)S(1)} %get-tuple-element.43.refs_3_.refs_1_.refs_0_), channel_id=1, source_target_pairs={{0,1},{1,0},{2,3},{3,2},{4,5},{5,4},{6,7},{7,6},{8,9},{9,8},{10,11... | collective-permute-start | bytes 1290248 | tf_op jit(solution)/shard_map/ppermute | solution.py:348
  45.2 3.4 %collective-permute-start.9 = (bf16[560,384]{1,0:T(8,128)(2,1)S(1)}, bf16[560,384]{1,0:T(8,128)(2,1)S(1)}, u32[]{:S(2)}, u32[]{:S(2)}) collective-permute-start(bf16[560,384]{1,0:T(8,128)(2,1)S(1)} %collective-permute-done.2.refs_4_.refs_2_.refs_1_), channel_id=1, source_target_pairs={{0,1},{1,0},{2,3},{3,2},{4,5},{5,4},{6,7},{7,6},{8,9},{9,8},{10,11... | collective-permute-start | bytes 1290248 | tf_op jit(solution)/shard_map/ppermute | solution.py:348
  45.7 2.9 %collective-permute-start.10 = (bf16[560,384]{1,0:T(8,128)(2,1)S(1)}, bf16[560,384]{1,0:T(8,128)(2,1)S(1)}, u32[]{:S(2)}, u32[]{:S(2)}) collective-permute-start(bf16[560,384]{1,0:T(8,128)(2,1)S(1)} %collective-permute-done.1.refs_5_.refs_3_.refs_2_), channel_id=1, source_target_pairs={{0,1},{1,0},{2,3},{3,2},{4,5},{5,4},{6,7},{7,6},{8,9},{9,8},{10,11... | collective-permute-start | bytes 1290248 | tf_op jit(solution)/shard_map/ppermute | solution.py:348
  45.7 9.2 %collective-permute-start.7 = (bf16[288,384]{1,0:T(8,128)(2,1)S(1)}, bf16[288,384]{1,0:T(8,128)(2,1)S(1)}, u32[]{:S(2)}, u32[]{:S(2)}) collective-permute-start(bf16[288,384]{1,0:T(8,128)(2,1)S(1)} %collective-permute-done.4.refs_0_.q_ref), channel_id=1, source_target_pairs={{0,64},{64,128},{128,192},{192,0},{1,65},{65,129},{129,193},{193,1... | collective-permute-start | bytes 663560 | tf_op jit(solution)/shard_map/ppermute | solution.py:348
  46.5 8.5 %collective-permute-start.5 = (bf16[256,384]{1,0:T(8,128)(2,1)S(1)}, bf16[256,384]{1,0:T(8,128)(2,1)S(1)}, u32[]{:S(2)}, u32[]{:S(2)}) collective-permute-start(bf16[256,384]{1,0:T(8,128)(2,1)S(1)} %slice.6), channel_id=1, source_target_pairs={{0,16},{16,32},{32,48},{48,0},{1,17},{17,33},{33,49},{49,1},{2,18}... | collective-permute-start | bytes 589832 | tf_op jit(solution)/shard_map/ppermute | solution.py:348
  47.0 8.9 %collective-permute-start.6 = (bf16[304,384]{1,0:T(8,128)(2,1)S(1)}, bf16[304,384]{1,0:T(8,128)(2,1)S(1)}, u32[]{:S(2)}, u32[]{:S(2)}) collective-permute-start(bf16[304,384]{1,0:T(8,128)(2,1)S(1)} %slice.7), channel_id=1, source_target_pairs={{0,48},{16,0},{32,16},{48,32},{1,49},{17,1},{33,17},{49,33},{2,50}... | collective-permute-start | bytes 700424 | tf_op jit(solution)/shard_map/ppermute | solution.py:348
  55.9 2.4 %collective-permute-start.12 = (bf16[304,384]{1,0:T(8,128)(2,1)S(1)}, bf16[304,384]{1,0:T(8,128)(2,1)S(1)}, u32[]{:S(2)}, u32[]{:S(2)}) collective-permute-start(bf16[304,384]{1,0:T(8,128)(2,1)S(1)} %collective-permute-done.6.refs_7_), channel_id=1, source_target_pairs={{0,1},{1,0},{2,3},{3,2},{4,5},{5,4},{6,7},{7,6},{8,9},{9,8},{10,11... | collective-permute-start | bytes 700424 | tf_op jit(solution)/shard_map/ppermute | solution.py:348
  55.9 2.4 %collective-permute-start.11 = (bf16[256,384]{1,0:T(8,128)(2,1)S(1)}, bf16[256,384]{1,0:T(8,128)(2,1)S(1)}, u32[]{:S(2)}, u32[]{:S(2)}) collective-permute-start(bf16[256,384]{1,0:T(8,128)(2,1)S(1)} %collective-permute-done.5.refs_6_), channel_id=1, source_target_pairs={{0,1},{1,0},{2,3},{3,2},{4,5},{5,4},{6,7},{7,6},{8,9},{9,8},{10,11... | collective-permute-start | bytes 589832 | tf_op jit(solution)/shard_map/ppermute | solution.py:348
  59.6 10.3 %collective-permute-start.13 = (bf16[288,384]{1,0:T(8,128)(2,1)S(1)}, bf16[288,384]{1,0:T(8,128)(2,1)S(1)}, u32[]{:S(2)}, u32[]{:S(2)}) collective-permute-start(bf16[288,384]{1,0:T(8,128)(2,1)S(1)} %late.4), channel_id=1, source_target_pairs={{0,128},{64,192},{128,0},{192,64},{1,129},{65,193},{129,1},{193,65... | collective-permute-start | bytes 663560 | tf_op jit(solution)/shard_map/ppermute | solution.py:348
  64.8 8.9 %collective-permute-start.14 = (bf16[288,384]{1,0:T(8,128)(2,1)S(1)}, bf16[288,384]{1,0:T(8,128)(2,1)S(1)}, u32[]{:S(2)}, u32[]{:S(2)}) collective-permute-start(bf16[288,384]{1,0:T(8,128)(2,1)S(1)} %late.6), channel_id=1, source_target_pairs={{0,192},{64,0},{128,64},{192,128},{1,193},{65,1},{129,65},{193,129... | collective-permute-start | bytes 663560 | tf_op jit(solution)/shard_map/ppermute | solution.py:348
  68.0 8.1 %collective-permute-start.15 = (bf16[288,384]{1,0:T(8,128)(2,1)S(1)}, bf16[288,384]{1,0:T(8,128)(2,1)S(1)}, u32[]{:S(2)}, u32[]{:S(2)}) collective-permute-start(bf16[288,384]{1,0:T(8,128)(2,1)S(1)} %late.7), channel_id=1, source_target_pairs={{0,64},{64,128},{128,192},{192,0},{1,65},{65,129},{129,193},{193,1... | collective-permute-start | bytes 663560 | tf_op jit(solution)/shard_map/ppermute | solution.py:348
  77.3 15.5 %all-to-all-start.1 = ((bf16[8,32,384]{2,1,0:T(8,128)(2,1)}), bf16[8,32,384]{2,1,0:T(8,128)(2,1)S(1)}, u32[]{:S(2)}, u32[]{:S(2)}) async-start(bf16[8,32,384]{2,1,0:T(8,128)(2,1)} %get-tuple-element.68), calls=%async_computation.1 | async-start | bytes 393216 | tf_op jit(solution)/shard_map/all_to_all | solution.py:405
  83.0 8.2 %collective-permute-start.16 = (bf16[16,384]{1,0:T(8,128)(2,1)S(1)}, bf16[16,384]{1,0:T(8,128)(2,1)S(1)}, u32[]{:S(2)}, u32[]{:S(2)}) collective-permute-start(bf16[16,384]{1,0:T(8,128)(2,1)S(1)} %get-tuple-element.69), channel_id=1, source_target_pairs={{160,0},{96,2},{128,4},{64,6},{0,8},{192,10},{32,12},{224,14},{130... | collective-permute-start | bytes 36872 | tf_op jit(solution)/shard_map/ppermute | solution.py:378

commit v6 on v5

--- a/solution.py
+++ b/solution.py
@@ -40,20 +40,23 @@
         row = jnp.where(lane == first + i, align_ref[i], row)
     high = (row >> 4).astype(F32)
     low = (row & 15).astype(F32)
-    which = lax.broadcasted_iota(jnp.int32, (STAMPS, GW), 0)
-    stamps = jnp.where(which == 0, high, jnp.where(which == 1, low, 0.0)).astype(BF16)
+    which = lax.broadcasted_iota(jnp.int32, (STAMPS, HD), 0)
+    stamps = jnp.zeros((STAMPS, HD), F32)
+    for n, part in enumerate((high[:, 0:HD], high[:, HD:VID], low[:, 0:HD], low[:, HD:VID])):
+        stamps = jnp.where(which == n, part, stamps)
+    stamps = stamps.astype(BF16)
     for g in range(NZ):
-        cols = slice(g * GW, (g + 1) * GW)
-        out[g, 0:TOK, :] = q_ref[:, cols]
-        out[g, TOK : 2 * TOK, :] = k_ref[:, cols]
-        out[g, 2 * TOK : 3 * TOK, :] = v_ref[:, cols]
-        out[g, 3 * TOK :, :] = stamps
+        for n, ref in enumerate((q_ref, k_ref, v_ref)):
+            for h in range(HPG):
+                at = (n * HPG + h) * TOK
+                out[g, at : at + TOK, :] = ref[:, (g * HPG + h) * HD : (g * HPG + h + 1) * HD]
+        out[g, 3 * HPG * TOK :, :] = stamps
 
 
 def pack(align, q, k, v):
     return pl.pallas_call(
         pack_body,
-        out_shape=jax.ShapeDtypeStruct((NZ, 3 * TOK + STAMPS, GW), BF16),
+        out_shape=jax.ShapeDtypeStruct((NZ, 3 * HPG * TOK + STAMPS, HD), BF16),
         in_specs=[SMEM, VMEM, VMEM, VMEM],
         out_specs=VMEM,
         name="pack",
@@ -61,8 +64,8 @@
 
 
 def audio_times(start):
-    lane = lax.broadcasted_iota(jnp.int32, (STAMPS, GW), 1) - VID
-    which = lax.broadcasted_iota(jnp.int32, (STAMPS, GW), 0)
+    lane = lax.broadcasted_iota(jnp.int32, (AUX, GW), 1) - VID
+    which = lax.broadcasted_iota(jnp.int32, (AUX, GW), 0)
     stamp = lane + start
     here = (lane >= 0) & (lane < AUD)
     part = jnp.where(which == 0, stamp >> 4, jnp.where(which == 1, stamp & 15, 0))
@@ -71,19 +74,25 @@
 
 def join_body(got_ref, aud_ref, q_out, kv_out):
     block = lax.axis_index("yl") * 16 + audio_z() * 2 + lax.axis_index("c")
-    total = audio_times(block * AUD)
+    stamps = jnp.zeros((STAMPS, HD), F32)
     for g in range(NZ):
-        at = g * TOK
-        q_out[at : at + TOK, :] = got_ref[g, 0:TOK, :]
-        kv_out[at : at + TOK, :] = got_ref[g, TOK : 2 * TOK, :]
-        kv_out[VID + at : VID + at + TOK, :] = got_ref[g, 2 * TOK : 3 * TOK, :]
-        total = total + got_ref[g, 3 * TOK :, :].astype(F32)
-    total = jnp.concatenate([total, jnp.zeros((AUX - STAMPS, GW), F32)], axis=0)
+        for h in range(HPG):
+            cols = slice(h * HD, (h + 1) * HD)
+            for n, (out, first) in enumerate(((q_out, 0), (kv_out, 0), (kv_out, VID))):
+                at = (n * HPG + h) * TOK
+                out[first + g * TOK : first + (g + 1) * TOK, cols] = got_ref[g, at : at + TOK, :]
+        stamps = stamps + got_ref[g, 3 * HPG * TOK :, :].astype(F32)
+    none = jnp.zeros((1, HD), F32)
+    high = jnp.concatenate([stamps[0:1], stamps[1:2], none], axis=1)
+    low = jnp.concatenate([stamps[2:3], stamps[3:4], none], axis=1)
+    which = lax.broadcasted_iota(jnp.int32, (AUX, GW), 0)
+    aux = jnp.where(which == 0, high, jnp.where(which == 1, low, 0.0)) + audio_times(block * AUD)
+    aux = aux.astype(BF16)
     q_out[VID : VID + AUD, :] = aud_ref[:, 0:GW]
     kv_out[2 * VID : 2 * VID + AUD, :] = aud_ref[:, GW : 2 * GW]
     kv_out[2 * VID + AUD : 2 * VID + 2 * AUD, :] = aud_ref[:, 2 * GW :]
-    q_out[VID + AUD :, :] = total.astype(BF16)
-    kv_out[2 * VID + 2 * AUD :, :] = total.astype(BF16)
+    q_out[VID + AUD :, :] = aux
+    kv_out[2 * VID + 2 * AUD :, :] = aux
 
 
 def join(got, aud):
@@ -197,13 +206,21 @@
     )(*qs, *kvs)
 
 
+class Block:
+    def __init__(self, keys, rest):
+        self.keys, self.rest = keys, rest
+
+    def __getitem__(self, at):
+        rows, cols = at
+        if rows.stop <= VID:
+            return self.keys[rows, cols]
+        return self.rest[rows.start - VID : rows.stop - VID, cols]
+
+
 def late_body(q_ref, o_ref, l_ref, *refs):
-    out, s_ref, far_ref, twin_ref = refs[EARLY + 4 :]
+    out, s_ref = refs[EARLY + 4 :]
     rows = VID + AUD
-    for n, ref in enumerate((far_ref, twin_ref)):
-        ref[0:VID, :] = refs[EARLY + 2 * n][...]
-        ref[VID:, :] = refs[EARLY + 2 * n + 1][...]
-    rest = (far_ref, twin_ref)
+    rest = (Block(*refs[EARLY : EARLY + 2]), Block(*refs[EARLY + 2 : EARLY + 4]))
     k_refs = refs[0:EARLY] + rest
     ka_times = place([times_of(k_ref, 2 * VID + 2 * AUD)[:, VID:] for k_ref in k_refs])
     k_times = [times_of(k_ref, 2 * VID + 2 * AUD) for k_ref in rest]
@@ -262,11 +279,7 @@
         out_shape=jax.ShapeDtypeStruct((QROWS, GW), BF16),
         in_specs=[VMEM] * (3 + EARLY + 4),
         out_specs=VMEM,
-        scratch_shapes=[
-            pltpu.VMEM((HPG, rows, nk), F32),
-            pltpu.VMEM((KROWS, GW), BF16),
-            pltpu.VMEM((KROWS, GW), BF16),
-        ],
+        scratch_shapes=[pltpu.VMEM((HPG, rows, nk), F32)],
         compiler_params=pltpu.CompilerParams(vmem_limit_bytes=16 * 2**20),
         cost_estimate=pl.CostEstimate(flops=6 * area * HD, bytes_accessed=5 << 20, transcendentals=area),
         name="late",

time: 94 us -> 93.2 us (level)
  no operation moved by 1% of the time
where the time goes in v6:
time: 93.2 us; the launch traced here: 92.9 us
  starting transfers between devices  38.4 us (41%)
  waiting for transfers between devices  37.5 us (40%)
  Pallas kernels  16 us (17%)
  between operations  0.94 us (1%)
    ppermute x15, waiting for transfers between devices, shift(): return lax.ppermute(x, axis, [(i, (i + k) % n) for i in range(n)])  16.9 us
    ppermute x15, starting transfers between devices, shift(): return lax.ppermute(x, axis, [(i, (i + k) % n) for i in range(n)])  15.5 us
    ppermute x1, waiting for transfers between devices, to_group(): return lax.ppermute(x, ('x', 'yh', 'z'), audio_pairs())  14.5 us
    all_to_all x1, starting transfers between devices, on_device(): lax.all_to_all(pack(align, video_q, video_k, video_v), 'z', split_axis=0,...  8.6 us
    pallas_call x2, Pallas kernels, early(): pl.pallas_call(early_body, out_shape=tuple((jax.ShapeDtypeStruct((rows, G...  6.87 us
    all_to_all x1, starting transfers between devices, on_device(): video = lax.all_to_all(video, 'z', split_axis=0, concat_axis=0, tiled=True)  5.7 us
    pallas_call x4, Pallas kernels, late(): pl.pallas_call(late_body, out_shape=jax.ShapeDtypeStruct((QROWS, GW), BF1...  4.99 us
    ppermute x1, starting transfers between devices, to_group(): return lax.ppermute(x, ('x', 'yh', 'z'), audio_pairs())  4.96 us
  transfers between devices with their start and end apart: 19, of which 12 were waited for; matrix products, arithmetic and copies ran while one was open for 0% of the time, Pallas kernels for 11%

profile of v6, /device:TPU:24, one launch (start us, length us, event | category | flops | bytes accessed | tf_op | source)
XLA Modules:
  0.0 92.9 jit_solution(17075861345112032345)
XLA Ops:
  0.6 2.1 %pack.1 = bf16[8,296,128]{2,1,0:T(8,128)(2,1)} custom-call(s32[32]{0:T(128)} %align_ref.1, bf16[32,3072]{1,0:T(8,128)(2,1)} %q_ref.1, bf16[32,3072]{1,0:T(8,128)(2,1)} %k_ref.1, bf16[32,3072]{1,0:T(8,128)(2,1)} %v_ref.1), custom_call_target="tpu_custom_call" | custom-call | tf_op jit(solution)/shard_map/pack/pallas_call | solution.py:57
  2.7 8.6 %all-to-all-start = ((bf16[8,296,128]{2,1,0:T(8,128)(2,1)}), bf16[8,296,128]{2,1,0:T(8,128)(2,1)S(1)}, u32[]{:S(2)}, u32[]{:S(2)}) async-start(bf16[8,296,128]{2,1,0:T(8,128)(2,1)} %pack.1), calls=%async_computation | async-start | bytes 1212416 | tf_op jit(solution)/shard_map/all_to_all | solution.py:396
  11.4 5.0 %collective-permute-start = (bf16[16,1152]{1,0:T(8,128)(2,1)S(1)}, bf16[16,1152]{1,0:T(8,128)(2,1)S(1)}, u32[]{:S(2)}, u32[]{:S(2)}) collective-permute-start(bf16[16,1152]{1,0:T(8,128)(2,1)S(1)} %pad_maximum_fusion), channel_id=1, source_target_pairs={{0,160},{2,96},{4,128},{6,64},{8,0},{10,192},{12,32},{14,224},{34,... | collective-permute-start | bytes 110600 | tf_op jit(solution)/shard_map/ppermute | solution.py:387
  16.3 14.5 %collective-permute-done.aud_ref = bf16[16,1152]{1,0:T(8,128)(2,1)S(1)} collective-permute-done((bf16[16,1152]{1,0:T(8,128)(2,1)S(1)}, bf16[16,1152]{1,0:T(8,128)(2,1)S(1)}, u32[]{:S(2)}, u32[]{:S(2)}) %collective-permute-start) | collective-permute-done | bytes 36896 | tf_op jit(solution)/shard_map/ppermute | solution.py:387
  31.8 1.3 %collective-permute-start.1 = (bf16[560,384]{1,0:T(8,128)(2,1)S(1)}, bf16[560,384]{1,0:T(8,128)(2,1)S(1)}, u32[]{:S(2)}, u32[]{:S(2)}) collective-permute-start(bf16[560,384]{1,0:T(8,128)(2,1)S(1)} %get-tuple-element.43.refs_3_.refs_1_.refs_0_), channel_id=1, source_target_pairs={{0,48},{16,0},{32,16},{48,32},{1,49},{17,1},{33,17},{49,33},{2,50}... | collective-permute-start | bytes 1290248 | tf_op jit(solution)/shard_map/ppermute | solution.py:361
  33.4 2.9 %collective-permute-start.3 = (bf16[288,384]{1,0:T(8,128)(2,1)S(1)}, bf16[288,384]{1,0:T(8,128)(2,1)S(1)}, u32[]{:S(2)}, u32[]{:S(2)}) collective-permute-start(bf16[288,384]{1,0:T(8,128)(2,1)S(1)} %get-tuple-element.38.refs_2_.q_ref), channel_id=1, source_target_pairs={{0,192},{64,0},{128,64},{192,128},{1,193},{65,1},{129,65},{193,129... | collective-permute-start | bytes 663560 | tf_op jit(solution)/shard_map/ppermute | solution.py:361
  36.3 4.5 %collective-permute-done.4.refs_0_.q_ref = bf16[288,384]{1,0:T(8,128)(2,1)S(1)} collective-permute-done((bf16[288,384]{1,0:T(8,128)(2,1)S(1)}, bf16[288,384]{1,0:T(8,128)(2,1)S(1)}, u32[]{:S(2)}, u32[]{:S(2)}) %collective-permute-start.4) | collective-permute-done | bytes 221216 | tf_op jit(solution)/shard_map/ppermute | solution.py:361
  42.6 1.9 %collective-permute-done.1.refs_5_.refs_3_.refs_2_ = bf16[560,384]{1,0:T(8,128)(2,1)S(1)} collective-permute-done((bf16[560,384]{1,0:T(8,128)(2,1)S(1)}, bf16[560,384]{1,0:T(8,128)(2,1)S(1)}, u32[]{:S(2)}, u32[]{:S(2)}) %collective-permute-start.1) | collective-permute-done | bytes 430112 | tf_op jit(solution)/shard_map/ppermute | solution.py:361
  46.3 1.6 %collective-permute-start.6 = (bf16[304,384]{1,0:T(8,128)(2,1)S(1)}, bf16[304,384]{1,0:T(8,128)(2,1)S(1)}, u32[]{:S(2)}, u32[]{:S(2)}) collective-permute-start(bf16[304,384]{1,0:T(8,128)(2,1)S(1)} %slice.7), channel_id=1, source_target_pairs={{0,48},{16,0},{32,16},{48,32},{1,49},{17,1},{33,17},{49,33},{2,50}... | collective-permute-start | bytes 700424 | tf_op jit(solution)/shard_map/ppermute | solution.py:361
  48.0 5.0 %early.2 = (f32[272,384]{1,0:T(8,128)S(1)}, f32[272,384]{1,0:T(8,128)S(1)}, f32[272,384]{1,0:T(8,128)S(1)}, f32[272,384]{1,0:T(8,128)S(1)}, f32[272,384]{1,0:T(8,128)S(1)}, /*index=5*/f32[272,384]{1,0:T(8,128)S(1)}) custom-call(bf16[288,384]{1,0:T(8,128)(2,1)S(1)} %collective-permute-done.4.refs_0_.q_ref, ...), custom_call_target="tpu_custom_call" | custom-call | flops 2887778304 | bytes 4194304 | tf_op jit(solution)/shard_map/early/pallas_call | solution.py:197
  53.0 1.4 %collective-permute-done.7.refs_0_.q_ref = bf16[288,384]{1,0:T(8,128)(2,1)S(1)} collective-permute-done((bf16[288,384]{1,0:T(8,128)(2,1)S(1)}, bf16[288,384]{1,0:T(8,128)(2,1)S(1)}, u32[]{:S(2)}, u32[]{:S(2)}) %collective-permute-start.7) | collective-permute-done | bytes 221216 | tf_op jit(solution)/shard_map/ppermute | solution.py:361
  55.8 1.9 %early.3 = (f32[272,384]{1,0:T(8,128)S(1)}, f32[272,384]{1,0:T(8,128)S(1)}) custom-call(bf16[288,384]{1,0:T(8,128)(2,1)S(1)} %collective-permute-done.7.refs_0_.q_ref, bf16[560,384]{1,0:T(8,128)(2,1)S(1)} %get-tuple-element.43.refs_3_.refs_1_.refs_0_, bf16[560,384]{1,0:T(8,128)(2,1)S(1)} %collective-permute-done.2.refs_4_.refs_2_.refs_1_, ...), custom_call_target="tpu_custom_call" | custom-call | flops 962592768 | bytes 4194304 | tf_op jit(solution)/shard_map/early/pallas_call | solution.py:197
  57.7 1.2 %late.4 = bf16[288,384]{1,0:T(8,128)(2,1)S(1)} custom-call(bf16[288,384]{1,0:T(8,128)(2,1)S(1)} %collective-permute-done.7.refs_0_.q_ref, f32[272,384]{1,0:T(8,128)S(1)} %get-tuple-element.51.o_ref, f32[272,384]{1,0:T(8,128)S(1)} %get-tuple-element.52.l_ref, bf16[560,384]{1,0:T(8,128)(2,1)S(1)} %get-tuple-element.43.refs_3_.refs_1_.refs_0_, ...), custom_call_target="tpu_custom_call" | custom-call | flops 401080320 | bytes 5242880 | tf_op jit(solution)/shard_map/late/pallas_call | solution.py:277
  58.9 4.0 %collective-permute-start.13 = (bf16[288,384]{1,0:T(8,128)(2,1)S(1)}, bf16[288,384]{1,0:T(8,128)(2,1)S(1)}, u32[]{:S(2)}, u32[]{:S(2)}) collective-permute-start(bf16[288,384]{1,0:T(8,128)(2,1)S(1)} %late.4), channel_id=1, source_target_pairs={{0,128},{64,192},{128,0},{192,64},{1,129},{65,193},{129,1},{193,65... | collective-permute-start | bytes 663560 | tf_op jit(solution)/shard_map/ppermute | solution.py:361
  62.9 1.3 %late.6 = bf16[288,384]{1,0:T(8,128)(2,1)S(1)} custom-call(bf16[288,384]{1,0:T(8,128)(2,1)S(1)} %collective-permute-done.4.refs_0_.q_ref, f32[272,384]{1,0:T(8,128)S(1)} %get-tuple-element.64.o_ref, f32[272,384]{1,0:T(8,128)S(1)} %get-tuple-element.65.l_ref, bf16[560,384]{1,0:T(8,128)(2,1)S(1)} %get-tuple-element.43.refs_3_.refs_1_.refs_0_, ...), custom_call_target="tpu_custom_call" | custom-call | flops 401080320 | bytes 5242880 | tf_op jit(solution)/shard_map/late/pallas_call | solution.py:277
  64.2 1.9 %collective-permute-start.14 = (bf16[288,384]{1,0:T(8,128)(2,1)S(1)}, bf16[288,384]{1,0:T(8,128)(2,1)S(1)}, u32[]{:S(2)}, u32[]{:S(2)}) collective-permute-start(bf16[288,384]{1,0:T(8,128)(2,1)S(1)} %late.6), channel_id=1, source_target_pairs={{0,192},{64,0},{128,64},{192,128},{1,193},{65,1},{129,65},{193,129... | collective-permute-start | bytes 663560 | tf_op jit(solution)/shard_map/ppermute | solution.py:361
  66.0 1.2 %late.7 = bf16[288,384]{1,0:T(8,128)(2,1)S(1)} custom-call(bf16[288,384]{1,0:T(8,128)(2,1)S(1)} %collective-permute-done.3.refs_1_.q_ref, f32[272,384]{1,0:T(8,128)S(1)} %get-tuple-element.66.o_ref, f32[272,384]{1,0:T(8,128)S(1)} %get-tuple-element.67.l_ref, bf16[560,384]{1,0:T(8,128)(2,1)S(1)} %get-tuple-element.43.refs_3_.refs_1_.refs_0_, ...), custom_call_target="tpu_custom_call" | custom-call | flops 401080320 | bytes 5242880 | tf_op jit(solution)/shard_map/late/pallas_call | solution.py:277
  67.8 1.2 %late.5.a_ref = bf16[288,384]{1,0:T(8,128)(2,1)S(1)} custom-call(bf16[288,384]{1,0:T(8,128)(2,1)S(1)} %get-tuple-element.38.refs_2_.q_ref, f32[272,384]{1,0:T(8,128)S(1)} %get-tuple-element.61.o_ref, f32[272,384]{1,0:T(8,128)S(1)} %get-tuple-element.62.l_ref, bf16[560,384]{1,0:T(8,128)(2,1)S(1)} %get-tuple-element.43.refs_3_.refs_1_.refs_0_, ...), custom_call_target="tpu_custom_call" | custom-call | flops 401080320 | bytes 5242880 | tf_op jit(solution)/shard_map/late/pallas_call | solution.py:277
  69.1 4.0 %collective-permute-done.14.c_ref = bf16[288,384]{1,0:T(8,128)(2,1)S(1)} collective-permute-done((bf16[288,384]{1,0:T(8,128)(2,1)S(1)}, bf16[288,384]{1,0:T(8,128)(2,1)S(1)}, u32[]{:S(2)}, u32[]{:S(2)}) %collective-permute-start.14) | collective-permute-done | bytes 221216 | tf_op jit(solution)/shard_map/ppermute | solution.py:361
  73.1 2.2 %collective-permute-done.15.d_ref = bf16[288,384]{1,0:T(8,128)(2,1)S(1)} collective-permute-done((bf16[288,384]{1,0:T(8,128)(2,1)S(1)}, bf16[288,384]{1,0:T(8,128)(2,1)S(1)}, u32[]{:S(2)}, u32[]{:S(2)}) %collective-permute-start.15) | collective-permute-done | bytes 221216 | tf_op jit(solution)/shard_map/ppermute | solution.py:361
  76.5 5.7 %all-to-all-start.1 = ((bf16[8,32,384]{2,1,0:T(8,128)(2,1)}), bf16[8,32,384]{2,1,0:T(8,128)(2,1)S(1)}, u32[]{:S(2)}, u32[]{:S(2)}) async-start(bf16[8,32,384]{2,1,0:T(8,128)(2,1)} %get-tuple-element.68), calls=%async_computation.1 | async-start | bytes 393216 | tf_op jit(solution)/shard_map/all_to_all | solution.py:418
  82.2 3.7 %collective-permute-start.16 = (bf16[16,384]{1,0:T(8,128)(2,1)S(1)}, bf16[16,384]{1,0:T(8,128)(2,1)S(1)}, u32[]{:S(2)}, u32[]{:S(2)}) collective-permute-start(bf16[16,384]{1,0:T(8,128)(2,1)S(1)} %get-tuple-element.69), channel_id=1, source_target_pairs={{160,0},{96,2},{128,4},{64,6},{0,8},{192,10},{32,12},{224,14},{130... | collective-permute-start | bytes 36872 | tf_op jit(solution)/shard_map/ppermute | solution.py:391
  86.0 4.5 %collective-permute-done.16.audio_ref = bf16[16,384]{1,0:T(8,128)(2,1)S(1)} collective-permute-done((bf16[16,384]{1,0:T(8,128)(2,1)S(1)}, bf16[16,384]{1,0:T(8,128)(2,1)S(1)}, u32[]{:S(2)}, u32[]{:S(2)}) %collective-permute-start.16) | collective-permute-done | bytes 12320 | tf_op jit(solution)/shard_map/ppermute | solution.py:391
  90.5 1.6 %all-to-all-done.1.video_ref = bf16[8,32,384]{2,1,0:T(8,128)(2,1)S(1)} async-done(((bf16[8,32,384]{2,1,0:T(8,128)(2,1)}), bf16[8,32,384]{2,1,0:T(8,128)(2,1)S(1)}, u32[]{:S(2)}, u32[]{:S(2)}) %all-to-all-start.1) | async-done | bytes 196640 | tf_op jit(solution)/shard_map/all_to_all | solution.py:418
  (33 shorter events, 8.8 us)
Async XLA Ops:
  2.7 8.6 %copy-start = (bf16[16,384]{1,0:T(8,128)(2,1)S(1)}, bf16[16,384]{1,0:T(8,128)(2,1)}, u32[]{:S(2)}) copy-start(bf16[16,384]{1,0:T(8,128)(2,1)} %param.12) | copy-start | bytes 36868
  2.7 8.6 %copy-start.1 = (bf16[16,384]{1,0:T(8,128)(2,1)S(1)}, bf16[16,384]{1,0:T(8,128)(2,1)}, u32[]{:S(2)}) copy-start(bf16[16,384]{1,0:T(8,128)(2,1)} %param.11) | copy-start | bytes 36868
  2.7 8.6 %copy-start.2 = (bf16[16,384]{1,0:T(8,128)(2,1)S(1)}, bf16[16,384]{1,0:T(8,128)(2,1)}, u32[]{:S(2)}) copy-start(bf16[16,384]{1,0:T(8,128)(2,1)} %param.10) | copy-start | bytes 36868
  2.7 28.1 %all-to-all-start = ((bf16[8,296,128]{2,1,0:T(8,128)(2,1)}), bf16[8,296,128]{2,1,0:T(8,128)(2,1)S(1)}, u32[]{:S(2)}, u32[]{:S(2)}) async-start(bf16[8,296,128]{2,1,0:T(8,128)(2,1)} %pack.1), calls=%async_computation | async-start | bytes 1212416 | tf_op jit(solution)/shard_map/all_to_all | solution.py:396
  11.4 19.5 %collective-permute-start = (bf16[16,1152]{1,0:T(8,128)(2,1)S(1)}, bf16[16,1152]{1,0:T(8,128)(2,1)S(1)}, u32[]{:S(2)}, u32[]{:S(2)}) collective-permute-start(bf16[16,1152]{1,0:T(8,128)(2,1)S(1)} %pad_maximum_fusion), channel_id=1, source_target_pairs={{0,160},{2,96},{4,128},{6,64},{8,0},{10,192},{12,32},{14,224},{34,... | collective-permute-start | bytes 110600 | tf_op jit(solution)/shard_map/ppermute | solution.py:387
  31.0 11.6 %collective-permute-start.2 = (bf16[560,384]{1,0:T(8,128)(2,1)S(1)}, bf16[560,384]{1,0:T(8,128)(2,1)S(1)}, u32[]{:S(2)}, u32[]{:S(2)}) collective-permute-start(bf16[560,384]{1,0:T(8,128)(2,1)S(1)} %get-tuple-element.43.refs_3_.refs_1_.refs_0_), channel_id=1, source_target_pairs={{0,16},{16,32},{32,48},{48,0},{1,17},{17,33},{33,49},{49,1},{2,18}... | collective-permute-start | bytes 1290248 | tf_op jit(solution)/shard_map/ppermute | solution.py:361
  31.8 12.8 %collective-permute-start.1 = (bf16[560,384]{1,0:T(8,128)(2,1)S(1)}, bf16[560,384]{1,0:T(8,128)(2,1)S(1)}, u32[]{:S(2)}, u32[]{:S(2)}) collective-permute-start(bf16[560,384]{1,0:T(8,128)(2,1)S(1)} %get-tuple-element.43.refs_3_.refs_1_.refs_0_), channel_id=1, source_target_pairs={{0,48},{16,0},{32,16},{48,32},{1,49},{17,1},{33,17},{49,33},{2,50}... | collective-permute-start | bytes 1290248 | tf_op jit(solution)/shard_map/ppermute | solution.py:361
  33.1 7.7 %collective-permute-start.4 = (bf16[288,384]{1,0:T(8,128)(2,1)S(1)}, bf16[288,384]{1,0:T(8,128)(2,1)S(1)}, u32[]{:S(2)}, u32[]{:S(2)}) collective-permute-start(bf16[288,384]{1,0:T(8,128)(2,1)S(1)} %get-tuple-element.38.refs_2_.q_ref), channel_id=1, source_target_pairs={{0,64},{64,128},{128,192},{192,0},{1,65},{65,129},{129,193},{193,1... | collective-permute-start | bytes 663560 | tf_op jit(solution)/shard_map/ppermute | solution.py:361
  33.4 8.3 %collective-permute-start.3 = (bf16[288,384]{1,0:T(8,128)(2,1)S(1)}, bf16[288,384]{1,0:T(8,128)(2,1)S(1)}, u32[]{:S(2)}, u32[]{:S(2)}) collective-permute-start(bf16[288,384]{1,0:T(8,128)(2,1)S(1)} %get-tuple-element.38.refs_2_.q_ref), channel_id=1, source_target_pairs={{0,192},{64,0},{128,64},{192,128},{1,193},{65,1},{129,65},{193,129... | collective-permute-start | bytes 663560 | tf_op jit(solution)/shard_map/ppermute | solution.py:361
  44.6 1.8 %collective-permute-start.8 = (bf16[560,384]{1,0:T(8,128)(2,1)S(1)}, bf16[560,384]{1,0:T(8,128)(2,1)S(1)}, u32[]{:S(2)}, u32[]{:S(2)}) collective-permute-start(bf16[560,384]{1,0:T(8,128)(2,1)S(1)} %get-tuple-element.43.refs_3_.refs_1_.refs_0_), channel_id=1, source_target_pairs={{0,1},{1,0},{2,3},{3,2},{4,5},{5,4},{6,7},{7,6},{8,9},{9,8},{10,11... | collective-permute-start | bytes 1290248 | tf_op jit(solution)/shard_map/ppermute | solution.py:361
  44.6 3.4 %collective-permute-start.9 = (bf16[560,384]{1,0:T(8,128)(2,1)S(1)}, bf16[560,384]{1,0:T(8,128)(2,1)S(1)}, u32[]{:S(2)}, u32[]{:S(2)}) collective-permute-start(bf16[560,384]{1,0:T(8,128)(2,1)S(1)} %collective-permute-done.2.refs_4_.refs_2_.refs_1_), channel_id=1, source_target_pairs={{0,1},{1,0},{2,3},{3,2},{4,5},{5,4},{6,7},{7,6},{8,9},{9,8},{10,11... | collective-permute-start | bytes 1290248 | tf_op jit(solution)/shard_map/ppermute | solution.py:361
  45.1 2.9 %collective-permute-start.10 = (bf16[560,384]{1,0:T(8,128)(2,1)S(1)}, bf16[560,384]{1,0:T(8,128)(2,1)S(1)}, u32[]{:S(2)}, u32[]{:S(2)}) collective-permute-start(bf16[560,384]{1,0:T(8,128)(2,1)S(1)} %collective-permute-done.1.refs_5_.refs_3_.refs_2_), channel_id=1, source_target_pairs={{0,1},{1,0},{2,3},{3,2},{4,5},{5,4},{6,7},{7,6},{8,9},{9,8},{10,11... | collective-permute-start | bytes 1290248 | tf_op jit(solution)/shard_map/ppermute | solution.py:361
  45.1 9.2 %collective-permute-start.7 = (bf16[288,384]{1,0:T(8,128)(2,1)S(1)}, bf16[288,384]{1,0:T(8,128)(2,1)S(1)}, u32[]{:S(2)}, u32[]{:S(2)}) collective-permute-start(bf16[288,384]{1,0:T(8,128)(2,1)S(1)} %collective-permute-done.4.refs_0_.q_ref), channel_id=1, source_target_pairs={{0,64},{64,128},{128,192},{192,0},{1,65},{65,129},{129,193},{193,1... | collective-permute-start | bytes 663560 | tf_op jit(solution)/shard_map/ppermute | solution.py:361
  45.8 8.5 %collective-permute-start.5 = (bf16[256,384]{1,0:T(8,128)(2,1)S(1)}, bf16[256,384]{1,0:T(8,128)(2,1)S(1)}, u32[]{:S(2)}, u32[]{:S(2)}) collective-permute-start(bf16[256,384]{1,0:T(8,128)(2,1)S(1)} %slice.6), channel_id=1, source_target_pairs={{0,16},{16,32},{32,48},{48,0},{1,17},{17,33},{33,49},{49,1},{2,18}... | collective-permute-start | bytes 589832 | tf_op jit(solution)/shard_map/ppermute | solution.py:361
  46.3 8.9 %collective-permute-start.6 = (bf16[304,384]{1,0:T(8,128)(2,1)S(1)}, bf16[304,384]{1,0:T(8,128)(2,1)S(1)}, u32[]{:S(2)}, u32[]{:S(2)}) collective-permute-start(bf16[304,384]{1,0:T(8,128)(2,1)S(1)} %slice.7), channel_id=1, source_target_pairs={{0,48},{16,0},{32,16},{48,32},{1,49},{17,1},{33,17},{49,33},{2,50}... | collective-permute-start | bytes 700424 | tf_op jit(solution)/shard_map/ppermute | solution.py:361
  55.3 2.4 %collective-permute-start.12 = (bf16[304,384]{1,0:T(8,128)(2,1)S(1)}, bf16[304,384]{1,0:T(8,128)(2,1)S(1)}, u32[]{:S(2)}, u32[]{:S(2)}) collective-permute-start(bf16[304,384]{1,0:T(8,128)(2,1)S(1)} %collective-permute-done.6.refs_7_), channel_id=1, source_target_pairs={{0,1},{1,0},{2,3},{3,2},{4,5},{5,4},{6,7},{7,6},{8,9},{9,8},{10,11... | collective-permute-start | bytes 700424 | tf_op jit(solution)/shard_map/ppermute | solution.py:361
  55.3 2.4 %collective-permute-start.11 = (bf16[256,384]{1,0:T(8,128)(2,1)S(1)}, bf16[256,384]{1,0:T(8,128)(2,1)S(1)}, u32[]{:S(2)}, u32[]{:S(2)}) collective-permute-start(bf16[256,384]{1,0:T(8,128)(2,1)S(1)} %collective-permute-done.5.refs_6_), channel_id=1, source_target_pairs={{0,1},{1,0},{2,3},{3,2},{4,5},{5,4},{6,7},{7,6},{8,9},{9,8},{10,11... | collective-permute-start | bytes 589832 | tf_op jit(solution)/shard_map/ppermute | solution.py:361
  58.9 10.1 %collective-permute-start.13 = (bf16[288,384]{1,0:T(8,128)(2,1)S(1)}, bf16[288,384]{1,0:T(8,128)(2,1)S(1)}, u32[]{:S(2)}, u32[]{:S(2)}) collective-permute-start(bf16[288,384]{1,0:T(8,128)(2,1)S(1)} %late.4), channel_id=1, source_target_pairs={{0,128},{64,192},{128,0},{192,64},{1,129},{65,193},{129,1},{193,65... | collective-permute-start | bytes 663560 | tf_op jit(solution)/shard_map/ppermute | solution.py:361
  64.2 8.9 %collective-permute-start.14 = (bf16[288,384]{1,0:T(8,128)(2,1)S(1)}, bf16[288,384]{1,0:T(8,128)(2,1)S(1)}, u32[]{:S(2)}, u32[]{:S(2)}) collective-permute-start(bf16[288,384]{1,0:T(8,128)(2,1)S(1)} %late.6), channel_id=1, source_target_pairs={{0,192},{64,0},{128,64},{192,128},{1,193},{65,1},{129,65},{193,129... | collective-permute-start | bytes 663560 | tf_op jit(solution)/shard_map/ppermute | solution.py:361
  67.3 8.1 %collective-permute-start.15 = (bf16[288,384]{1,0:T(8,128)(2,1)S(1)}, bf16[288,384]{1,0:T(8,128)(2,1)S(1)}, u32[]{:S(2)}, u32[]{:S(2)}) collective-permute-start(bf16[288,384]{1,0:T(8,128)(2,1)S(1)} %late.7), channel_id=1, source_target_pairs={{0,64},{64,128},{128,192},{192,0},{1,65},{65,129},{129,193},{193,1... | collective-permute-start | bytes 663560 | tf_op jit(solution)/shard_map/ppermute | solution.py:361
  76.5 15.5 %all-to-all-start.1 = ((bf16[8,32,384]{2,1,0:T(8,128)(2,1)}), bf16[8,32,384]{2,1,0:T(8,128)(2,1)S(1)}, u32[]{:S(2)}, u32[]{:S(2)}) async-start(bf16[8,32,384]{2,1,0:T(8,128)(2,1)} %get-tuple-element.68), calls=%async_computation.1 | async-start | bytes 393216 | tf_op jit(solution)/shard_map/all_to_all | solution.py:418
  82.2 8.2 %collective-permute-start.16 = (bf16[16,384]{1,0:T(8,128)(2,1)S(1)}, bf16[16,384]{1,0:T(8,128)(2,1)S(1)}, u32[]{:S(2)}, u32[]{:S(2)}) collective-permute-start(bf16[16,384]{1,0:T(8,128)(2,1)S(1)} %get-tuple-element.69), channel_id=1, source_target_pairs={{160,0},{96,2},{128,4},{64,6},{0,8},{192,10},{32,12},{224,14},{130... | collective-permute-start | bytes 36872 | tf_op jit(solution)/shard_map/ppermute | solution.py:391

commit v7 on v6

--- a/solution.py
+++ b/solution.py
@@ -399,12 +399,12 @@
     q_own, kv_own = join(got, aud)
     y = ("yh", "yl")
     core = functools.partial(shift, axis="c", n=NC, k=1)
-    right, left = [shift(kv_own, y, NY, k) for k in (1, 3)]
-    q_right, q_left = [shift(q_own, "x", NX, k) for k in (1, 3)]
-    q_far = shift(q_right, "x", NX, 1)
+    right, left = [shift(kv_own, "x", NX, k) for k in (1, 3)]
+    q_right, q_left = [shift(q_own, y, NY, k) for k in (1, 3)]
+    q_far = shift(q_right, y, NY, 1)
     got = lax.optimization_barrier([left, right, q_left, q_right, q_own, kv_own])
     left, right, q_left, q_right, q_own, kv_own = got
-    far = [shift(right[0:VID], y, NY, 1), shift(left[VID:], y, NY, 3)]
+    far = [shift(right[0:VID], "x", NX, 1), shift(left[VID:], "x", NX, 3)]
     kvs = [kv_own, right, left] + [core(b) for b in (kv_own, right, left)]
     state = early([q_right, q_left, q_own], kvs)
     far, q_far, state = lax.optimization_barrier((far, q_far, state))
@@ -413,7 +413,7 @@
     kvs = kvs + far + others
     part_far, state = lax.optimization_barrier((late(q_far, state_far, kvs), state))
     parts = [part_far] + [late(q, state[2 * i : 2 * i + 2], kvs) for i, q in enumerate([q_right, q_left, q_own])]
-    back = [shift(p, "x", NX, -k) for p, k in zip(parts, (2, 1, 3))]
+    back = [shift(p, y, NY, -k) for p, k in zip(parts, (2, 1, 3))]
     video, audio = combine(parts[3:] + back)
     video = lax.all_to_all(video, "z", split_axis=0, concat_axis=0, tiled=True)
     return spread(video, from_group(audio))

time: 93.2 us -> 92.5 us (level); the launches traced: 92.9 us -> 91 us
  waiting for transfers between devices: 37.5 us -> 34.2 us
  starting transfers between devices: 38.4 us -> 39.8 us
    ppermute x15, waiting for transfers between devices: 16.9 us -> 13 us  [shift(): return lax.ppermute(x, axis, [(i, (i + k) % n) for i in range(n)])]
    ppermute x1, waiting for transfers between devices: 4.48 us -> 5.75 us  [from_group(): return lax.ppermute(x, ('x', 'yh', 'z'), [(b, a) for a, b in audio_pairs()])]
  transfers between devices with their start and end apart: 19 -> 19, of which waited for: 12 -> 9; matrix products, arithmetic and copies ran while one was open for 0% -> 0% of each run, Pallas kernels for 11% -> 12%
where the time goes in v7:
time: 92.5 us; the launch traced here: 91 us
  starting transfers between devices  39.8 us (43%)
  waiting for transfers between devices  34.2 us (37%)
  Pallas kernels  16 us (17%)
  between operations  0.96 us (1%)
    ppermute x15, starting transfers between devices, shift(): return lax.ppermute(x, axis, [(i, (i + k) % n) for i in range(n)])  16.2 us
    ppermute x1, waiting for transfers between devices, to_group(): return lax.ppermute(x, ('x', 'yh', 'z'), audio_pairs())  14.5 us
    ppermute x15, waiting for transfers between devices, shift(): return lax.ppermute(x, axis, [(i, (i + k) % n) for i in range(n)])  13 us
    all_to_all x1, starting transfers between devices, on_device(): lax.all_to_all(pack(align, video_q, video_k, video_v), 'z', split_axis=0,...  8.6 us
    pallas_call x2, Pallas kernels, early(): pl.pallas_call(early_body, out_shape=tuple((jax.ShapeDtypeStruct((rows, G...  6.87 us
    all_to_all x1, starting transfers between devices, on_device(): video = lax.all_to_all(video, 'z', split_axis=0, concat_axis=0, tiled=True)  5.97 us
    ppermute x1, waiting for transfers between devices, from_group(): return lax.ppermute(x, ('x', 'yh', 'z'), [(b, a) for a, b in audio_pairs()])  5.75 us
    pallas_call x4, Pallas kernels, late(): pl.pallas_call(late_body, out_shape=jax.ShapeDtypeStruct((QROWS, GW), BF1...  5 us
  transfers between devices with their start and end apart: 19, of which 9 were waited for; matrix products, arithmetic and copies ran while one was open for 0% of the time, Pallas kernels for 12%

profile of v7, /device:TPU:24, one launch (start us, length us, event | category | flops | bytes accessed | tf_op | source)
XLA Modules:
  0.0 91.0 jit_solution(4149357182676032374)
XLA Ops:
  0.6 2.1 %pack.1 = bf16[8,296,128]{2,1,0:T(8,128)(2,1)} custom-call(s32[32]{0:T(128)} %align_ref.1, bf16[32,3072]{1,0:T(8,128)(2,1)} %q_ref.1, bf16[32,3072]{1,0:T(8,128)(2,1)} %k_ref.1, bf16[32,3072]{1,0:T(8,128)(2,1)} %v_ref.1), custom_call_target="tpu_custom_call" | custom-call | tf_op jit(solution)/shard_map/pack/pallas_call | solution.py:57
  2.7 8.6 %all-to-all-start = ((bf16[8,296,128]{2,1,0:T(8,128)(2,1)}), bf16[8,296,128]{2,1,0:T(8,128)(2,1)S(1)}, u32[]{:S(2)}, u32[]{:S(2)}) async-start(bf16[8,296,128]{2,1,0:T(8,128)(2,1)} %pack.1), calls=%async_computation | async-start | bytes 1212416 | tf_op jit(solution)/shard_map/all_to_all | solution.py:396
  11.4 5.0 %collective-permute-start = (bf16[16,1152]{1,0:T(8,128)(2,1)S(1)}, bf16[16,1152]{1,0:T(8,128)(2,1)S(1)}, u32[]{:S(2)}, u32[]{:S(2)}) collective-permute-start(bf16[16,1152]{1,0:T(8,128)(2,1)S(1)} %pad_maximum_fusion), channel_id=1, source_target_pairs={{0,160},{2,96},{4,128},{6,64},{8,0},{10,192},{12,32},{14,224},{34,... | collective-permute-start | bytes 110600 | tf_op jit(solution)/shard_map/ppermute | solution.py:387
  16.3 14.5 %collective-permute-done.aud_ref = bf16[16,1152]{1,0:T(8,128)(2,1)S(1)} collective-permute-done((bf16[16,1152]{1,0:T(8,128)(2,1)S(1)}, bf16[16,1152]{1,0:T(8,128)(2,1)S(1)}, u32[]{:S(2)}, u32[]{:S(2)}) %collective-permute-start) | collective-permute-done | bytes 36896 | tf_op jit(solution)/shard_map/ppermute | solution.py:387
  31.4 2.9 %collective-permute-start.1 = (bf16[560,384]{1,0:T(8,128)(2,1)S(1)}, bf16[560,384]{1,0:T(8,128)(2,1)S(1)}, u32[]{:S(2)}, u32[]{:S(2)}) collective-permute-start(bf16[560,384]{1,0:T(8,128)(2,1)S(1)} %get-tuple-element.43.refs_3_.refs_1_.refs_0_), channel_id=1, source_target_pairs={{0,192},{64,0},{128,64},{192,128},{1,193},{65,1},{129,65},{193,129... | collective-permute-start | bytes 1290248 | tf_op jit(solution)/shard_map/ppermute | solution.py:361
  34.3 1.2 %collective-permute-start.4 = (bf16[288,384]{1,0:T(8,128)(2,1)S(1)}, bf16[288,384]{1,0:T(8,128)(2,1)S(1)}, u32[]{:S(2)}, u32[]{:S(2)}) collective-permute-start(bf16[288,384]{1,0:T(8,128)(2,1)S(1)} %get-tuple-element.38.refs_2_.q_ref), channel_id=1, source_target_pairs={{0,16},{16,32},{32,48},{48,0},{1,17},{17,33},{33,49},{49,1},{2,18}... | collective-permute-start | bytes 663560 | tf_op jit(solution)/shard_map/ppermute | solution.py:361
  36.3 4.5 %collective-permute-done.4.refs_0_.q_ref = bf16[288,384]{1,0:T(8,128)(2,1)S(1)} collective-permute-done((bf16[288,384]{1,0:T(8,128)(2,1)S(1)}, bf16[288,384]{1,0:T(8,128)(2,1)S(1)}, u32[]{:S(2)}, u32[]{:S(2)}) %collective-permute-start.4) | collective-permute-done | bytes 221216 | tf_op jit(solution)/shard_map/ppermute | solution.py:361
  40.8 2.2 %collective-permute-done.3.refs_1_.q_ref = bf16[288,384]{1,0:T(8,128)(2,1)S(1)} collective-permute-done((bf16[288,384]{1,0:T(8,128)(2,1)S(1)}, bf16[288,384]{1,0:T(8,128)(2,1)S(1)}, u32[]{:S(2)}, u32[]{:S(2)}) %collective-permute-start.3) | collective-permute-done | bytes 221216 | tf_op jit(solution)/shard_map/ppermute | solution.py:361
  43.8 0.9 %collective-permute-done.1.refs_5_.refs_3_.refs_2_ = bf16[560,384]{1,0:T(8,128)(2,1)S(1)} collective-permute-done((bf16[560,384]{1,0:T(8,128)(2,1)S(1)}, bf16[560,384]{1,0:T(8,128)(2,1)S(1)}, u32[]{:S(2)}, u32[]{:S(2)}) %collective-permute-start.1) | collective-permute-done | bytes 430112 | tf_op jit(solution)/shard_map/ppermute | solution.py:361
  45.6 1.5 %collective-permute-start.5 = (bf16[256,384]{1,0:T(8,128)(2,1)S(1)}, bf16[256,384]{1,0:T(8,128)(2,1)S(1)}, u32[]{:S(2)}, u32[]{:S(2)}) collective-permute-start(bf16[256,384]{1,0:T(8,128)(2,1)S(1)} %slice.6), channel_id=1, source_target_pairs={{0,64},{64,128},{128,192},{192,0},{1,65},{65,129},{129,193},{193,1... | collective-permute-start | bytes 589832 | tf_op jit(solution)/shard_map/ppermute | solution.py:361
  47.2 1.9 %collective-permute-start.6 = (bf16[304,384]{1,0:T(8,128)(2,1)S(1)}, bf16[304,384]{1,0:T(8,128)(2,1)S(1)}, u32[]{:S(2)}, u32[]{:S(2)}) collective-permute-start(bf16[304,384]{1,0:T(8,128)(2,1)S(1)} %slice.7), channel_id=1, source_target_pairs={{0,192},{64,0},{128,64},{192,128},{1,193},{65,1},{129,65},{193,129... | collective-permute-start | bytes 700424 | tf_op jit(solution)/shard_map/ppermute | solution.py:361
  49.0 5.0 %early.2 = (f32[272,384]{1,0:T(8,128)S(1)}, f32[272,384]{1,0:T(8,128)S(1)}, f32[272,384]{1,0:T(8,128)S(1)}, f32[272,384]{1,0:T(8,128)S(1)}, f32[272,384]{1,0:T(8,128)S(1)}, /*index=5*/f32[272,384]{1,0:T(8,128)S(1)}) custom-call(bf16[288,384]{1,0:T(8,128)(2,1)S(1)} %collective-permute-done.4.refs_0_.q_ref, ...), custom_call_target="tpu_custom_call" | custom-call | flops 2887778304 | bytes 4194304 | tf_op jit(solution)/shard_map/early/pallas_call | solution.py:197
  55.5 1.9 %early.3 = (f32[272,384]{1,0:T(8,128)S(1)}, f32[272,384]{1,0:T(8,128)S(1)}) custom-call(bf16[288,384]{1,0:T(8,128)(2,1)S(1)} %collective-permute-done.7.refs_0_.q_ref, bf16[560,384]{1,0:T(8,128)(2,1)S(1)} %get-tuple-element.43.refs_3_.refs_1_.refs_0_, bf16[560,384]{1,0:T(8,128)(2,1)S(1)} %collective-permute-done.2.refs_4_.refs_2_.refs_1_, ...), custom_call_target="tpu_custom_call" | custom-call | flops 962592768 | bytes 4194304 | tf_op jit(solution)/shard_map/early/pallas_call | solution.py:197
  57.4 1.3 %late.4 = bf16[288,384]{1,0:T(8,128)(2,1)S(1)} custom-call(bf16[288,384]{1,0:T(8,128)(2,1)S(1)} %collective-permute-done.7.refs_0_.q_ref, f32[272,384]{1,0:T(8,128)S(1)} %get-tuple-element.51.o_ref, f32[272,384]{1,0:T(8,128)S(1)} %get-tuple-element.52.l_ref, bf16[560,384]{1,0:T(8,128)(2,1)S(1)} %get-tuple-element.43.refs_3_.refs_1_.refs_0_, ...), custom_call_target="tpu_custom_call" | custom-call | flops 401080320 | bytes 5242880 | tf_op jit(solution)/shard_map/late/pallas_call | solution.py:277
  58.7 2.6 %collective-permute-start.13 = (bf16[288,384]{1,0:T(8,128)(2,1)S(1)}, bf16[288,384]{1,0:T(8,128)(2,1)S(1)}, u32[]{:S(2)}, u32[]{:S(2)}) collective-permute-start(bf16[288,384]{1,0:T(8,128)(2,1)S(1)} %late.4), channel_id=1, source_target_pairs={{0,32},{16,48},{32,0},{48,16},{1,33},{17,49},{33,1},{49,17},{2,34}... | collective-permute-start | bytes 663560 | tf_op jit(solution)/shard_map/ppermute | solution.py:361
  61.3 1.2 %late.6 = bf16[288,384]{1,0:T(8,128)(2,1)S(1)} custom-call(bf16[288,384]{1,0:T(8,128)(2,1)S(1)} %collective-permute-done.4.refs_0_.q_ref, f32[272,384]{1,0:T(8,128)S(1)} %get-tuple-element.64.o_ref, f32[272,384]{1,0:T(8,128)S(1)} %get-tuple-element.65.l_ref, bf16[560,384]{1,0:T(8,128)(2,1)S(1)} %get-tuple-element.43.refs_3_.refs_1_.refs_0_, ...), custom_call_target="tpu_custom_call" | custom-call | flops 401080320 | bytes 5242880 | tf_op jit(solution)/shard_map/late/pallas_call | solution.py:277
  62.8 1.3 %late.7 = bf16[288,384]{1,0:T(8,128)(2,1)S(1)} custom-call(bf16[288,384]{1,0:T(8,128)(2,1)S(1)} %collective-permute-done.3.refs_1_.q_ref, f32[272,384]{1,0:T(8,128)S(1)} %get-tuple-element.66.o_ref, f32[272,384]{1,0:T(8,128)S(1)} %get-tuple-element.67.l_ref, bf16[560,384]{1,0:T(8,128)(2,1)S(1)} %get-tuple-element.43.refs_3_.refs_1_.refs_0_, ...), custom_call_target="tpu_custom_call" | custom-call | flops 401080320 | bytes 5242880 | tf_op jit(solution)/shard_map/late/pallas_call | solution.py:277
  64.1 3.3 %collective-permute-start.15 = (bf16[288,384]{1,0:T(8,128)(2,1)S(1)}, bf16[288,384]{1,0:T(8,128)(2,1)S(1)}, u32[]{:S(2)}, u32[]{:S(2)}) collective-permute-start(bf16[288,384]{1,0:T(8,128)(2,1)S(1)} %late.7), channel_id=1, source_target_pairs={{0,16},{16,32},{32,48},{48,0},{1,17},{17,33},{33,49},{49,1},{2,18}... | collective-permute-start | bytes 663560 | tf_op jit(solution)/shard_map/ppermute | solution.py:361
  67.4 1.2 %late.5.a_ref = bf16[288,384]{1,0:T(8,128)(2,1)S(1)} custom-call(bf16[288,384]{1,0:T(8,128)(2,1)S(1)} %get-tuple-element.38.refs_2_.q_ref, f32[272,384]{1,0:T(8,128)S(1)} %get-tuple-element.61.o_ref, f32[272,384]{1,0:T(8,128)S(1)} %get-tuple-element.62.l_ref, bf16[560,384]{1,0:T(8,128)(2,1)S(1)} %get-tuple-element.43.refs_3_.refs_1_.refs_0_, ...), custom_call_target="tpu_custom_call" | custom-call | flops 401080320 | bytes 5242880 | tf_op jit(solution)/shard_map/late/pallas_call | solution.py:277
  68.6 3.7 %collective-permute-done.14.c_ref = bf16[288,384]{1,0:T(8,128)(2,1)S(1)} collective-permute-done((bf16[288,384]{1,0:T(8,128)(2,1)S(1)}, bf16[288,384]{1,0:T(8,128)(2,1)S(1)}, u32[]{:S(2)}, u32[]{:S(2)}) %collective-permute-start.14) | collective-permute-done | bytes 221216 | tf_op jit(solution)/shard_map/ppermute | solution.py:361
  72.3 1.2 %combine.1 = (bf16[8,32,384]{2,1,0:T(8,128)(2,1)}, bf16[16,384]{1,0:T(8,128)(2,1)S(1)}) custom-call(bf16[288,384]{1,0:T(8,128)(2,1)S(1)} %late.5.a_ref, bf16[288,384]{1,0:T(8,128)(2,1)S(1)} %collective-permute-done.13.b_ref, bf16[288,384]{1,0:T(8,128)(2,1)S(1)} %collective-permute-done.14.c_ref, bf16[288,384]{1,0:T(8,128)(2,1)S(1)} %collective-permute-done.15.d_ref), custom_call_target="tpu_custom_call" | custom-call | tf_op jit(solution)/shard_map/combine/pallas_call | solution.py:321
  73.5 6.0 %all-to-all-start.1 = ((bf16[8,32,384]{2,1,0:T(8,128)(2,1)}), bf16[8,32,384]{2,1,0:T(8,128)(2,1)S(1)}, u32[]{:S(2)}, u32[]{:S(2)}) async-start(bf16[8,32,384]{2,1,0:T(8,128)(2,1)} %get-tuple-element.68), calls=%async_computation.1 | async-start | bytes 393216 | tf_op jit(solution)/shard_map/all_to_all | solution.py:418
  79.5 4.1 %collective-permute-start.16 = (bf16[16,384]{1,0:T(8,128)(2,1)S(1)}, bf16[16,384]{1,0:T(8,128)(2,1)S(1)}, u32[]{:S(2)}, u32[]{:S(2)}) collective-permute-start(bf16[16,384]{1,0:T(8,128)(2,1)S(1)} %get-tuple-element.69), channel_id=1, source_target_pairs={{160,0},{96,2},{128,4},{64,6},{0,8},{192,10},{32,12},{224,14},{130... | collective-permute-start | bytes 36872 | tf_op jit(solution)/shard_map/ppermute | solution.py:391
  83.5 5.7 %collective-permute-done.16.audio_ref = bf16[16,384]{1,0:T(8,128)(2,1)S(1)} collective-permute-done((bf16[16,384]{1,0:T(8,128)(2,1)S(1)}, bf16[16,384]{1,0:T(8,128)(2,1)S(1)}, u32[]{:S(2)}, u32[]{:S(2)}) %collective-permute-start.16) | collective-permute-done | bytes 12320 | tf_op jit(solution)/shard_map/ppermute | solution.py:391
  (33 shorter events, 6.3 us)
Async XLA Ops:
  2.7 8.6 %copy-start = (bf16[16,384]{1,0:T(8,128)(2,1)S(1)}, bf16[16,384]{1,0:T(8,128)(2,1)}, u32[]{:S(2)}) copy-start(bf16[16,384]{1,0:T(8,128)(2,1)} %param.12) | copy-start | bytes 36868
  2.7 8.6 %copy-start.1 = (bf16[16,384]{1,0:T(8,128)(2,1)S(1)}, bf16[16,384]{1,0:T(8,128)(2,1)}, u32[]{:S(2)}) copy-start(bf16[16,384]{1,0:T(8,128)(2,1)} %param.11) | copy-start | bytes 36868
  2.7 8.6 %copy-start.2 = (bf16[16,384]{1,0:T(8,128)(2,1)S(1)}, bf16[16,384]{1,0:T(8,128)(2,1)}, u32[]{:S(2)}) copy-start(bf16[16,384]{1,0:T(8,128)(2,1)} %param.10) | copy-start | bytes 36868
  2.7 28.1 %all-to-all-start = ((bf16[8,296,128]{2,1,0:T(8,128)(2,1)}), bf16[8,296,128]{2,1,0:T(8,128)(2,1)S(1)}, u32[]{:S(2)}, u32[]{:S(2)}) async-start(bf16[8,296,128]{2,1,0:T(8,128)(2,1)} %pack.1), calls=%async_computation | async-start | bytes 1212416 | tf_op jit(solution)/shard_map/all_to_all | solution.py:396
  11.4 19.5 %collective-permute-start = (bf16[16,1152]{1,0:T(8,128)(2,1)S(1)}, bf16[16,1152]{1,0:T(8,128)(2,1)S(1)}, u32[]{:S(2)}, u32[]{:S(2)}) collective-permute-start(bf16[16,1152]{1,0:T(8,128)(2,1)S(1)} %pad_maximum_fusion), channel_id=1, source_target_pairs={{0,160},{2,96},{4,128},{6,64},{8,0},{10,192},{12,32},{14,224},{34,... | collective-permute-start | bytes 110600 | tf_op jit(solution)/shard_map/ppermute | solution.py:387
  31.0 12.8 %collective-permute-start.2 = (bf16[560,384]{1,0:T(8,128)(2,1)S(1)}, bf16[560,384]{1,0:T(8,128)(2,1)S(1)}, u32[]{:S(2)}, u32[]{:S(2)}) collective-permute-start(bf16[560,384]{1,0:T(8,128)(2,1)S(1)} %get-tuple-element.43.refs_3_.refs_1_.refs_0_), channel_id=1, source_target_pairs={{0,64},{64,128},{128,192},{192,0},{1,65},{65,129},{129,193},{193,1... | collective-permute-start | bytes 1290248 | tf_op jit(solution)/shard_map/ppermute | solution.py:361
  31.4 13.4 %collective-permute-start.1 = (bf16[560,384]{1,0:T(8,128)(2,1)S(1)}, bf16[560,384]{1,0:T(8,128)(2,1)S(1)}, u32[]{:S(2)}, u32[]{:S(2)}) collective-permute-start(bf16[560,384]{1,0:T(8,128)(2,1)S(1)} %get-tuple-element.43.refs_3_.refs_1_.refs_0_), channel_id=1, source_target_pairs={{0,192},{64,0},{128,64},{192,128},{1,193},{65,1},{129,65},{193,129... | collective-permute-start | bytes 1290248 | tf_op jit(solution)/shard_map/ppermute | solution.py:361
  34.3 6.5 %collective-permute-start.4 = (bf16[288,384]{1,0:T(8,128)(2,1)S(1)}, bf16[288,384]{1,0:T(8,128)(2,1)S(1)}, u32[]{:S(2)}, u32[]{:S(2)}) collective-permute-start(bf16[288,384]{1,0:T(8,128)(2,1)S(1)} %get-tuple-element.38.refs_2_.q_ref), channel_id=1, source_target_pairs={{0,16},{16,32},{32,48},{48,0},{1,17},{17,33},{33,49},{49,1},{2,18}... | collective-permute-start | bytes 663560 | tf_op jit(solution)/shard_map/ppermute | solution.py:361
  35.5 7.5 %collective-permute-start.3 = (bf16[288,384]{1,0:T(8,128)(2,1)S(1)}, bf16[288,384]{1,0:T(8,128)(2,1)S(1)}, u32[]{:S(2)}, u32[]{:S(2)}) collective-permute-start(bf16[288,384]{1,0:T(8,128)(2,1)S(1)} %get-tuple-element.38.refs_2_.q_ref), channel_id=1, source_target_pairs={{0,48},{16,0},{32,16},{48,32},{1,49},{17,1},{33,17},{49,33},{2,50}... | collective-permute-start | bytes 663560 | tf_op jit(solution)/shard_map/ppermute | solution.py:361
  44.8 2.4 %collective-permute-start.8 = (bf16[560,384]{1,0:T(8,128)(2,1)S(1)}, bf16[560,384]{1,0:T(8,128)(2,1)S(1)}, u32[]{:S(2)}, u32[]{:S(2)}) collective-permute-start(bf16[560,384]{1,0:T(8,128)(2,1)S(1)} %get-tuple-element.43.refs_3_.refs_1_.refs_0_), channel_id=1, source_target_pairs={{0,1},{1,0},{2,3},{3,2},{4,5},{5,4},{6,7},{7,6},{8,9},{9,8},{10,11... | collective-permute-start | bytes 1290248 | tf_op jit(solution)/shard_map/ppermute | solution.py:361
  44.8 4.3 %collective-permute-start.9 = (bf16[560,384]{1,0:T(8,128)(2,1)S(1)}, bf16[560,384]{1,0:T(8,128)(2,1)S(1)}, u32[]{:S(2)}, u32[]{:S(2)}) collective-permute-start(bf16[560,384]{1,0:T(8,128)(2,1)S(1)} %collective-permute-done.2.refs_4_.refs_2_.refs_1_), channel_id=1, source_target_pairs={{0,1},{1,0},{2,3},{3,2},{4,5},{5,4},{6,7},{7,6},{8,9},{9,8},{10,11... | collective-permute-start | bytes 1290248 | tf_op jit(solution)/shard_map/ppermute | solution.py:361
  45.3 3.7 %collective-permute-start.10 = (bf16[560,384]{1,0:T(8,128)(2,1)S(1)}, bf16[560,384]{1,0:T(8,128)(2,1)S(1)}, u32[]{:S(2)}, u32[]{:S(2)}) collective-permute-start(bf16[560,384]{1,0:T(8,128)(2,1)S(1)} %collective-permute-done.1.refs_5_.refs_3_.refs_2_), channel_id=1, source_target_pairs={{0,1},{1,0},{2,3},{3,2},{4,5},{5,4},{6,7},{7,6},{8,9},{9,8},{10,11... | collective-permute-start | bytes 1290248 | tf_op jit(solution)/shard_map/ppermute | solution.py:361
  45.3 8.8 %collective-permute-start.7 = (bf16[288,384]{1,0:T(8,128)(2,1)S(1)}, bf16[288,384]{1,0:T(8,128)(2,1)S(1)}, u32[]{:S(2)}, u32[]{:S(2)}) collective-permute-start(bf16[288,384]{1,0:T(8,128)(2,1)S(1)} %collective-permute-done.4.refs_0_.q_ref), channel_id=1, source_target_pairs={{0,16},{16,32},{32,48},{48,0},{1,17},{17,33},{33,49},{49,1},{2,18}... | collective-permute-start | bytes 663560 | tf_op jit(solution)/shard_map/ppermute | solution.py:361
  45.6 8.4 %collective-permute-start.5 = (bf16[256,384]{1,0:T(8,128)(2,1)S(1)}, bf16[256,384]{1,0:T(8,128)(2,1)S(1)}, u32[]{:S(2)}, u32[]{:S(2)}) collective-permute-start(bf16[256,384]{1,0:T(8,128)(2,1)S(1)} %slice.6), channel_id=1, source_target_pairs={{0,64},{64,128},{128,192},{192,0},{1,65},{65,129},{129,193},{193,1... | collective-permute-start | bytes 589832 | tf_op jit(solution)/shard_map/ppermute | solution.py:361
  47.2 7.8 %collective-permute-start.6 = (bf16[304,384]{1,0:T(8,128)(2,1)S(1)}, bf16[304,384]{1,0:T(8,128)(2,1)S(1)}, u32[]{:S(2)}, u32[]{:S(2)}) collective-permute-start(bf16[304,384]{1,0:T(8,128)(2,1)S(1)} %slice.7), channel_id=1, source_target_pairs={{0,192},{64,0},{128,64},{192,128},{1,193},{65,1},{129,65},{193,129... | collective-permute-start | bytes 700424 | tf_op jit(solution)/shard_map/ppermute | solution.py:361
  55.0 2.4 %collective-permute-start.12 = (bf16[304,384]{1,0:T(8,128)(2,1)S(1)}, bf16[304,384]{1,0:T(8,128)(2,1)S(1)}, u32[]{:S(2)}, u32[]{:S(2)}) collective-permute-start(bf16[304,384]{1,0:T(8,128)(2,1)S(1)} %collective-permute-done.6.refs_7_), channel_id=1, source_target_pairs={{0,1},{1,0},{2,3},{3,2},{4,5},{5,4},{6,7},{7,6},{8,9},{9,8},{10,11... | collective-permute-start | bytes 700424 | tf_op jit(solution)/shard_map/ppermute | solution.py:361
  55.0 2.4 %collective-permute-start.11 = (bf16[256,384]{1,0:T(8,128)(2,1)S(1)}, bf16[256,384]{1,0:T(8,128)(2,1)S(1)}, u32[]{:S(2)}, u32[]{:S(2)}) collective-permute-start(bf16[256,384]{1,0:T(8,128)(2,1)S(1)} %collective-permute-done.5.refs_6_), channel_id=1, source_target_pairs={{0,1},{1,0},{2,3},{3,2},{4,5},{5,4},{6,7},{7,6},{8,9},{9,8},{10,11... | collective-permute-start | bytes 589832 | tf_op jit(solution)/shard_map/ppermute | solution.py:361
  58.7 10.0 %collective-permute-start.13 = (bf16[288,384]{1,0:T(8,128)(2,1)S(1)}, bf16[288,384]{1,0:T(8,128)(2,1)S(1)}, u32[]{:S(2)}, u32[]{:S(2)}) collective-permute-start(bf16[288,384]{1,0:T(8,128)(2,1)S(1)} %late.4), channel_id=1, source_target_pairs={{0,32},{16,48},{32,0},{48,16},{1,33},{17,49},{33,1},{49,17},{2,34}... | collective-permute-start | bytes 663560 | tf_op jit(solution)/shard_map/ppermute | solution.py:361
  62.5 9.8 %collective-permute-start.14 = (bf16[288,384]{1,0:T(8,128)(2,1)S(1)}, bf16[288,384]{1,0:T(8,128)(2,1)S(1)}, u32[]{:S(2)}, u32[]{:S(2)}) collective-permute-start(bf16[288,384]{1,0:T(8,128)(2,1)S(1)} %late.6), channel_id=1, source_target_pairs={{0,48},{16,0},{32,16},{48,32},{1,49},{17,1},{33,17},{49,33},{2,50}... | collective-permute-start | bytes 663560 | tf_op jit(solution)/shard_map/ppermute | solution.py:361
  64.1 8.2 %collective-permute-start.15 = (bf16[288,384]{1,0:T(8,128)(2,1)S(1)}, bf16[288,384]{1,0:T(8,128)(2,1)S(1)}, u32[]{:S(2)}, u32[]{:S(2)}) collective-permute-start(bf16[288,384]{1,0:T(8,128)(2,1)S(1)} %late.7), channel_id=1, source_target_pairs={{0,16},{16,32},{32,48},{48,0},{1,17},{17,33},{33,49},{49,1},{2,18}... | collective-permute-start | bytes 663560 | tf_op jit(solution)/shard_map/ppermute | solution.py:361
  73.5 16.6 %all-to-all-start.1 = ((bf16[8,32,384]{2,1,0:T(8,128)(2,1)}), bf16[8,32,384]{2,1,0:T(8,128)(2,1)S(1)}, u32[]{:S(2)}, u32[]{:S(2)}) async-start(bf16[8,32,384]{2,1,0:T(8,128)(2,1)} %get-tuple-element.68), calls=%async_computation.1 | async-start | bytes 393216 | tf_op jit(solution)/shard_map/all_to_all | solution.py:418
  79.5 9.8 %collective-permute-start.16 = (bf16[16,384]{1,0:T(8,128)(2,1)S(1)}, bf16[16,384]{1,0:T(8,128)(2,1)S(1)}, u32[]{:S(2)}, u32[]{:S(2)}) collective-permute-start(bf16[16,384]{1,0:T(8,128)(2,1)S(1)} %get-tuple-element.69), channel_id=1, source_target_pairs={{160,0},{96,2},{128,4},{64,6},{0,8},{192,10},{32,12},{224,14},{130... | collective-permute-start | bytes 36872 | tf_op jit(solution)/shard_map/ppermute | solution.py:391

commit v8 on v7

--- a/solution.py
+++ b/solution.py
@@ -402,10 +402,11 @@
     right, left = [shift(kv_own, "x", NX, k) for k in (1, 3)]
     q_right, q_left = [shift(q_own, y, NY, k) for k in (1, 3)]
     q_far = shift(q_right, y, NY, 1)
-    got = lax.optimization_barrier([left, right, q_left, q_right, q_own, kv_own])
-    left, right, q_left, q_right, q_own, kv_own = got
+    other = core(kv_own)
+    got = lax.optimization_barrier([left, right, q_left, q_right, q_own, kv_own, other])
+    left, right, q_left, q_right, q_own, kv_own, other = got
     far = [shift(right[0:VID], "x", NX, 1), shift(left[VID:], "x", NX, 3)]
-    kvs = [kv_own, right, left] + [core(b) for b in (kv_own, right, left)]
+    kvs = [kv_own, right, left, other] + [core(b) for b in (right, left)]
     state = early([q_right, q_left, q_own], kvs)
     far, q_far, state = lax.optimization_barrier((far, q_far, state))
     others = [core(b) for b in far]

time: 92.5 us -> 92.5 us (level)
  no operation moved by 1% of the time
where the time goes in v8:
time: 92.5 us; the launch traced here: 91.5 us
  starting transfers between devices  40.6 us (44%)
  waiting for transfers between devices  33.9 us (37%)
  Pallas kernels  16 us (17%)
  between operations  0.97 us (1%)
    ppermute x15, starting transfers between devices, shift(): return lax.ppermute(x, axis, [(i, (i + k) % n) for i in range(n)])  16.2 us
    ppermute x1, waiting for transfers between devices, to_group(): return lax.ppermute(x, ('x', 'yh', 'z'), audio_pairs())  14.5 us
    ppermute x15, waiting for transfers between devices, shift(): return lax.ppermute(x, axis, [(i, (i + k) % n) for i in range(n)])  13.6 us
    all_to_all x1, starting transfers between devices, on_device(): lax.all_to_all(pack(align, video_q, video_k, video_v), 'z', split_axis=0,...  8.6 us
    pallas_call x2, Pallas kernels, early(): pl.pallas_call(early_body, out_shape=tuple((jax.ShapeDtypeStruct((rows, G...  6.83 us
    all_to_all x1, starting transfers between devices, on_device(): video = lax.all_to_all(video, 'z', split_axis=0, concat_axis=0, tiled=True)  5.95 us
    ppermute x1, waiting for transfers between devices, from_group(): return lax.ppermute(x, ('x', 'yh', 'z'), [(b, a) for a, b in audio_pairs()])  5.07 us
    pallas_call x4, Pallas kernels, late(): pl.pallas_call(late_body, out_shape=jax.ShapeDtypeStruct((QROWS, GW), BF1...  5.01 us
  transfers between devices with their start and end apart: 19, of which 9 were waited for; matrix products, arithmetic and copies ran while one was open for 0% of the time, Pallas kernels for 12%

profile of v8, /device:TPU:24, one launch (start us, length us, event | category | flops | bytes accessed | tf_op | source)
XLA Modules:
  0.0 91.5 jit_solution(13579308179060442643)
XLA Ops:
  0.6 2.1 %pack.1 = bf16[8,296,128]{2,1,0:T(8,128)(2,1)} custom-call(s32[32]{0:T(128)} %align_ref.1, bf16[32,3072]{1,0:T(8,128)(2,1)} %q_ref.1, bf16[32,3072]{1,0:T(8,128)(2,1)} %k_ref.1, bf16[32,3072]{1,0:T(8,128)(2,1)} %v_ref.1), custom_call_target="tpu_custom_call" | custom-call | tf_op jit(solution)/shard_map/pack/pallas_call | solution.py:57
  2.7 8.6 %all-to-all-start = ((bf16[8,296,128]{2,1,0:T(8,128)(2,1)}), bf16[8,296,128]{2,1,0:T(8,128)(2,1)S(1)}, u32[]{:S(2)}, u32[]{:S(2)}) async-start(bf16[8,296,128]{2,1,0:T(8,128)(2,1)} %pack.1), calls=%async_computation | async-start | bytes 1212416 | tf_op jit(solution)/shard_map/all_to_all | solution.py:396
  11.4 5.0 %collective-permute-start = (bf16[16,1152]{1,0:T(8,128)(2,1)S(1)}, bf16[16,1152]{1,0:T(8,128)(2,1)S(1)}, u32[]{:S(2)}, u32[]{:S(2)}) collective-permute-start(bf16[16,1152]{1,0:T(8,128)(2,1)S(1)} %pad_maximum_fusion), channel_id=1, source_target_pairs={{0,160},{2,96},{4,128},{6,64},{8,0},{10,192},{12,32},{14,224},{34,... | collective-permute-start | bytes 110600 | tf_op jit(solution)/shard_map/ppermute | solution.py:387
  16.3 14.5 %collective-permute-done.aud_ref = bf16[16,1152]{1,0:T(8,128)(2,1)S(1)} collective-permute-done((bf16[16,1152]{1,0:T(8,128)(2,1)S(1)}, bf16[16,1152]{1,0:T(8,128)(2,1)S(1)}, u32[]{:S(2)}, u32[]{:S(2)}) %collective-permute-start) | collective-permute-done | bytes 36896 | tf_op jit(solution)/shard_map/ppermute | solution.py:387
  31.5 2.9 %collective-permute-start.1 = (bf16[560,384]{1,0:T(8,128)(2,1)S(1)}, bf16[560,384]{1,0:T(8,128)(2,1)S(1)}, u32[]{:S(2)}, u32[]{:S(2)}) collective-permute-start(bf16[560,384]{1,0:T(8,128)(2,1)S(1)} %get-tuple-element.44.refs_3_.refs_1_.refs_0_), channel_id=1, source_target_pairs={{0,192},{64,0},{128,64},{192,128},{1,193},{65,1},{129,65},{193,129... | collective-permute-start | bytes 1290248 | tf_op jit(solution)/shard_map/ppermute | solution.py:361
  34.4 1.2 %collective-permute-start.4 = (bf16[288,384]{1,0:T(8,128)(2,1)S(1)}, bf16[288,384]{1,0:T(8,128)(2,1)S(1)}, u32[]{:S(2)}, u32[]{:S(2)}) collective-permute-start(bf16[288,384]{1,0:T(8,128)(2,1)S(1)} %get-tuple-element.39.refs_2_.q_ref), channel_id=1, source_target_pairs={{0,16},{16,32},{32,48},{48,0},{1,17},{17,33},{33,49},{49,1},{2,18}... | collective-permute-start | bytes 663560 | tf_op jit(solution)/shard_map/ppermute | solution.py:361
  36.4 5.2 %collective-permute-done.4.refs_0_.q_ref = bf16[288,384]{1,0:T(8,128)(2,1)S(1)} collective-permute-done((bf16[288,384]{1,0:T(8,128)(2,1)S(1)}, bf16[288,384]{1,0:T(8,128)(2,1)S(1)}, u32[]{:S(2)}, u32[]{:S(2)}) %collective-permute-start.4) | collective-permute-done | bytes 221216 | tf_op jit(solution)/shard_map/ppermute | solution.py:361
  41.6 2.3 %collective-permute-done.3.refs_1_.q_ref = bf16[288,384]{1,0:T(8,128)(2,1)S(1)} collective-permute-done((bf16[288,384]{1,0:T(8,128)(2,1)S(1)}, bf16[288,384]{1,0:T(8,128)(2,1)S(1)}, u32[]{:S(2)}, u32[]{:S(2)}) %collective-permute-start.3) | collective-permute-done | bytes 221216 | tf_op jit(solution)/shard_map/ppermute | solution.py:361
  44.6 1.1 %collective-permute-done.1.refs_5_.refs_3_.refs_2_ = bf16[560,384]{1,0:T(8,128)(2,1)S(1)} collective-permute-done((bf16[560,384]{1,0:T(8,128)(2,1)S(1)}, bf16[560,384]{1,0:T(8,128)(2,1)S(1)}, u32[]{:S(2)}, u32[]{:S(2)}) %collective-permute-start.1) | collective-permute-done | bytes 430112 | tf_op jit(solution)/shard_map/ppermute | solution.py:361
  46.6 1.6 %collective-permute-start.6 = (bf16[256,384]{1,0:T(8,128)(2,1)S(1)}, bf16[256,384]{1,0:T(8,128)(2,1)S(1)}, u32[]{:S(2)}, u32[]{:S(2)}) collective-permute-start(bf16[256,384]{1,0:T(8,128)(2,1)S(1)} %slice.6), channel_id=1, source_target_pairs={{0,64},{64,128},{128,192},{192,0},{1,65},{65,129},{129,193},{193,1... | collective-permute-start | bytes 589832 | tf_op jit(solution)/shard_map/ppermute | solution.py:361
  48.2 1.8 %collective-permute-start.7 = (bf16[304,384]{1,0:T(8,128)(2,1)S(1)}, bf16[304,384]{1,0:T(8,128)(2,1)S(1)}, u32[]{:S(2)}, u32[]{:S(2)}) collective-permute-start(bf16[304,384]{1,0:T(8,128)(2,1)S(1)} %slice.7), channel_id=1, source_target_pairs={{0,192},{64,0},{128,64},{192,128},{1,193},{65,1},{129,65},{193,129... | collective-permute-start | bytes 700424 | tf_op jit(solution)/shard_map/ppermute | solution.py:361
  49.9 5.0 %early.2 = (f32[272,384]{1,0:T(8,128)S(1)}, f32[272,384]{1,0:T(8,128)S(1)}, f32[272,384]{1,0:T(8,128)S(1)}, f32[272,384]{1,0:T(8,128)S(1)}, f32[272,384]{1,0:T(8,128)S(1)}, /*index=5*/f32[272,384]{1,0:T(8,128)S(1)}) custom-call(bf16[288,384]{1,0:T(8,128)(2,1)S(1)} %collective-permute-done.4.refs_0_.q_ref, ...), custom_call_target="tpu_custom_call" | custom-call | flops 2887778304 | bytes 4194304 | tf_op jit(solution)/shard_map/early/pallas_call | solution.py:197
  56.0 1.9 %early.3 = (f32[272,384]{1,0:T(8,128)S(1)}, f32[272,384]{1,0:T(8,128)S(1)}) custom-call(bf16[288,384]{1,0:T(8,128)(2,1)S(1)} %collective-permute-done.8.refs_0_.q_ref, bf16[560,384]{1,0:T(8,128)(2,1)S(1)} %get-tuple-element.44.refs_3_.refs_1_.refs_0_, bf16[560,384]{1,0:T(8,128)(2,1)S(1)} %collective-permute-done.2.refs_4_.refs_2_.refs_1_, ...), custom_call_target="tpu_custom_call" | custom-call | flops 962592768 | bytes 4194304 | tf_op jit(solution)/shard_map/early/pallas_call | solution.py:197
  57.9 1.2 %late.4 = bf16[288,384]{1,0:T(8,128)(2,1)S(1)} custom-call(bf16[288,384]{1,0:T(8,128)(2,1)S(1)} %collective-permute-done.8.refs_0_.q_ref, f32[272,384]{1,0:T(8,128)S(1)} %get-tuple-element.53.o_ref, f32[272,384]{1,0:T(8,128)S(1)} %get-tuple-element.54.l_ref, bf16[560,384]{1,0:T(8,128)(2,1)S(1)} %get-tuple-element.44.refs_3_.refs_1_.refs_0_, ...), custom_call_target="tpu_custom_call" | custom-call | flops 401080320 | bytes 5242880 | tf_op jit(solution)/shard_map/late/pallas_call | solution.py:277
  59.1 2.6 %collective-permute-start.13 = (bf16[288,384]{1,0:T(8,128)(2,1)S(1)}, bf16[288,384]{1,0:T(8,128)(2,1)S(1)}, u32[]{:S(2)}, u32[]{:S(2)}) collective-permute-start(bf16[288,384]{1,0:T(8,128)(2,1)S(1)} %late.4), channel_id=1, source_target_pairs={{0,32},{16,48},{32,0},{48,16},{1,33},{17,49},{33,1},{49,17},{2,34}... | collective-permute-start | bytes 663560 | tf_op jit(solution)/shard_map/ppermute | solution.py:361
  61.7 1.2 %late.6 = bf16[288,384]{1,0:T(8,128)(2,1)S(1)} custom-call(bf16[288,384]{1,0:T(8,128)(2,1)S(1)} %collective-permute-done.4.refs_0_.q_ref, f32[272,384]{1,0:T(8,128)S(1)} %get-tuple-element.66.o_ref, f32[272,384]{1,0:T(8,128)S(1)} %get-tuple-element.67.l_ref, bf16[560,384]{1,0:T(8,128)(2,1)S(1)} %get-tuple-element.44.refs_3_.refs_1_.refs_0_, ...), custom_call_target="tpu_custom_call" | custom-call | flops 401080320 | bytes 5242880 | tf_op jit(solution)/shard_map/late/pallas_call | solution.py:277
  63.3 1.3 %late.7 = bf16[288,384]{1,0:T(8,128)(2,1)S(1)} custom-call(bf16[288,384]{1,0:T(8,128)(2,1)S(1)} %collective-permute-done.3.refs_1_.q_ref, f32[272,384]{1,0:T(8,128)S(1)} %get-tuple-element.68.o_ref, f32[272,384]{1,0:T(8,128)S(1)} %get-tuple-element.69.l_ref, bf16[560,384]{1,0:T(8,128)(2,1)S(1)} %get-tuple-element.44.refs_3_.refs_1_.refs_0_, ...), custom_call_target="tpu_custom_call" | custom-call | flops 401080320 | bytes 5242880 | tf_op jit(solution)/shard_map/late/pallas_call | solution.py:277
  64.6 3.3 %collective-permute-start.15 = (bf16[288,384]{1,0:T(8,128)(2,1)S(1)}, bf16[288,384]{1,0:T(8,128)(2,1)S(1)}, u32[]{:S(2)}, u32[]{:S(2)}) collective-permute-start(bf16[288,384]{1,0:T(8,128)(2,1)S(1)} %late.7), channel_id=1, source_target_pairs={{0,16},{16,32},{32,48},{48,0},{1,17},{17,33},{33,49},{49,1},{2,18}... | collective-permute-start | bytes 663560 | tf_op jit(solution)/shard_map/ppermute | solution.py:361
  67.9 1.3 %late.5.a_ref = bf16[288,384]{1,0:T(8,128)(2,1)S(1)} custom-call(bf16[288,384]{1,0:T(8,128)(2,1)S(1)} %get-tuple-element.39.refs_2_.q_ref, f32[272,384]{1,0:T(8,128)S(1)} %get-tuple-element.63.o_ref, f32[272,384]{1,0:T(8,128)S(1)} %get-tuple-element.64.l_ref, bf16[560,384]{1,0:T(8,128)(2,1)S(1)} %get-tuple-element.44.refs_3_.refs_1_.refs_0_, ...), custom_call_target="tpu_custom_call" | custom-call | flops 401080320 | bytes 5242880 | tf_op jit(solution)/shard_map/late/pallas_call | solution.py:277
  69.1 3.7 %collective-permute-done.14.c_ref = bf16[288,384]{1,0:T(8,128)(2,1)S(1)} collective-permute-done((bf16[288,384]{1,0:T(8,128)(2,1)S(1)}, bf16[288,384]{1,0:T(8,128)(2,1)S(1)}, u32[]{:S(2)}, u32[]{:S(2)}) %collective-permute-start.14) | collective-permute-done | bytes 221216 | tf_op jit(solution)/shard_map/ppermute | solution.py:361
  72.8 1.2 %combine.1 = (bf16[8,32,384]{2,1,0:T(8,128)(2,1)}, bf16[16,384]{1,0:T(8,128)(2,1)S(1)}) custom-call(bf16[288,384]{1,0:T(8,128)(2,1)S(1)} %late.5.a_ref, bf16[288,384]{1,0:T(8,128)(2,1)S(1)} %collective-permute-done.13.b_ref, bf16[288,384]{1,0:T(8,128)(2,1)S(1)} %collective-permute-done.14.c_ref, bf16[288,384]{1,0:T(8,128)(2,1)S(1)} %collective-permute-done.15.d_ref), custom_call_target="tpu_custom_call" | custom-call | tf_op jit(solution)/shard_map/combine/pallas_call | solution.py:321
  74.0 5.9 %all-to-all-start.1 = ((bf16[8,32,384]{2,1,0:T(8,128)(2,1)}), bf16[8,32,384]{2,1,0:T(8,128)(2,1)S(1)}, u32[]{:S(2)}, u32[]{:S(2)}) async-start(bf16[8,32,384]{2,1,0:T(8,128)(2,1)} %get-tuple-element.70), calls=%async_computation.1 | async-start | bytes 393216 | tf_op jit(solution)/shard_map/all_to_all | solution.py:419
  80.0 4.8 %collective-permute-start.16 = (bf16[16,384]{1,0:T(8,128)(2,1)S(1)}, bf16[16,384]{1,0:T(8,128)(2,1)S(1)}, u32[]{:S(2)}, u32[]{:S(2)}) collective-permute-start(bf16[16,384]{1,0:T(8,128)(2,1)S(1)} %get-tuple-element.71), channel_id=1, source_target_pairs={{160,0},{96,2},{128,4},{64,6},{0,8},{192,10},{32,12},{224,14},{130... | collective-permute-start | bytes 36872 | tf_op jit(solution)/shard_map/ppermute | solution.py:391
  84.8 5.1 %collective-permute-done.16.audio_ref = bf16[16,384]{1,0:T(8,128)(2,1)S(1)} collective-permute-done((bf16[16,384]{1,0:T(8,128)(2,1)S(1)}, bf16[16,384]{1,0:T(8,128)(2,1)S(1)}, u32[]{:S(2)}, u32[]{:S(2)}) %collective-permute-start.16) | collective-permute-done | bytes 12320 | tf_op jit(solution)/shard_map/ppermute | solution.py:391
  (33 shorter events, 5.8 us)
Async XLA Ops:
  2.7 8.6 %copy-start = (bf16[16,384]{1,0:T(8,128)(2,1)S(1)}, bf16[16,384]{1,0:T(8,128)(2,1)}, u32[]{:S(2)}) copy-start(bf16[16,384]{1,0:T(8,128)(2,1)} %param.12) | copy-start | bytes 36868
  2.7 8.6 %copy-start.1 = (bf16[16,384]{1,0:T(8,128)(2,1)S(1)}, bf16[16,384]{1,0:T(8,128)(2,1)}, u32[]{:S(2)}) copy-start(bf16[16,384]{1,0:T(8,128)(2,1)} %param.11) | copy-start | bytes 36868
  2.7 8.6 %copy-start.2 = (bf16[16,384]{1,0:T(8,128)(2,1)S(1)}, bf16[16,384]{1,0:T(8,128)(2,1)}, u32[]{:S(2)}) copy-start(bf16[16,384]{1,0:T(8,128)(2,1)} %param.10) | copy-start | bytes 36868
  2.7 28.1 %all-to-all-start = ((bf16[8,296,128]{2,1,0:T(8,128)(2,1)}), bf16[8,296,128]{2,1,0:T(8,128)(2,1)S(1)}, u32[]{:S(2)}, u32[]{:S(2)}) async-start(bf16[8,296,128]{2,1,0:T(8,128)(2,1)} %pack.1), calls=%async_computation | async-start | bytes 1212416 | tf_op jit(solution)/shard_map/all_to_all | solution.py:396
  11.4 19.5 %collective-permute-start = (bf16[16,1152]{1,0:T(8,128)(2,1)S(1)}, bf16[16,1152]{1,0:T(8,128)(2,1)S(1)}, u32[]{:S(2)}, u32[]{:S(2)}) collective-permute-start(bf16[16,1152]{1,0:T(8,128)(2,1)S(1)} %pad_maximum_fusion), channel_id=1, source_target_pairs={{0,160},{2,96},{4,128},{6,64},{8,0},{10,192},{12,32},{14,224},{34,... | collective-permute-start | bytes 110600 | tf_op jit(solution)/shard_map/ppermute | solution.py:387
  31.0 13.0 %collective-permute-start.5 = (bf16[560,384]{1,0:T(8,128)(2,1)S(1)}, bf16[560,384]{1,0:T(8,128)(2,1)S(1)}, u32[]{:S(2)}, u32[]{:S(2)}) collective-permute-start(bf16[560,384]{1,0:T(8,128)(2,1)S(1)} %get-tuple-element.44.refs_3_.refs_1_.refs_0_), channel_id=1, source_target_pairs={{0,1},{1,0},{2,3},{3,2},{4,5},{5,4},{6,7},{7,6},{8,9},{9,8},{10,11... | collective-permute-start | bytes 1290248 | tf_op jit(solution)/shard_map/ppermute | solution.py:361
  31.1 13.5 %collective-permute-start.2 = (bf16[560,384]{1,0:T(8,128)(2,1)S(1)}, bf16[560,384]{1,0:T(8,128)(2,1)S(1)}, u32[]{:S(2)}, u32[]{:S(2)}) collective-permute-start(bf16[560,384]{1,0:T(8,128)(2,1)S(1)} %get-tuple-element.44.refs_3_.refs_1_.refs_0_), channel_id=1, source_target_pairs={{0,64},{64,128},{128,192},{192,0},{1,65},{65,129},{129,193},{193,1... | collective-permute-start | bytes 1290248 | tf_op jit(solution)/shard_map/ppermute | solution.py:361
  31.5 14.3 %collective-permute-start.1 = (bf16[560,384]{1,0:T(8,128)(2,1)S(1)}, bf16[560,384]{1,0:T(8,128)(2,1)S(1)}, u32[]{:S(2)}, u32[]{:S(2)}) collective-permute-start(bf16[560,384]{1,0:T(8,128)(2,1)S(1)} %get-tuple-element.44.refs_3_.refs_1_.refs_0_), channel_id=1, source_target_pairs={{0,192},{64,0},{128,64},{192,128},{1,193},{65,1},{129,65},{193,129... | collective-permute-start | bytes 1290248 | tf_op jit(solution)/shard_map/ppermute | solution.py:361
  34.4 7.2 %collective-permute-start.4 = (bf16[288,384]{1,0:T(8,128)(2,1)S(1)}, bf16[288,384]{1,0:T(8,128)(2,1)S(1)}, u32[]{:S(2)}, u32[]{:S(2)}) collective-permute-start(bf16[288,384]{1,0:T(8,128)(2,1)S(1)} %get-tuple-element.39.refs_2_.q_ref), channel_id=1, source_target_pairs={{0,16},{16,32},{32,48},{48,0},{1,17},{17,33},{33,49},{49,1},{2,18}... | collective-permute-start | bytes 663560 | tf_op jit(solution)/shard_map/ppermute | solution.py:361
  35.6 8.3 %collective-permute-start.3 = (bf16[288,384]{1,0:T(8,128)(2,1)S(1)}, bf16[288,384]{1,0:T(8,128)(2,1)S(1)}, u32[]{:S(2)}, u32[]{:S(2)}) collective-permute-start(bf16[288,384]{1,0:T(8,128)(2,1)S(1)} %get-tuple-element.39.refs_2_.q_ref), channel_id=1, source_target_pairs={{0,48},{16,0},{32,16},{48,32},{1,49},{17,1},{33,17},{49,33},{2,50}... | collective-permute-start | bytes 663560 | tf_op jit(solution)/shard_map/ppermute | solution.py:361
  45.8 4.2 %collective-permute-start.9 = (bf16[560,384]{1,0:T(8,128)(2,1)S(1)}, bf16[560,384]{1,0:T(8,128)(2,1)S(1)}, u32[]{:S(2)}, u32[]{:S(2)}) collective-permute-start(bf16[560,384]{1,0:T(8,128)(2,1)S(1)} %collective-permute-done.2.refs_4_.refs_2_.refs_1_), channel_id=1, source_target_pairs={{0,1},{1,0},{2,3},{3,2},{4,5},{5,4},{6,7},{7,6},{8,9},{9,8},{10,11... | collective-permute-start | bytes 1290248 | tf_op jit(solution)/shard_map/ppermute | solution.py:361
  45.8 4.2 %collective-permute-start.10 = (bf16[560,384]{1,0:T(8,128)(2,1)S(1)}, bf16[560,384]{1,0:T(8,128)(2,1)S(1)}, u32[]{:S(2)}, u32[]{:S(2)}) collective-permute-start(bf16[560,384]{1,0:T(8,128)(2,1)S(1)} %collective-permute-done.1.refs_5_.refs_3_.refs_2_), channel_id=1, source_target_pairs={{0,1},{1,0},{2,3},{3,2},{4,5},{5,4},{6,7},{7,6},{8,9},{9,8},{10,11... | collective-permute-start | bytes 1290248 | tf_op jit(solution)/shard_map/ppermute | solution.py:361
  46.3 8.6 %collective-permute-start.8 = (bf16[288,384]{1,0:T(8,128)(2,1)S(1)}, bf16[288,384]{1,0:T(8,128)(2,1)S(1)}, u32[]{:S(2)}, u32[]{:S(2)}) collective-permute-start(bf16[288,384]{1,0:T(8,128)(2,1)S(1)} %collective-permute-done.4.refs_0_.q_ref), channel_id=1, source_target_pairs={{0,16},{16,32},{32,48},{48,0},{1,17},{17,33},{33,49},{49,1},{2,18}... | collective-permute-start | bytes 663560 | tf_op jit(solution)/shard_map/ppermute | solution.py:361
  46.6 8.3 %collective-permute-start.6 = (bf16[256,384]{1,0:T(8,128)(2,1)S(1)}, bf16[256,384]{1,0:T(8,128)(2,1)S(1)}, u32[]{:S(2)}, u32[]{:S(2)}) collective-permute-start(bf16[256,384]{1,0:T(8,128)(2,1)S(1)} %slice.6), channel_id=1, source_target_pairs={{0,64},{64,128},{128,192},{192,0},{1,65},{65,129},{129,193},{193,1... | collective-permute-start | bytes 589832 | tf_op jit(solution)/shard_map/ppermute | solution.py:361
  48.2 7.3 %collective-permute-start.7 = (bf16[304,384]{1,0:T(8,128)(2,1)S(1)}, bf16[304,384]{1,0:T(8,128)(2,1)S(1)}, u32[]{:S(2)}, u32[]{:S(2)}) collective-permute-start(bf16[304,384]{1,0:T(8,128)(2,1)S(1)} %slice.7), channel_id=1, source_target_pairs={{0,192},{64,0},{128,64},{192,128},{1,193},{65,1},{129,65},{193,129... | collective-permute-start | bytes 700424 | tf_op jit(solution)/shard_map/ppermute | solution.py:361
  55.5 2.4 %collective-permute-start.12 = (bf16[304,384]{1,0:T(8,128)(2,1)S(1)}, bf16[304,384]{1,0:T(8,128)(2,1)S(1)}, u32[]{:S(2)}, u32[]{:S(2)}) collective-permute-start(bf16[304,384]{1,0:T(8,128)(2,1)S(1)} %collective-permute-done.7.refs_7_), channel_id=1, source_target_pairs={{0,1},{1,0},{2,3},{3,2},{4,5},{5,4},{6,7},{7,6},{8,9},{9,8},{10,11... | collective-permute-start | bytes 700424 | tf_op jit(solution)/shard_map/ppermute | solution.py:361
  55.5 2.4 %collective-permute-start.11 = (bf16[256,384]{1,0:T(8,128)(2,1)S(1)}, bf16[256,384]{1,0:T(8,128)(2,1)S(1)}, u32[]{:S(2)}, u32[]{:S(2)}) collective-permute-start(bf16[256,384]{1,0:T(8,128)(2,1)S(1)} %collective-permute-done.6.refs_6_), channel_id=1, source_target_pairs={{0,1},{1,0},{2,3},{3,2},{4,5},{5,4},{6,7},{7,6},{8,9},{9,8},{10,11... | collective-permute-start | bytes 589832 | tf_op jit(solution)/shard_map/ppermute | solution.py:361
  59.1 10.0 %collective-permute-start.13 = (bf16[288,384]{1,0:T(8,128)(2,1)S(1)}, bf16[288,384]{1,0:T(8,128)(2,1)S(1)}, u32[]{:S(2)}, u32[]{:S(2)}) collective-permute-start(bf16[288,384]{1,0:T(8,128)(2,1)S(1)} %late.4), channel_id=1, source_target_pairs={{0,32},{16,48},{32,0},{48,16},{1,33},{17,49},{33,1},{49,17},{2,34}... | collective-permute-start | bytes 663560 | tf_op jit(solution)/shard_map/ppermute | solution.py:361
  63.0 9.8 %collective-permute-start.14 = (bf16[288,384]{1,0:T(8,128)(2,1)S(1)}, bf16[288,384]{1,0:T(8,128)(2,1)S(1)}, u32[]{:S(2)}, u32[]{:S(2)}) collective-permute-start(bf16[288,384]{1,0:T(8,128)(2,1)S(1)} %late.6), channel_id=1, source_target_pairs={{0,48},{16,0},{32,16},{48,32},{1,49},{17,1},{33,17},{49,33},{2,50}... | collective-permute-start | bytes 663560 | tf_op jit(solution)/shard_map/ppermute | solution.py:361
  64.6 8.2 %collective-permute-start.15 = (bf16[288,384]{1,0:T(8,128)(2,1)S(1)}, bf16[288,384]{1,0:T(8,128)(2,1)S(1)}, u32[]{:S(2)}, u32[]{:S(2)}) collective-permute-start(bf16[288,384]{1,0:T(8,128)(2,1)S(1)} %late.7), channel_id=1, source_target_pairs={{0,16},{16,32},{32,48},{48,0},{1,17},{17,33},{33,49},{49,1},{2,18}... | collective-permute-start | bytes 663560 | tf_op jit(solution)/shard_map/ppermute | solution.py:361
  74.0 16.6 %all-to-all-start.1 = ((bf16[8,32,384]{2,1,0:T(8,128)(2,1)}), bf16[8,32,384]{2,1,0:T(8,128)(2,1)S(1)}, u32[]{:S(2)}, u32[]{:S(2)}) async-start(bf16[8,32,384]{2,1,0:T(8,128)(2,1)} %get-tuple-element.70), calls=%async_computation.1 | async-start | bytes 393216 | tf_op jit(solution)/shard_map/all_to_all | solution.py:419
  80.0 9.9 %collective-permute-start.16 = (bf16[16,384]{1,0:T(8,128)(2,1)S(1)}, bf16[16,384]{1,0:T(8,128)(2,1)S(1)}, u32[]{:S(2)}, u32[]{:S(2)}) collective-permute-start(bf16[16,384]{1,0:T(8,128)(2,1)S(1)} %get-tuple-element.71), channel_id=1, source_target_pairs={{160,0},{96,2},{128,4},{64,6},{0,8},{192,10},{32,12},{224,14},{130... | collective-permute-start | bytes 36872 | tf_op jit(solution)/shard_map/ppermute | solution.py:391
